TPU v7x, 32 devices: a whole 2x2x4 slice. The times are simulated.
32 devices in a mesh: dp: 8 (over z, y), tp: 4 (over x, core).
Axes of the slice: x: 2, y: 2, z: 4, core: 2. Of those that a mesh axis runs over, the one named last changes fastest.
Arguments:
- tile_vectors: bfloat16 [16384, 768], P(('dp', 'tp')), may hold values from -6 to 6
- snapshot_horizon_slot: int32 [8], P('dp'), may hold values from 0 to 39
- horizon_sample_tally: int32 [40], replicated, may hold values from 1 to 9
- specialist_outlooks: bfloat16 [3, 69, 64, 16384], P(None, None, None, ('dp', 'tp')), may hold values from -6 to 6
- early_layernorm_scale: float32 [768], replicated, may hold values from 0.5 to 1.5
- early_layernorm_shift: float32 [768], replicated, may hold values from -1.75 to 1.75
- horizon_vectors: float32 [40, 768], replicated, may hold values from -3 to 3
- triple_head_matrix: bfloat16 [3, 768, 768], P(None, None, 'tp'), may hold values from -0.21875 to 0.21875
- attending_matrix: bfloat16 [768, 768], P('tp'), may hold values from -3.5 to 3.5
- attending_offset: float32 [768], replicated, may hold values from -1.75 to 1.75
- later_layernorm_scale: float32 [768], replicated, may hold values from 0.5 to 1.5
- later_layernorm_shift: float32 [768], replicated, may hold values from -1.75 to 1.75
- widening_matrix: bfloat16 [768, 3072], P(None, 'tp'), may hold values from -0.21875 to 0.21875
- widening_offset: float32 [3072], P('tp'), may hold values from -3 to 3
- narrowing_matrix: bfloat16 [3072, 768], P('tp'), may hold values from -0.109375 to 0.109375
- narrowing_offset: float32 [768], replicated, may hold values from -1.75 to 1.75
- router_matrix: bfloat16 [768, 207], replicated, may hold values from -0.109375 to 0.109375
- router_offset: float32 [207], replicated, may hold values from -1.75 to 1.75
- adjuster_matrix: bfloat16 [768, 69], replicated, may hold values from -0.21875 to 0.21875
- adjuster_offset: float32 [69], replicated, may hold values from -3 to 3
- combined_loss_slope: bfloat16 [69, 64, 16384], P(None, None, ('dp', 'tp')), may hold values from -6 to 6
Outputs:
- blended: float32 [69, 64, 16384], P(None, None, ('dp', 'tp'))
- tokens_grad: float32 [16384, 768], P(('dp', 'tp'))
- first_gain_grad: float32 [768], replicated
- first_shift_grad: float32 [768], replicated
- lead_table_grad: float32 [40, 768], replicated
- qkv_weight_grad: float32 [3, 768, 768], P(None, None, 'tp')
- proj_weight_grad: float32 [768, 768], P('tp')
- proj_bias_grad: float32 [768], replicated
- second_gain_grad: float32 [768], replicated
- second_shift_grad: float32 [768], replicated
- in_weight_grad: float32 [768, 3072], P(None, 'tp')
- in_bias_grad: float32 [3072], P('tp')
- out_weight_grad: float32 [3072, 768], P('tp')
- out_bias_grad: float32 [768], replicated
- gate_weight_grad: float32 [768, 207], replicated
- gate_bias_grad: float32 [207], replicated
- correct_weight_grad: float32 [768, 69], replicated
- correct_bias_grad: float32 [69], replicated
All inputs are finite; a program needn't handle non-finite values.
Results may differ from a plain program's by a relative error of at most 0.017.
The roundings to bfloat16 on the way count: a program that leaves them out, or rounds other values in their place, can miss the bound.
Values may be sent and summed in bfloat16 or wider, within the bound.
A program may use at most 128 MiB of HBM per device.

v0:
```python
import jax
import jax.numpy as jnp
from jax import lax
from jax.sharding import PartitionSpec as P

HEAD_DIM = 64
SPECIALIST_TOTAL = 3
TILES_PER_SHOT = 2048
QBLOCK = 512


HIGH = lax.Precision.HIGHEST
EPSILON = 1e-05


def layer_norm(values, gain_vec, shift_vec):
    center = values - jnp.mean(values, axis=-1, keepdims=True)
    spread = jnp.mean(center * center, axis=-1, keepdims=True)
    return center * lax.rsqrt(spread + EPSILON) * gain_vec + shift_vec


def softmax_axis(scores, axis_num):
    highest = jnp.max(scores, axis=axis_num, keepdims=True)
    raised = jnp.exp(scores - highest)
    return raised / jnp.sum(raised, axis=axis_num, keepdims=True)


def gelu_exact(values):
    return jax.nn.gelu(values, approximate=False)


def split_heads(projected):
    total_rows = projected.shape[1]
    heads_local = projected.shape[2] // HEAD_DIM
    queries = projected[0].reshape(total_rows, heads_local, HEAD_DIM)
    keys_all = projected[1].reshape(total_rows, heads_local, HEAD_DIM)
    values_all = projected[2].reshape(total_rows, heads_local, HEAD_DIM)
    return (queries, keys_all, values_all)


def attention_forward(projected, scale_val):
    total_rows = projected.shape[1]
    queries, keys_all, values_all = split_heads(projected)

    def one_block(block_id):
        query_part = lax.dynamic_slice_in_dim(queries, block_id * QBLOCK, QBLOCK, 0)
        scores = (
            jnp.einsum("qhd,khd->hqk", query_part, keys_all, preferred_element_type=jnp.float32)
            * scale_val
        )
        highest = jnp.max(scores, axis=-1, keepdims=True)
        raised = jnp.exp(scores - highest)
        summed = jnp.sum(raised, axis=-1, keepdims=True)
        prob_low = (raised / summed).astype(jnp.bfloat16)
        output = jnp.einsum(
            "hqk,khd->qhd", prob_low, values_all, preferred_element_type=jnp.float32
        )
        return (output.astype(jnp.bfloat16), (highest + jnp.log(summed))[..., 0])

    outputs, log_totals = lax.map(one_block, jnp.arange(total_rows // QBLOCK, dtype=jnp.int32))
    return (outputs.reshape(total_rows, projected.shape[2]), log_totals)


def attention_backward(projected, log_totals, grad_out, scale_val):
    total_rows = projected.shape[1]
    width_local = projected.shape[2]
    queries, keys_all, values_all = split_heads(projected)
    grad_heads = grad_out.reshape(queries.shape)

    def one_block(carry, block_id):
        key_grad, value_grad = carry
        query_part = lax.dynamic_slice_in_dim(queries, block_id * QBLOCK, QBLOCK, 0)
        grad_part = lax.dynamic_slice_in_dim(grad_heads, block_id * QBLOCK, QBLOCK, 0)
        scores = (
            jnp.einsum("qhd,khd->hqk", query_part, keys_all, preferred_element_type=jnp.float32)
            * scale_val
        )
        prob_rows = jnp.exp(scores - log_totals[block_id][..., None])
        prob_grad = jnp.einsum(
            "qhd,khd->hqk", grad_part, values_all, preferred_element_type=jnp.float32
        )
        inner_sum = jnp.sum(prob_rows * prob_grad, axis=-1, keepdims=True)
        score_grad = (prob_rows * (prob_grad - inner_sum)).astype(jnp.bfloat16)
        query_grad = (
            jnp.einsum("hqk,khd->qhd", score_grad, keys_all, preferred_element_type=jnp.float32)
            * scale_val
        )
        key_add = (
            jnp.einsum("hqk,qhd->khd", score_grad, query_part, preferred_element_type=jnp.float32)
            * scale_val
        )
        value_add = jnp.einsum(
            "hqk,qhd->khd",
            prob_rows.astype(jnp.bfloat16),
            grad_part,
            preferred_element_type=jnp.float32,
        )
        key_grad = key_grad + key_add
        value_grad = value_grad + value_add
        return ((key_grad, value_grad), query_grad)

    zeros_grad = jnp.zeros(queries.shape, jnp.float32)
    (key_grad, value_grad), query_grad = lax.scan(
        one_block, (zeros_grad, zeros_grad), jnp.arange(total_rows // QBLOCK, dtype=jnp.int32)
    )
    return jnp.stack(
        [
            query_grad.reshape(total_rows, width_local),
            key_grad.reshape(total_rows, width_local),
            value_grad.reshape(total_rows, width_local),
        ]
    ).astype(jnp.bfloat16)


def body(
    tile_vectors,
    snapshot_horizon_slot,
    horizon_sample_tally,
    specialist_outlooks,
    early_layernorm_scale,
    early_layernorm_shift,
    horizon_vectors,
    triple_head_matrix,
    attending_matrix,
    attending_offset,
    later_layernorm_scale,
    later_layernorm_shift,
    widening_matrix,
    widening_offset,
    narrowing_matrix,
    narrowing_offset,
    router_matrix,
    router_offset,
    adjuster_matrix,
    adjuster_offset,
    combined_loss_slope,
):
    rows_dev = tile_vectors.shape[0]
    frames_dev = snapshot_horizon_slot.shape[0]
    scale_val = HEAD_DIM ** (-0.5)
    row_start = lax.axis_index("tp") * rows_dev
    row_frame = (row_start + jnp.arange(rows_dev, dtype=jnp.int32)) // TILES_PER_SHOT
    frame_pick = (row_frame[:, None] == jnp.arange(frames_dev, dtype=jnp.int32)[None, :]).astype(
        jnp.int32
    )
    row_lead = jnp.sum(frame_pick * snapshot_horizon_slot[None, :], axis=1)
    lead_onehot = (
        row_lead[:, None] == jnp.arange(horizon_vectors.shape[0], dtype=jnp.int32)[None, :]
    ).astype(jnp.float32)
    row_scale = lax.rsqrt(
        jnp.dot(lead_onehot, horizon_sample_tally.astype(jnp.float32), precision=HIGH)
    )
    residual = tile_vectors.astype(jnp.float32)

    def first_norm(values, gain_vec, shift_vec, embed_table):
        return layer_norm(values, gain_vec, shift_vec) + jnp.dot(
            lead_onehot, embed_table, precision=HIGH
        )

    attn_in, first_back = jax.vjp(
        first_norm, residual, early_layernorm_scale, early_layernorm_shift, horizon_vectors
    )
    attn_rows = lax.all_gather(attn_in.astype(jnp.bfloat16), "tp", axis=0, tiled=True)
    projected = jnp.einsum(
        "td,sdh->sth", attn_rows, triple_head_matrix, preferred_element_type=jnp.float32
    ).astype(jnp.bfloat16)
    attended, log_totals = attention_forward(projected, scale_val)
    after_attn = (
        residual
        + lax.psum_scatter(
            jnp.dot(attended, attending_matrix, preferred_element_type=jnp.float32),
            "tp",
            scatter_dimension=0,
            tiled=True,
        )
        + attending_offset
    )
    mlp_in, second_back = jax.vjp(
        layer_norm, after_attn, later_layernorm_scale, later_layernorm_shift
    )
    mlp_low = mlp_in.astype(jnp.bfloat16)
    mlp_rows = lax.all_gather(mlp_low, "tp", axis=0, tiled=True)
    hidden = (
        jnp.dot(mlp_rows, widening_matrix, preferred_element_type=jnp.float32) + widening_offset
    )
    activated, gelu_back = jax.vjp(gelu_exact, hidden)
    act_low = activated.astype(jnp.bfloat16)
    mlp_out = lax.psum_scatter(
        jnp.dot(act_low, narrowing_matrix, preferred_element_type=jnp.float32),
        "tp",
        scatter_dimension=0,
        tiled=True,
    )
    after_mlp = after_attn + mlp_out + narrowing_offset
    head_in = after_mlp.astype(jnp.bfloat16)
    logits = jnp.dot(head_in, router_matrix, preferred_element_type=jnp.float32) + router_offset
    correction = (
        jnp.dot(head_in, adjuster_matrix, preferred_element_type=jnp.float32) + adjuster_offset
    )

    def combine_experts(logit_rows, correct_rows):
        gate_probabilities = softmax_axis(logit_rows.reshape(rows_dev, SPECIALIST_TOTAL, -1), 1)
        expert_mixture = (correct_rows * row_scale[:, None]).T[:, None, :]
        for specialist_item in range(SPECIALIST_TOTAL):
            expert_mixture = expert_mixture + gate_probabilities[:, specialist_item, :].T[
                :, None, :
            ] * specialist_outlooks[specialist_item].astype(jnp.float32)
        return expert_mixture

    blended, combine_back = jax.vjp(combine_experts, logits, correction)
    logit_grad, correct_grad = combine_back(combined_loss_slope.astype(jnp.float32))
    logit_low = logit_grad.astype(jnp.bfloat16)
    correct_low = correct_grad.astype(jnp.bfloat16)
    gate_weight_grad = jnp.einsum(
        "td,tk->dk", head_in, logit_low, preferred_element_type=jnp.float32
    )
    gate_bias_grad = jnp.sum(logit_low.astype(jnp.float32), axis=0)
    correct_weight_grad = jnp.einsum(
        "td,tk->dk", head_in, correct_low, preferred_element_type=jnp.float32
    )
    correct_bias_grad = jnp.sum(correct_low.astype(jnp.float32), axis=0)
    mlp_grad = jnp.einsum(
        "tk,dk->td", logit_low, router_matrix, preferred_element_type=jnp.float32
    ) + jnp.einsum("tk,dk->td", correct_low, adjuster_matrix, preferred_element_type=jnp.float32)
    out_bias_grad = jnp.sum(mlp_grad, axis=0)
    grad_low = mlp_grad.astype(jnp.bfloat16)
    mlp_out_rows = lax.all_gather(grad_low, "tp", axis=0, tiled=True)
    out_weight_grad = jnp.einsum(
        "tf,td->fd", act_low, mlp_out_rows, preferred_element_type=jnp.float32
    )
    act_grad = jnp.einsum(
        "td,fd->tf", mlp_out_rows, narrowing_matrix, preferred_element_type=jnp.float32
    )
    hidden_low = gelu_back(act_grad)[0].astype(jnp.bfloat16)
    in_bias_grad = jnp.sum(hidden_low.astype(jnp.float32), axis=0)
    in_weight_grad = jnp.einsum(
        "td,tf->df", mlp_rows, hidden_low, preferred_element_type=jnp.float32
    )
    norm_grad = lax.psum_scatter(
        jnp.einsum("tf,df->td", hidden_low, widening_matrix, preferred_element_type=jnp.float32),
        "tp",
        scatter_dimension=0,
        tiled=True,
    )
    attn_part, second_gain_grad, second_shift_grad = second_back(norm_grad)
    attn_grad = mlp_grad + attn_part
    proj_bias_grad = jnp.sum(attn_grad, axis=0)
    attn_out_rows = lax.all_gather(attn_grad.astype(jnp.bfloat16), "tp", axis=0, tiled=True)
    proj_weight_grad = jnp.einsum(
        "tk,td->kd", attended, attn_out_rows, preferred_element_type=jnp.float32
    )
    attended_grad = jnp.einsum(
        "td,kd->tk", attn_out_rows, attending_matrix, preferred_element_type=jnp.float32
    ).astype(jnp.bfloat16)
    projected_grad = attention_backward(projected, log_totals, attended_grad, scale_val)
    qkv_weight_grad = jnp.einsum(
        "td,sth->sdh", attn_rows, projected_grad, preferred_element_type=jnp.float32
    )
    first_grad = lax.psum_scatter(
        jnp.einsum(
            "sth,sdh->td", projected_grad, triple_head_matrix, preferred_element_type=jnp.float32
        ),
        "tp",
        scatter_dimension=0,
        tiled=True,
    )
    token_part, first_gain_grad, first_shift_grad, lead_table_grad = first_back(first_grad)
    tokens_grad = attn_grad + token_part
    qkv_weight_grad, proj_weight_grad, in_weight_grad, in_bias_grad, out_weight_grad = lax.psum(
        (qkv_weight_grad, proj_weight_grad, in_weight_grad, in_bias_grad, out_weight_grad), "dp"
    )
    (
        first_gain_grad,
        first_shift_grad,
        lead_table_grad,
        proj_bias_grad,
        second_gain_grad,
        second_shift_grad,
        out_bias_grad,
        gate_weight_grad,
        gate_bias_grad,
        correct_weight_grad,
        correct_bias_grad,
    ) = lax.psum(
        (
            first_gain_grad,
            first_shift_grad,
            lead_table_grad,
            proj_bias_grad,
            second_gain_grad,
            second_shift_grad,
            out_bias_grad,
            gate_weight_grad,
            gate_bias_grad,
            correct_weight_grad,
            correct_bias_grad,
        ),
        ("dp", "tp"),
    )
    return (
        blended,
        tokens_grad,
        first_gain_grad,
        first_shift_grad,
        lead_table_grad,
        qkv_weight_grad,
        proj_weight_grad,
        proj_bias_grad,
        second_gain_grad,
        second_shift_grad,
        in_weight_grad,
        in_bias_grad,
        out_weight_grad,
        out_bias_grad,
        gate_weight_grad,
        gate_bias_grad,
        correct_weight_grad,
        correct_bias_grad,
    )


def solution(mesh):
    return jax.shard_map(
        body,
        mesh=mesh,
        in_specs=(
            P(("dp", "tp"), None),
            P("dp"),
            P(),
            P(None, None, None, ("dp", "tp")),
            P(),
            P(),
            P(),
            P(None, None, "tp"),
            P("tp", None),
            P(),
            P(),
            P(),
            P(None, "tp"),
            P("tp"),
            P("tp", None),
            P(),
            P(),
            P(),
            P(),
            P(),
            P(None, None, ("dp", "tp")),
        ),
        out_specs=(
            P(None, None, ("dp", "tp")),
            P(("dp", "tp"), None),
            P(),
            P(),
            P(),
            P(None, None, "tp"),
            P("tp", None),
            P(),
            P(),
            P(),
            P(None, "tp"),
            P("tp"),
            P("tp", None),
            P(),
            P(),
            P(),
            P(),
            P(),
        ),
        check_vma=False,
    )
```

profile of v0, /device:TPU:0, one launch (start us, length us, event | category | flops | bytes accessed | tf_op | source)
XLA Modules:
  0.0 1033.3 jit_solution(6794998011685710122)
XLA Ops:
  10.9 3.0 fusion.57
  14.0 31.3 %all-gather.5.cloned.1.call-done = bf16[2048,768]{1,0:T(8,128)(2,1)} async-done(((bf16[512,768]{1,0:T(8,128)(2,1)}), bf16[2048,768]{1,0:T(8,128)(2,1)}) %all-gather.5.cloned.1.call-update) | async-done | bytes 3145744 | tf_op jit(solution)/shard_map/all_gather | solution.py:163
  45.4 3.9 fusion.95
  50.0 41.0 %while.27 = (s32[]{:T(128)}, bf16[4,512,3,64]{1,3,2,0:T(8,128)(2,1)}, f32[4,3,512]{2,1,0:T(4,128)}, s32[4]{0:T(128)S(1)}, bf16[2048,3,64]{0,2,1:T(8,128)(2,1)S(1...) while((s32[]{:T(128)}, ...), condition=%wide.region_5.6_spmd, body=%wide.region_2.0_spmd.sunk | while | flops 833714688 | bytes 39766204 | solution.py:60
  53.2 2.5 fusion.166
  55.6 4.0 fusion.167
  63.4 2.5 fusion.166
  65.9 4.0 fusion.167
  73.7 2.5 fusion.166
  76.1 4.0 fusion.167
  86.4 4.0 fusion.167
  94.4 3.7 fusion.96
  98.3 58.4 %reduce-scatter.5.cloned.1.call-done = f32[512,768]{1,0:T(8,128)} async-done(((f32[2048,768]{1,0:T(8,128)}), f32[512,768]{1,0:T(8,128)}) %reduce-scatter.5.cloned.1.call-update) | async-done | bytes 1572880 | tf_op jit(solution)/shard_map/reduce_scatter | solution.py:170
  161.2 28.2 %all-gather.7.cloned.1.call-done = bf16[2048,768]{1,0:T(8,128)(2,1)} async-done(((bf16[512,768]{1,0:T(8,128)(2,1)}), bf16[2048,768]{1,0:T(8,128)(2,1)}) %all-gather.7.cloned.1.call-update) | async-done | bytes 3145744 | tf_op jit(solution)/shard_map/all_gather | solution.py:182
  189.4 18.4 %multiply_convert_fusion.1 = (bf16[2048,768]{1,0:T(8,128)(2,1)S(1)}, f32[2048,768]{1,0:T(8,128)}, f32[2048,768]{1,0:T(8,128)}) fusion(f32[768]{0:T(1024)} %param.38, bf16[2048,768]{1,0:T(8,128)(2,1)} %all-gather.7.cloned.1.call-done, bf16[768,768]{1,0:T(8,128)(2,1)S(1)} %copy-done), kind=kOutput, calls=%fused_computation.57 | convolution fusion | flops 2519728128 | bytes 20057088 | tf_op jit(solution)/shard_map/dot_general | solution.py:184
  209.5 4.5 fusion.97
  215.6 56.9 %reduce-scatter.7.cloned.1.call-done = f32[512,768]{1,0:T(8,128)} async-done(((f32[2048,768]{1,0:T(8,128)}), f32[512,768]{1,0:T(8,128)}) %reduce-scatter.7.cloned.1.call-update) | async-done | bytes 1572880 | tf_op jit(solution)/shard_map/reduce_scatter | solution.py:188
  284.1 14.6 %fusion.38 = (f32[69,512]{1,0:T(8,128)S(1)}, f32[69,512]{1,0:T(8,128)S(1)}, f32[69,512]{1,0:T(8,128)S(1)}, f32[69,512]{1,0:T(8,128)S(1)}, f32[69,64,512]{2,1,0:T(8,128)}) fusion(bf16[69,64,512]{2,1,0:T(8,128)(2,1)} %param.45, bf16[3,69,64,512]{3,2,1,0:T(8,128)(2,1)} %param.28, f32[69,512]{1,0:T(8,128)S(1)} %get-tuple-element.237, ...), kind=kLoop, calls=%fused_computation.51 | loop fusion | flops 38295552 | bytes 28262400 | tf_op jit(solution)/shard_map/transpose(jvp())/reduce_sum | solution.py:205
  304.9 2.7 fusion.94
  307.8 28.5 %all-gather.9.cloned.1.call-done = bf16[2048,768]{1,0:T(8,128)(2,1)} async-done(((bf16[512,768]{1,0:T(8,128)(2,1)}), bf16[2048,768]{1,0:T(8,128)(2,1)}) %all-gather.9.cloned.1.call-update) | async-done | bytes 3145744 | tf_op jit(solution)/shard_map/all_gather | solution.py:227
  336.3 11.1 %convert_reduce_fusion.1 = (f32[768]{0:T(1024)}, bf16[2048,768]{1,0:T(8,128)(2,1)S(1)}) fusion(f32[2048,768]{1,0:T(8,128)} %get-tuple-element.223, f32[2048,768]{1,0:T(8,128)} %get-tuple-element.239, f32[768]{0:T(1024)S(1)} %copy-done.65, bf16[2048,768]{1,0:T(8,128)(2,1)} %all-gather.9.cloned.1.call-done, bf16[768,768]{1,0:T(8,128)(2,1)} %param.39), kind=kOutput, calls=%fused_computation.55 | convolution fusion | flops 2442657024 | bytes 20060160 | tf_op jit(solution)/shard_map/td,fd->tf/dot_general | solution.py:231
  349.1 4.5 fusion.99
  353.7 58.5 %reduce-scatter.9.cloned.1.call-done = f32[512,768]{1,0:T(8,128)} async-done(((f32[2048,768]{1,0:T(8,128)}), f32[512,768]{1,0:T(8,128)}) %reduce-scatter.9.cloned.1.call-update) | async-done | bytes 1572880 | tf_op jit(solution)/shard_map/reduce_scatter | solution.py:239
  412.2 2.7 multiply_reduce_fusion.2
  418.6 28.4 %all-gather.11.cloned.1.call-done = bf16[2048,768]{1,0:T(8,128)(2,1)} async-done(((bf16[512,768]{1,0:T(8,128)(2,1)}), bf16[2048,768]{1,0:T(8,128)(2,1)}) %all-gather.11.cloned.1.call-update) | async-done | bytes 3145744 | tf_op jit(solution)/shard_map/all_gather | solution.py:248
  447.0 4.0 convolution_convert_fusion
  450.9 115.3 %while.28 = (s32[]{:T(128)}, f32[2048,3,64]{0,2,1:T(8,128)}, f32[2048,3,64]{0,2,1:T(8,128)S(1)}, bf16[4,512,3,64]{1,3,2,0:T(8,128)(2,1)}, s32[4]{0:T(128)S(1)}, ...) while((s32[]{:T(128)}, f32[2048,3,64]{0,2,1:T(8,128)}, ...), condition=%wide.region_24.25_spmd.clone, body=%wide.region_22.24_spmd.clone.sunk | while | flops 2053077504 | bytes 129411376 | solution.py:103
  455.0 2.7 fusion.177
  457.8 3.5 fusion.179
  461.3 4.4 multiply_reduce_fusion.9
  465.8 4.7 multiply_convert_fusion.5
  470.5 5.6 fusion.180
  476.1 3.4 fusion.178
  483.3 2.8 fusion.177
  486.1 3.5 fusion.179
  489.6 4.4 multiply_reduce_fusion.9
  494.1 4.7 multiply_convert_fusion.5
  498.8 5.6 fusion.180
  504.4 4.0 fusion.178
  512.3 2.8 fusion.177
  515.0 3.5 fusion.179
  518.5 4.4 multiply_reduce_fusion.9
  523.0 4.7 multiply_convert_fusion.5
  527.7 5.6 fusion.180
  533.3 4.0 fusion.178
  541.2 2.8 fusion.177
  543.9 3.5 fusion.179
  547.5 4.4 multiply_reduce_fusion.9
  551.9 4.7 multiply_convert_fusion.5
  556.6 5.6 fusion.180
  562.3 4.0 fusion.178
  566.2 2.7 copy.43
  569.0 2.8 stack_reshape.12
  573.7 4.6 convolution_bitcast_fusion
  580.2 6.1 fusion.102
  586.3 4.2 fusion.101
  592.6 3.2 fusion.62
  599.2 22.1 %psum.121 = f32[768]{0:T(1024)} all-reduce(f32[768]{0:T(1024)S(1)} %copy-done.56), channel_id=1, replica_groups=mesh['dp'=8,'tp'=4] {'dp'}, use_global_device_ids=true, to_apply=%region_43.44 | all-reduce | flops 768 | bytes 6144 | tf_op jit(solution)/shard_map/psum | solution.py:269
  621.3 15.6 %reduce-scatter.11.cloned.1.call-done = f32[512,768]{1,0:T(8,128)} async-done(((f32[2048,768]{1,0:T(8,128)}), f32[512,768]{1,0:T(8,128)}) %reduce-scatter.11.cloned.1.call-update) | async-done | bytes 1572880 | tf_op jit(solution)/shard_map/reduce_scatter | solution.py:259
  641.2 44.4 %all-reduce.3 = (f32[768]{0:T(1024)}, f32[768]{0:T(1024)}, f32[768]{0:T(1024)}, f32[768]{0:T(1024)}, f32[768]{0:T(1024)}, /*index=5*/f32[768]{0:T(1024)}, f32[207]{0:T(256)}, f32[69]{0:T(128)}) all-reduce(f32[768]{0:T(1024)S(1)} %get-tuple-element.154, f32[768]{0:T(1024)S(1)} %get-tuple-element.157, ...), channel_id=1, replica_groups=mesh['dp'=8,'tp'=4] {'dp','tp'}, use_global_device_ids=true, to_apply=%region_29.30 | all-reduce | flops 4884 | bytes 39072 | tf_op jit(solution)/shard_map/psum | solution.py:284
  685.6 3.2 add_add_fusion.2
  688.7 190.5 %all-reduce.11.cloned.1.call-done = (f32[3,768,192]{1,2,0:T(8,128)}, f32[192,768]{1,0:T(8,128)}, f32[768,768]{1,0:T(8,128)}, f32[768,768]{1,0:T(8,128)}) async-done(((f32[3,768,192]{1,2,0:T(8,128)}, f32[192,768]{1,0:T(8,128)}, f32[768,768]{1,0:T(8,128)}, f32[768,768]{1,0:T(8,128)}), (f32[3,768,192]{1,2,0:T(8,128)}, f32[192,768]{1,0:T(8,128)}, f32[768,768]{1,0:T(8,128)}, ...) | async-done | bytes 7077904 | tf_op jit(solution)/shard_map/psum | solution.py:269
  879.3 136.9 %all-reduce.9.cloned.1.call-done = (f32[40,768]{1,0:T(8,128)}, f32[768,207]{0,1:T(8,128)}, f32[768,69]{0,1:T(8,128)}) async-done(((f32[40,768]{1,0:T(8,128)}, f32[768,207]{0,1:T(8,128)}, f32[768,69]{0,1:T(8,128)}), (f32[40,768]{1,0:T(8,128)}, f32[768,207]{0,1:T(8,128)}, f32[768,69]{0,1:T(8,128)})) %all-reduce.9.cloned.1.call-update) | async-done | bytes 970768 | tf_op jit(solution)/shard_map/psum | solution.py:284
  1017.9 2.8 copy.78
  (247 shorter events, 78.6 us)
Async XLA Ops:
  7.2 182.2 %copy-start = (bf16[768,768]{1,0:T(8,128)(2,1)S(1)}, bf16[768,768]{1,0:T(8,128)(2,1)}, u32[]{:S(2)}) copy-start(bf16[768,768]{1,0:T(8,128)(2,1)} %param.37) | copy-start | bytes 3538948
  7.2 38.2 %copy-start.63 = (bf16[3,768,192]{1,2,0:T(8,128)(2,1)S(1)}, bf16[3,768,192]{1,2,0:T(8,128)(2,1)}, u32[]{:S(2)}) copy-start(bf16[3,768,192]{1,2,0:T(8,128)(2,1)} %param.32) | copy-start | bytes 2654212
  7.2 38.1 %all-gather.5.cloned.1.call-start = ((), (), s32[]{:S(2)}) async-start(), calls=%async_computation.4 | async-start | bytes 3932160 | tf_op jit(solution)/shard_map/all_gather | solution.py:163
  9.4 39.9 %copy-start.37 = (f32[512]{0:T(512)}, f32[512]{0:T(512)S(1)}, u32[]{:S(2)}) copy-start(f32[512]{0:T(512)S(1)} %broadcast_multiply_fusion.1) | copy-start | bytes 6148
  10.9 38.4 %copy-start.43 = (f32[512]{0:T(512)}, f32[512]{0:T(512)S(1)}, u32[]{:S(2)}) copy-start(f32[512]{0:T(512)S(1)} %fusion.59) | copy-start | bytes 6148
  10.9 38.4 %copy-start.41 = (f32[512]{0:T(512)}, f32[512]{0:T(512)S(1)}, u32[]{:S(2)}) copy-start(f32[512]{0:T(512)S(1)} %fusion.79) | copy-start | bytes 6148
  10.9 38.4 %copy-start.51 = (s32[512]{0:T(512)}, s32[512]{0:T(512)S(1)}, u32[]{:S(2)}) copy-start(s32[512]{0:T(512)S(1)} %fusion.78) | copy-start | bytes 6148
  14.0 142.7 %reduce-scatter.5.cloned.1.call-start = ((), (), s32[]{:S(2)}) async-start(), calls=%async_computation.5 | async-start | bytes 7864320 | tf_op jit(solution)/shard_map/reduce_scatter | solution.py:170
  91.0 7.2 copy-start.4
  91.0 7.2 copy-start.11
  91.0 3.4 copy-start.34
  98.2 58.5 %copy-start.57 = (f32[768]{0:T(1024)S(1)}, f32[768]{0:T(1024)}, u32[]{:S(2)}) copy-start(f32[768]{0:T(1024)} %param.34) | copy-start | bytes 9220
  98.2 61.3 %copy-start.40 = (f32[768]{0:T(1024)S(1)}, f32[768]{0:T(1024)}, u32[]{:S(2)}) copy-start(f32[768]{0:T(1024)} %param.35) | copy-start | bytes 9220
  98.2 61.3 %copy-start.55 = (f32[768]{0:T(1024)S(1)}, f32[768]{0:T(1024)}, u32[]{:S(2)}) copy-start(f32[768]{0:T(1024)} %param.36) | copy-start | bytes 9220
  98.2 91.2 %all-gather.7.cloned.1.call-start = ((), (), s32[]{:S(2)}) async-start(), calls=%async_computation.6 | async-start | bytes 3932160 | tf_op jit(solution)/shard_map/all_gather | solution.py:182
  160.7 111.8 %reduce-scatter.7.cloned.1.call-start = ((), (), s32[]{:S(2)}) async-start(), calls=%async_computation.7 | async-start | bytes 7864320 | tf_op jit(solution)/shard_map/reduce_scatter | solution.py:188
  189.4 20.1 %copy-start.62 = (bf16[768,768]{1,0:T(8,128)(2,1)S(1)}, bf16[768,768]{1,0:T(8,128)(2,1)}, u32[]{:S(2)}) copy-start(bf16[768,768]{1,0:T(8,128)(2,1)} %param.39) | copy-start | bytes 3538948
  214.0 122.3 %all-gather.9.cloned.1.call-start = ((), (), s32[]{:S(2)}) async-start(), calls=%async_computation.8 | async-start | bytes 3932160 | tf_op jit(solution)/shard_map/all_gather | solution.py:227
  272.6 2.6 copy-start.23
  280.5 2.5 copy-start.9
  280.5 2.5 copy-start.33
  284.1 14.6 %copy-start.12 = (f32[512,3,69]{0,2,1:T(8,128)S(1)}, f32[512,3,69]{0,2,1:T(8,128)}, u32[]{:S(2)}) copy-start(f32[512,3,69]{0,2,1:T(8,128)} %reshape.213) | copy-start | bytes 1271812
  284.1 14.6 %copy-start.18 = (f32[512,69]{0,1:T(8,128)S(1)}, f32[512,69]{0,1:T(8,128)}, u32[]{:S(2)}) copy-start(f32[512,69]{0,1:T(8,128)} %reduce_max.18) | copy-start | bytes 423940
  303.4 33.0 %copy-start.65 = (f32[768]{0:T(1024)S(1)}, f32[768]{0:T(1024)}, u32[]{:S(2)}) copy-start(f32[768]{0:T(1024)} %param.38) | copy-start | bytes 9220
  307.6 104.6 %reduce-scatter.9.cloned.1.call-start = ((), (), s32[]{:S(2)}) async-start(), calls=%async_computation.9 | async-start | bytes 7864320 | tf_op jit(solution)/shard_map/reduce_scatter | solution.py:239
  353.7 61.3 %copy-start.46 = (f32[512]{0:T(512)S(1)}, f32[512]{0:T(512)}, u32[]{:S(2)}) copy-start(f32[512]{0:T(512)} %copy-done.45) | copy-start | bytes 6148
  353.7 93.3 %all-gather.11.cloned.1.call-start = ((), (), s32[]{:S(2)}) async-start(), calls=%async_computation.10 | async-start | bytes 3932160 | tf_op jit(solution)/shard_map/all_gather | solution.py:248
  412.2 2.8 copy-start.17
  416.3 30.7 %copy-start.35 = (bf16[192,768]{1,0:T(8,128)(2,1)S(1)}, bf16[192,768]{1,0:T(8,128)(2,1)}, u32[]{:S(2)}) copy-start(bf16[192,768]{1,0:T(8,128)(2,1)} %param.33) | copy-start | bytes 884740
  418.3 218.6 %reduce-scatter.11.cloned.1.call-start = ((), (), s32[]{:S(2)}) async-start(), calls=%async_computation.11 | async-start | bytes 7864320 | tf_op jit(solution)/shard_map/reduce_scatter | solution.py:259
  418.6 32.3 %copy-start.5 = (bf16[2048,3,64]{0,2,1:T(8,128)(2,1)S(1)}, bf16[2048,3,64]{0,2,1:T(8,128)(2,1)}, u32[]{:S(2)}) copy-start(bf16[2048,3,64]{0,2,1:T(8,128)(2,1)} %copy-done.4) | copy-start | bytes 2359300
  470.5 5.6 copy-start.2
  498.8 5.6 copy-start.2
  527.7 5.6 copy-start.2
  556.6 5.6 copy-start.2
  566.2 5.6 copy-start.3
  572.0 6.3 copy-start.28
  578.3 300.9 %all-reduce.11.cloned.1.call-start = ((), (), s32[]{:S(2)}) async-start(), calls=%async_computation.13 | async-start | bytes 14155776 | tf_op jit(solution)/shard_map/psum | solution.py:269
  580.2 6.1 copy-start.60
  580.2 6.1 copy-start.68
  586.3 4.2 copy-start.15
  586.3 4.2 copy-start.19
  586.3 5.9 copy-start.59
  590.5 2.1 copy-start.29
  595.9 2.1 copy-start.22
  595.9 3.3 copy-start.56
  595.9 40.9 %copy-start.6 = (bf16[512,768]{1,0:T(8,128)(2,1)S(1)}, bf16[512,768]{1,0:T(8,128)(2,1)}, u32[]{:S(2)}) copy-start(bf16[512,768]{1,0:T(8,128)(2,1)} %param.25) | copy-start | bytes 2359300
  595.9 40.9 %copy-start.38 = (f32[512]{0:T(512)S(1)}, f32[512]{0:T(512)}, u32[]{:S(2)}) copy-start(f32[512]{0:T(512)} %copy-done.37) | copy-start | bytes 6148
  595.9 40.9 %copy-start.39 = (f32[768]{0:T(1024)S(1)}, f32[768]{0:T(1024)}, u32[]{:S(2)}) copy-start(f32[768]{0:T(1024)} %param.29) | copy-start | bytes 9220
  596.0 42.9 %copy-start.44 = (f32[512]{0:T(512)S(1)}, f32[512]{0:T(512)}, u32[]{:S(2)}) copy-start(f32[512]{0:T(512)} %copy-done.43) | copy-start | bytes 6148
  596.0 42.9 %copy-start.53 = (s32[512]{0:T(512)S(1)}, s32[512]{0:T(512)}, u32[]{:S(2)}) copy-start(s32[512]{0:T(512)} %copy-done.51) | copy-start | bytes 6148
  596.0 420.2 %all-reduce.9.cloned.1.call-start = ((), (), s32[]{:S(2)}) async-start(), calls=%async_computation.12 | async-start | bytes 1966080 | tf_op jit(solution)/shard_map/psum | solution.py:284
  598.0 42.3 %copy-start.42 = (f32[512]{0:T(512)S(1)}, f32[512]{0:T(512)}, u32[]{:S(2)}) copy-start(f32[512]{0:T(512)} %copy-done.41) | copy-start | bytes 6148
  621.2 19.9 %copy-start.47 = (f32[768]{0:T(1024)S(1)}, f32[768]{0:T(1024)}, u32[]{:S(2)}) copy-start(f32[768]{0:T(1024)} %get-tuple-element.152) | copy-start | bytes 9220
  621.2 19.9 %copy-start.48 = (f32[768]{0:T(1024)S(1)}, f32[768]{0:T(1024)}, u32[]{:S(2)}) copy-start(f32[768]{0:T(1024)} %get-tuple-element.156) | copy-start | bytes 9220
  621.2 19.9 %copy-start.49 = (f32[768]{0:T(1024)S(1)}, f32[768]{0:T(1024)}, u32[]{:S(2)}) copy-start(f32[768]{0:T(1024)} %get-tuple-element.214) | copy-start | bytes 9220
  621.2 19.9 %copy-start.50 = (f32[768]{0:T(1024)S(1)}, f32[768]{0:T(1024)}, u32[]{:S(2)}) copy-start(f32[768]{0:T(1024)} %get-tuple-element.234) | copy-start | bytes 9220
  621.2 19.9 %copy-start.58 = (f32[69]{0:T(128)S(1)}, f32[69]{0:T(128)}, u32[]{:S(2)}) copy-start(f32[69]{0:T(128)} %get-tuple-element.210) | copy-start | bytes 832
  636.8 2.0 copy-start.7
  879.3 141.4 %copy-start.32 = (f32[192,768]{1,0:T(8,128)S(1)}, f32[192,768]{1,0:T(8,128)}, u32[]{:S(2)}) copy-start(f32[192,768]{1,0:T(8,128)} %get-tuple-element.438) | copy-start | bytes 1769476
  1016.2 5.3 copy-start.21
  1020.7 2.2 copy-start.20
  1021.5 4.4 copy-start.1
  1023.0 2.3 copy-start.36
  (18 other events, 23.3 us)
Sparse Core Ops, SparseCore 0:
  14.1 31.2 all-gather.4
  98.3 58.3 reduce-scatter.4
  160.8 28.5 all-gather.6
  214.1 58.3 reduce-scatter.6
  307.7 28.5 all-gather.8
  353.8 58.3 reduce-scatter.8
  418.4 28.5 all-gather.10
  578.5 58.3 reduce-scatter.10
  642.4 236.8 all-reduce.10
  887.4 128.8 all-reduce.8
where the time goes:
time: 1040 us; the launch traced here: 1030 us
  waiting for transfers between devices  633 us (61%)
  matrix products  189 us (18%)
  other arithmetic  72.4 us (7%)
  blocking collectives  66.5 us (6%)
  local copies, waits for them, and re-layouts  41.4 us (4%)
  between operations  16 us (2%)
  loops' own time  13.3 us (1%)
    psum x1, waiting for transfers between devices, body(): lax.psum((qkv_weight_grad, proj_weight_grad, in_weight_grad, in_bias_grad...  191 us
    psum x1, waiting for transfers between devices, body(): lax.psum((first_gain_grad, first_shift_grad, lead_table_grad, proj_bias_g...  137 us
    reduce_scatter x1, waiting for transfers between devices, body(): lax.psum_scatter(jnp.einsum('tf,df->td', hidden_low, widening_matrix, pre...  58.5 us
    reduce_scatter x1, waiting for transfers between devices, body(): lax.psum_scatter(jnp.dot(attended, attending_matrix, preferred_element_ty...  58.4 us
    reduce_scatter x1, waiting for transfers between devices, body(): lax.psum_scatter(jnp.dot(act_low, narrowing_matrix, preferred_element_typ...  56.9 us
    psum x1, blocking collectives, body(): lax.psum((first_gain_grad, first_shift_grad, lead_table_grad, proj_bias_g...  44.4 us
    all_gather x1, waiting for transfers between devices, body(): lax.all_gather(attn_in.astype(jnp.bfloat16), 'tp', axis=0, tiled=True)  31.3 us
    all_gather x1, waiting for transfers between devices, body(): mlp_out_rows = lax.all_gather(grad_low, 'tp', axis=0, tiled=True)  28.5 us
  transfers between devices with their start and end apart: 10, of which 10 were waited for; matrix products, arithmetic and copies ran while one was open for 2% of the time, Pallas kernels for 0%

commit v1 on v0

v1 whole, which is shorter than its diff:
```python
import functools
import jax
import jax.numpy as jnp
from jax import lax
from jax.experimental import pallas as pl
from jax.experimental.pallas import tpu as pltpu
from jax.sharding import PartitionSpec as P

HD = 64
EXPERTS = 3
EPSILON = 1e-05
F32 = jnp.float32
BF16 = jnp.bfloat16


def dot(a, b, dims=((1,), (0,))):
    return lax.dot_general(a, b, (dims, ((), ())), preferred_element_type=F32)


def fwd_kernel(q_ref, k_ref, v_ref, o_ref, lse_ref, ks, *, scale):
    @pl.when(pl.program_id(1) == 0)
    def _():
        ks[...] = k_ref[0, 0].T

    q = q_ref[0, 0] * jnp.bfloat16(scale)
    s = dot(ks[...], q)
    m = jnp.max(s, axis=0, keepdims=True)
    p = jnp.exp(s - m)
    l = jnp.sum(p, axis=0, keepdims=True)
    o = dot(v_ref[0, 0], p.astype(BF16))
    o_ref[0] = (o / l).astype(BF16)
    lse_ref[0] = m + jnp.log(l)


def attn_fwd(qkv, scale, bq):
    _, heads, _, rows = qkv.shape
    return pl.pallas_call(
        functools.partial(fwd_kernel, scale=scale),
        grid=(heads, rows // bq),
        in_specs=[
            pl.BlockSpec((1, 1, HD, bq), lambda h, i: (0, h, 0, i)),
            pl.BlockSpec((1, 1, HD, rows), lambda h, i: (1, h, 0, 0)),
            pl.BlockSpec((1, 1, HD, rows), lambda h, i: (2, h, 0, 0)),
        ],
        out_specs=[
            pl.BlockSpec((1, HD, bq), lambda h, i: (h, 0, i)),
            pl.BlockSpec((1, 1, bq), lambda h, i: (h, 0, i)),
        ],
        out_shape=[
            jax.ShapeDtypeStruct((heads, HD, rows), BF16),
            jax.ShapeDtypeStruct((heads, 1, rows), F32),
        ],
        scratch_shapes=[pltpu.VMEM((rows, HD), BF16)],
        compiler_params=pltpu.CompilerParams(vmem_limit_bytes=50 << 20),
        cost_estimate=pl.CostEstimate(
            flops=24_000_000_000, bytes_accessed=4 << 20, transcendentals=heads * rows * rows
        ),
        name="attn_fwd",
    )(qkv, qkv, qkv)


def bwd_kernel(
    q_ref, k_ref, v_ref, o_ref, do_ref, lse_ref, dq_ref, dk_ref, dv_ref, ks, vs, dks, dvs, *, scale
):
    i = pl.program_id(1)

    @pl.when(i == 0)
    def _():
        ks[...] = k_ref[0, 0].T
        vs[...] = v_ref[0, 0].T
        dks[...] = jnp.zeros_like(dks)
        dvs[...] = jnp.zeros_like(dvs)

    qt = q_ref[0, 0] * jnp.bfloat16(scale)
    dot_t = do_ref[0]
    dsum = jnp.sum(dot_t.astype(F32) * o_ref[0].astype(F32), axis=0, keepdims=True)
    s = dot(ks[...], qt)
    p = jnp.exp(s - lse_ref[0])
    dp = dot(vs[...], dot_t)
    ds = (p * (dp - dsum)).astype(BF16)
    dq_ref[0] = (dot(k_ref[0, 0], ds) * scale).astype(BF16)
    dvs[...] += dot(p.astype(BF16), dot_t.T)
    dks[...] += dot(ds, qt.T)

    @pl.when(i == pl.num_programs(1) - 1)
    def _():
        dk_ref[0] = dks[...].astype(BF16).T
        dv_ref[0] = dvs[...].astype(BF16).T


def attn_bwd(qkv, o, do, lse, scale, bq):
    _, heads, _, rows = qkv.shape

    def blk(j):
        return pl.BlockSpec((1, 1, HD, bq), lambda h, i: (j, h, 0, i))

    def full(j):
        return pl.BlockSpec((1, 1, HD, rows), lambda h, i: (j, h, 0, 0))

    return pl.pallas_call(
        functools.partial(bwd_kernel, scale=scale),
        grid=(heads, rows // bq),
        in_specs=[
            blk(0),
            full(1),
            full(2),
            pl.BlockSpec((1, HD, bq), lambda h, i: (h, 0, i)),
            pl.BlockSpec((1, HD, bq), lambda h, i: (h, 0, i)),
            pl.BlockSpec((1, 1, bq), lambda h, i: (h, 0, i)),
        ],
        out_specs=[
            pl.BlockSpec((1, HD, bq), lambda h, i: (h, 0, i)),
            pl.BlockSpec((1, HD, rows), lambda h, i: (h, 0, 0)),
            pl.BlockSpec((1, HD, rows), lambda h, i: (h, 0, 0)),
        ],
        out_shape=[jax.ShapeDtypeStruct((heads, HD, rows), BF16)] * 3,
        scratch_shapes=[pltpu.VMEM((rows, HD), BF16)] * 2 + [pltpu.VMEM((rows, HD), F32)] * 2,
        compiler_params=pltpu.CompilerParams(vmem_limit_bytes=50 << 20),
        cost_estimate=pl.CostEstimate(
            flops=46_000_000_000, bytes_accessed=8 << 20, transcendentals=heads * rows * rows
        ),
        name="attn_bwd",
    )(qkv, qkv, qkv, o, do, lse)


def norm_parts(values):
    center = values - jnp.mean(values, axis=-1, keepdims=True)
    rstd = lax.rsqrt(jnp.mean(center * center, axis=-1, keepdims=True) + EPSILON)
    return center * rstd, rstd


def norm_back(hat, rstd, gain, grad):
    g = grad * gain
    return rstd * (
        g
        - jnp.mean(g, axis=-1, keepdims=True)
        - hat * jnp.mean(g * hat, axis=-1, keepdims=True)
    )


def gelu_parts(u):
    half = jnp.exp(-0.5 * u * u)
    t = 1.0 / (1.0 + (0.3275911 * 0.7071067811865476) * jnp.abs(u))
    poly = t * (
        0.254829592
        + t * (-0.284496736 + t * (1.421413741 + t * (-1.453152027 + t * 1.061405429)))
    )
    tail = 0.5 * poly * half
    cdf = jnp.where(u >= 0, 1.0 - tail, tail)
    return u * cdf, cdf + u * half * 0.3989422804014327


def make_body(mesh):
    dp_size, tp_size = mesh.shape["dp"], mesh.shape["tp"]
    dp_bits = [1 << b for b in range(dp_size.bit_length() - 1)]

    def swap(x, axis, bit):
        size = dp_size if axis == "dp" else tp_size
        return lax.ppermute(x, axis, [(i, i ^ bit) for i in range(size)])

    def core(x):
        return swap(x, "tp", 1)

    def across(x):
        return swap(x, "tp", 2)

    def diag(x):
        return swap(x, "tp", 3)

    def my_bit(bit):
        return (lax.axis_index("dp") & bit) != 0

    def fold_tp(parts, cast=BF16):
        got1 = core(parts[3].astype(cast))
        got0 = core(parts[1].astype(cast))
        mid = parts[2].astype(F32) + got1.astype(F32)
        own = parts[0].astype(F32) + got0.astype(F32)
        return own + across(mid.astype(cast)).astype(F32)

    def dp_sum(x, bits):
        for bit in bits:
            n = x.shape[0] // 2
            lo, hi = x[:n], x[n:]
            mine = my_bit(bit)
            send = jnp.where(mine, lo, hi).astype(BF16)
            keep = jnp.where(mine, hi, lo).astype(F32)
            x = keep + swap(send, "dp", bit).astype(F32)
        x = x.astype(BF16)
        for bit in reversed(bits):
            got = swap(x, "dp", bit)
            mine = my_bit(bit)
            x = jnp.concatenate([jnp.where(mine, got, x), jnp.where(mine, x, got)], axis=0)
        return x

    def dp_sum_halves(x):
        n = x.shape[0] // 2
        order = list(dp_bits)
        if n % dp_size:
            return dp_sum(x, order).astype(F32)
        other = [order[1], order[0]] + order[2:]
        return jnp.concatenate([dp_sum(x[:n], order), dp_sum(x[n:], other)], axis=0).astype(F32)

    def butterfly_dp(x):
        for bit in dp_bits:
            x = x + swap(x, "dp", bit)
        return x

    def butterfly_all(x):
        x = x + core(x)
        x = x + across(x)
        return butterfly_dp(x)

    def gather_tp(x):
        n = x.shape[0] // 2
        mine = my_bit(1)
        half = across(jnp.where(mine, x[n:], x[:n]))
        other = swap(half, "dp", 1)
        far = jnp.concatenate([jnp.where(mine, other, half), jnp.where(mine, half, other)], axis=0)
        return [x, core(x), far, core(far)]

    def body(
        tile_vectors,
        snapshot_horizon_slot,
        horizon_sample_tally,
        specialist_outlooks,
        early_layernorm_scale,
        early_layernorm_shift,
        horizon_vectors,
        triple_head_matrix,
        attending_matrix,
        attending_offset,
        later_layernorm_scale,
        later_layernorm_shift,
        widening_matrix,
        widening_offset,
        narrowing_matrix,
        narrowing_offset,
        router_matrix,
        router_offset,
        adjuster_matrix,
        adjuster_offset,
        combined_loss_slope,
    ):
        rows_dev, width = tile_vectors.shape
        heads = triple_head_matrix.shape[2] // HD
        rows_frame = rows_dev * tp_size
        fields = adjuster_matrix.shape[1]
        sites = combined_loss_slope.shape[1]
        scale_val = HD ** (-0.5)
        tp_index = lax.axis_index("tp")
        lead = snapshot_horizon_slot[0]
        embed = lax.dynamic_slice_in_dim(horizon_vectors, lead, 1, 0)
        row_scale = lax.rsqrt(
            lax.dynamic_slice_in_dim(horizon_sample_tally, lead, 1, 0).astype(F32)
        )[0]
        residual = tile_vectors.astype(F32)

        hat1, rstd1 = norm_parts(residual)
        attn_own = (hat1 * early_layernorm_scale + early_layernorm_shift + embed).astype(BF16)
        rows2 = across(attn_own)
        rows1 = core(attn_own)
        rows3 = core(rows2)
        rows2, rows3, triple_w, proj_w, wide_w, narrow_w = lax.optimization_barrier(
            (rows2, rows3, triple_head_matrix, attending_matrix, widening_matrix, narrowing_matrix)
        )
        attn_rows = jnp.concatenate([attn_own, rows1, rows2, rows3], axis=0)

        proj_all = gather_tp(proj_w)
        wide_all = gather_tp(wide_w)
        narrow_all = gather_tp(narrow_w)
        off2 = across(widening_offset)
        off_all = [widening_offset, core(widening_offset), off2, core(off2)]

        qkv = jnp.einsum(
            "sdh,td->sht", triple_w, attn_rows, preferred_element_type=F32
        ).astype(BF16)
        qkv = qkv.reshape(3, heads, HD, rows_frame)
        o_heads, lse = attn_fwd(qkv, scale_val, min(512, rows_frame))

        slope = combined_loss_slope.astype(F32)
        expert_dot = jnp.stack(
            [
                jnp.sum(specialist_outlooks[e].astype(F32) * slope, axis=1)
                for e in range(EXPERTS)
            ]
        )
        slope_sum = jnp.sum(slope, axis=1)

        o_flat = o_heads.reshape(heads * HD, rows_frame)
        ob = [o_flat[:, p * rows_dev : (p + 1) * rows_dev] for p in range(tp_size)]
        o_own = jnp.concatenate([ob[0], core(ob[1]), across(ob[2]), diag(ob[3])], axis=0)
        proj_cat = jnp.concatenate(proj_all, axis=0)
        x1 = residual + dot(o_own, proj_cat, ((0,), (0,))) + attending_offset
        hat2, rstd2 = norm_parts(x1)
        c_low = (hat2 * later_layernorm_scale + later_layernorm_shift).astype(BF16)
        acts, slopes = [], []
        for p in range(tp_size):
            m, d = gelu_parts(dot(c_low, wide_all[p]) + off_all[p])
            acts.append(m.astype(BF16))
            slopes.append(d)
        mlp = dot(acts[0], narrow_all[0])
        for p in range(1, tp_size):
            mlp = mlp + dot(acts[p], narrow_all[p])
        x2 = x1 + mlp + narrowing_offset
        h_low = x2.astype(BF16)
        logits = dot(router_matrix, h_low, ((0,), (1,))) + router_offset[:, None]
        corr = (dot(adjuster_matrix, h_low, ((0,), (1,))) + adjuster_offset[:, None]) * row_scale
        logits = logits.reshape(EXPERTS, fields, rows_dev)
        top = jnp.max(logits, axis=0, keepdims=True)
        raised = jnp.exp(logits - top)
        gates = raised / jnp.sum(raised, axis=0, keepdims=True)
        mixed = jnp.sum(gates * expert_dot, axis=0, keepdims=True)
        dlog = (gates * (expert_dot - mixed)).astype(BF16).reshape(EXPERTS * fields, rows_dev)
        dcorr = (slope_sum * row_scale).astype(BF16)

        head_grads = jnp.concatenate([dlog, dcorr], axis=0)
        head_w = jnp.concatenate([router_matrix, adjuster_matrix], axis=1)
        dx2 = dot(head_grads, head_w, ((0,), (1,)))
        dz = dx2.astype(BF16)
        d_narrow = [dot(acts[p], dz, ((0,), (0,))).astype(BF16) for p in range(tp_size)]
        dus = [
            (dot(dz, narrow_all[p], ((1,), (1,))) * slopes[p]).astype(BF16) for p in range(tp_size)
        ]
        d_wide = [dot(c_low, dus[p], ((0,), (0,))).astype(BF16) for p in range(tp_size)]
        dc = dot(dus[0], wide_all[0], ((1,), (1,)))
        for p in range(1, tp_size):
            dc = dc + dot(dus[p], wide_all[p], ((1,), (1,)))
        dx1 = dx2 + norm_back(hat2, rstd2, later_layernorm_scale, dc)
        dy = dx1.astype(BF16)
        do_all = dot(proj_cat, dy, ((1,), (1,))).astype(BF16)
        nh = heads * HD
        db = [do_all[p * nh : (p + 1) * nh] for p in range(tp_size)]
        do = jnp.concatenate([db[0], core(db[1]), across(db[2]), diag(db[3])], axis=1)
        do = do.reshape(heads, HD, rows_frame)
        dqt, dkt, dvt = attn_bwd(qkv, o_heads, do, lse, scale_val, min(512, rows_frame))

        blended = (corr)[:, None, :]
        for e in range(EXPERTS):
            blended = blended + gates[e][:, None, :] * specialist_outlooks[e].astype(F32)

        d_proj = dot(o_own, dy, ((1,), (0,))).astype(BF16)
        d_head = dot(h_low, head_grads, ((0,), (1,))).astype(BF16)
        d_head = jnp.pad(d_head, ((0, 0), (0, (-d_head.shape[1]) % 128)))
        dproj_parts = []
        for p in range(tp_size):
            head_blk = lax.dynamic_slice_in_dim(d_head, (tp_index ^ p) * nh, nh, 0)
            dproj_parts.append(
                jnp.concatenate([d_proj[p * nh : (p + 1) * nh], head_blk], axis=1)
            )

        narrow_sum = dp_sum_halves(fold_tp(d_narrow))
        wide_sum = dp_sum_halves(fold_tp(d_wide))
        proj_sum = dp_sum_halves(fold_tp(dproj_parts))
        proj_weight_grad = proj_sum[:, :width]
        head_own = proj_sum[:, width:].astype(BF16)
        h2 = across(head_own)
        head_parts = [head_own, core(head_own), h2, core(h2)]
        head_sum = jnp.zeros((width, head_own.shape[1]), BF16)
        for p in range(tp_size):
            head_sum = lax.dynamic_update_slice_in_dim(
                head_sum, head_parts[p], (tp_index ^ p) * nh, 0
            )
        head_sum = head_sum.astype(F32)
        gate_weight_grad = head_sum[:, : EXPERTS * fields]
        correct_weight_grad = head_sum[:, EXPERTS * fields : (EXPERTS + 1) * fields]

        head_bias = jnp.sum(head_grads.astype(F32), axis=1)
        head_bias = jnp.pad(head_bias, (0, width - head_bias.shape[0]))
        small = jnp.stack(
            [
                jnp.sum(dx2, axis=0),
                jnp.sum(dc * hat2, axis=0),
                jnp.sum(dc, axis=0),
                jnp.sum(dx1, axis=0),
                head_bias,
            ]
        )
        small = butterfly_all(small)
        in_parts = [jnp.sum(dus[p].astype(F32), axis=0) for p in range(tp_size)]
        in_bias_grad = butterfly_dp(fold_tp(in_parts, F32))

        dqkv = jnp.stack([dqt, dkt, dvt]).reshape(3, nh, rows_frame)
        d_qkv = jnp.einsum("td,sht->sdh", attn_rows, dqkv, preferred_element_type=F32)
        qkv_sum = dp_sum_halves(d_qkv.reshape(3 * width, nh)).reshape(3, width, nh)
        da_parts = [
            jnp.einsum(
                "sht,sdh->td",
                dqkv[:, :, p * rows_dev : (p + 1) * rows_dev],
                triple_w,
                preferred_element_type=F32,
            )
            for p in range(tp_size)
        ]
        da = fold_tp(da_parts)
        tokens_grad = dx1 + norm_back(hat1, rstd1, early_layernorm_scale, da)
        da_sum = jnp.sum(da, axis=0)
        last = jnp.stack([jnp.sum(da * hat1, axis=0), da_sum])
        last = last + core(last)
        last = last + across(last)
        leads = horizon_vectors.shape[0]
        onehot = (jnp.arange(leads, dtype=jnp.int32) == lead).astype(F32)
        table = jnp.concatenate([last, onehot[:, None] * last[1][None, :]], axis=0)
        table = butterfly_dp(table)

        return (
            blended,
            tokens_grad,
            table[0],
            table[1],
            table[2:],
            qkv_sum,
            proj_weight_grad,
            small[3],
            small[1],
            small[2],
            wide_sum,
            in_bias_grad,
            narrow_sum,
            small[0],
            gate_weight_grad,
            small[4, : EXPERTS * fields],
            correct_weight_grad,
            small[4, EXPERTS * fields : (EXPERTS + 1) * fields],
        )

    return body


def solution(mesh):
    return jax.shard_map(
        make_body(mesh),
        mesh=mesh,
        in_specs=(
            P(("dp", "tp"), None),
            P("dp"),
            P(),
            P(None, None, None, ("dp", "tp")),
            P(),
            P(),
            P(),
            P(None, None, "tp"),
            P("tp", None),
            P(),
            P(),
            P(),
            P(None, "tp"),
            P("tp"),
            P("tp", None),
            P(),
            P(),
            P(),
            P(),
            P(),
            P(None, None, ("dp", "tp")),
        ),
        out_specs=(
            P(None, None, ("dp", "tp")),
            P(("dp", "tp"), None),
            P(),
            P(),
            P(),
            P(None, None, "tp"),
            P("tp", None),
            P(),
            P(),
            P(),
            P(None, "tp"),
            P("tp"),
            P("tp", None),
            P(),
            P(),
            P(),
            P(),
            P(),
        ),
        check_vma=False,
    )
```

time: 1040 us -> 550 us (0.53)
  waiting for transfers between devices: 633 us -> 218 us
  matrix products: 189 us -> 68 us
  starting transfers between devices: 1.3 us -> 73.4 us
  blocking collectives: 66.5 us -> 0 us
  Pallas kernels: 0 us -> 62.1 us
  local copies, waits for them, and re-layouts: 41.4 us -> 59 us
  other arithmetic: 72.4 us -> 57.7 us
  loops' own time: 13.3 us -> 0 us
  between operations: 16 us -> 4.24 us
    psum x2 -> x0, waiting for transfers between devices: 327 us -> none  [the longest x1 191 us: body(): lax.psum((qkv_weight_grad, proj_weight_grad, in_weight_grad, in_bias_grad...]
    ppermute x0 -> x103, waiting for transfers between devices: none -> 218 us  [swap(): return lax.ppermute(x, axis, [(i, i ^ bit) for i in range(size)])]
    reduce_scatter x4 -> x0, waiting for transfers between devices: 189 us -> none  [the longest x1 58.5 us: body(): lax.psum_scatter(jnp.einsum('tf,df->td', hidden_low, widening_matrix, pre...]
    dot_general x48 -> x37, matrix products: 185 us -> 68 us  [the longest x31 52.6 us: dot(): return lax.dot_general(a, b, (dims, ((), ())), preferred_element_type=F32)]
    all_gather x4 -> x0, waiting for transfers between devices: 116 us -> none  [the longest x1 31.3 us: body(): lax.all_gather(attn_in.astype(jnp.bfloat16), 'tp', axis=0, tiled=True)]
    ppermute x0 -> x103, starting transfers between devices: none -> 73.4 us  [swap(): return lax.ppermute(x, axis, [(i, i ^ bit) for i in range(size)])]
    psum x2 -> x0, blocking collectives: 66.5 us -> none  [the longest x1 44.4 us: body(): lax.psum((first_gain_grad, first_shift_grad, lead_table_grad, proj_bias_g...]
    pallas_call x0 -> x2, Pallas kernels: none -> 62.1 us  [the longest x1 36.8 us: attn_bwd(): pl.pallas_call(functools.partial(bwd_kernel, scale=scale), grid=(heads, r...]
  transfers between devices with their start and end apart: 10 -> 103, of which waited for: 10 -> 60; matrix products, arithmetic and copies ran while one was open for 2% -> 22% of each run, Pallas kernels for 0% -> 11%
where the time goes in v1:
time: 550 us; the launch traced here: 543 us
  waiting for transfers between devices  218 us (40%)
  starting transfers between devices  73.4 us (13%)
  matrix products  68 us (12%)
  Pallas kernels  62.1 us (11%)
  local copies, waits for them, and re-layouts  59 us (11%)
  other arithmetic  57.7 us (10%)
    ppermute x103, waiting for transfers between devices, swap(): return lax.ppermute(x, axis, [(i, i ^ bit) for i in range(size)])  218 us
    ppermute x103, starting transfers between devices, swap(): return lax.ppermute(x, axis, [(i, i ^ bit) for i in range(size)])  73.4 us
    dot_general x31, matrix products, dot(): return lax.dot_general(a, b, (dims, ((), ())), preferred_element_type=F32)  52.6 us
    pallas_call x1, Pallas kernels, attn_bwd(): pl.pallas_call(functools.partial(bwd_kernel, scale=scale), grid=(heads, r...  36.8 us
    pallas_call x1, Pallas kernels, attn_fwd(): pl.pallas_call(functools.partial(fwd_kernel, scale=scale), grid=(heads, r...  25.4 us
    dynamic_update_slice x4, local copies, waits for them, and re-layouts, body(): lax.dynamic_update_slice_in_dim(head_sum, head_parts[p], (tp_index ^ p) *...  13.4 us
  transfers between devices with their start and end apart: 103, of which 60 were waited for; matrix products, arithmetic and copies ran while one was open for 22% of the time, Pallas kernels for 11%

profile of v1, /device:TPU:0, one launch (start us, length us, event | category | flops | bytes accessed | tf_op | source)
XLA Modules:
  0.0 542.9 jit_solution(5298556128816194665)
XLA Ops:
  5.6 3.0 collective-permute-start
  8.8 17.4 %collective-permute-done = bf16[512,768]{1,0:T(8,128)(2,1)S(1)} collective-permute-done((bf16[512,768]{1,0:T(8,128)(2,1)S(1)}, bf16[512,768]{1,0:T(8,128)(2,1)S(1)}, u32[]{:S(2)}, u32[]{:S(2)}) %collective-permute-start) | collective-permute-done | bytes 786464 | tf_op jit(solution)/shard_map/ppermute | solution.py:159
  26.2 10.2 %fusion.3 = (f32[69,512]{1,0:T(8,128)}, f32[69,512]{1,0:T(8,128)}, f32[69,512]{1,0:T(8,128)}, f32[69,512]{1,0:T(8,128)S(1)}) fusion(bf16[69,64,512]{2,1,0:T(8,128)(2,1)} %param.41, bf16[3,69,64,512]{3,2,1,0:T(8,128)(2,1)} %param.24), kind=kLoop, calls=%fused_computation.10 | loop fusion | flops 24729600 | bytes 18653184 | tf_op jit(solution)/shard_map/reduce_sum | solution.py:283
  40.5 3.4 convolution_convert_fusion
  43.9 25.4 %attn_fwd.1 = (bf16[3,64,2048]{2,1,0:T(8,128)(2,1)S(1)}, f32[3,1,2048]{2,1,0:T(1,128)S(1)}) custom-call(bf16[3,3,64,2048]{3,2,1,0:T(8,128)(2,1)S(1)} %bitcast.128, bf16[3,3,64,2048]{3,2,1,0:T(8,128)(2,1)S(1)} %bitcast.129, bf16[3,3,64,2048]{3,2,1,0:T(8,128)(2,1)S(1)} %bitcast.130), custom_call_target="tpu_custom_call" | custom-call | flops 24000000000 | bytes 4194304 | tf_op jit(solution)/shard_map/attn_fwd/pallas_call | solution.py:37
  73.0 2.2 collective-permute-done.8
  79.4 2.8 collective-permute-done.5
  84.7 11.0 %collective-permute-done.13 = bf16[384,768]{1,0:T(8,128)(2,1)S(1)} collective-permute-done((bf16[384,768]{1,0:T(8,128)(2,1)S(1)}, bf16[384,768]{1,0:T(8,128)(2,1)S(1)}, u32[]{:S(2)}, u32[]{:S(2)}) %collective-permute-start.13) | collective-permute-done | bytes 589856 | tf_op jit(solution)/shard_map/ppermute | solution.py:159
  96.2 2.9 multiply_convert_fusion.3
  99.0 8.8 %collective-permute-done.16 = bf16[384,768]{1,0:T(8,128)(2,1)S(1)} collective-permute-done((bf16[384,768]{1,0:T(8,128)(2,1)S(1)}, bf16[384,768]{1,0:T(8,128)(2,1)S(1)}, u32[]{:S(2)}, u32[]{:S(2)}) %collective-permute-start.16) | collective-permute-done | bytes 589856 | tf_op jit(solution)/shard_map/ppermute | solution.py:159
  110.3 12.4 %collective-permute-done.17 = bf16[384,768]{1,0:T(8,128)(2,1)S(1)} collective-permute-done((bf16[384,768]{1,0:T(8,128)(2,1)S(1)}, bf16[384,768]{1,0:T(8,128)(2,1)S(1)}, u32[]{:S(2)}, u32[]{:S(2)}) %collective-permute-start.17) | collective-permute-done | bytes 589856 | tf_op jit(solution)/shard_map/ppermute | solution.py:159
  124.7 2.9 multiply_convert_fusion.2
  127.6 2.9 multiply_convert_fusion.1
  131.5 2.8 multiply_convert_fusion
  143.6 2.2 multiply_reduce_fusion.5
  163.6 2.4 convert_reduce_fusion.5
  168.0 2.4 convert_reduce_fusion.3
  170.5 2.4 convert_reduce_fusion.2
  176.5 2.6 convert_reduce_fusion.4
  194.8 2.1 fusion.82
  199.4 9.1 %fusion.2 = f32[69,64,512]{2,1,0:T(8,128)} fusion(f32[69,512]{1,0:T(8,128)S(1)} %get-tuple-element.150, f32[69,512]{1,0:T(8,128)S(1)} %get-tuple-element.151, f32[69,512]{1,0:T(8,128)S(1)} %get-tuple-element.149, f32[69,512]{1,0:T(8,128)S(1)} %fusion.54, bf16[3,69,64,512]{3,2,1,0:T(8,128)(2,1)} %param.24), kind=kLoop, calls=%fused_computation.9 | loop fusion | flops 20348928 | bytes 23175168 | tf_op jit(solution)/shard_map/add | solution.py:339
  219.9 2.6 collective-permute-start.84
  230.9 4.1 collective-permute-done.23
  236.0 36.8 %attn_bwd.1 = (bf16[3,64,2048]{2,1,0:T(8,128)(2,1)S(1)}, bf16[3,64,2048]{2,1,0:T(8,128)(2,1)S(1)}, bf16[3,64,2048]{2,1,0:T(8,128)(2,1)S(1)}) custom-call(bf16[3,3,64,2048]{3,2,1,0:T(8,128)(2,1)} %bitcast.131, bf16[3,3,64,2048]{3,2,1,0:T(8,128)(2,1)} %bitcast.132, bf16[3,3,64,2048]{3,2,1,0:T(8,128)(2,1)} %bitcast.133, ...), custom_call_target="tpu_custom_call" | custom-call | flops 46000001024 | bytes 8388608 | tf_op jit(solution)/shard_map/attn_bwd/pallas_call | solution.py:100
  274.2 4.2 convolution_bitcast_fusion
  284.1 2.7 collective-permute-done.32
  291.5 2.1 collective-permute-done.39
  295.3 2.1 collective-permute-start.40
  297.7 4.4 collective-permute-done.40
  303.1 7.3 %collective-permute-done.34 = bf16[144,192]{0,1:T(8,128)(2,1)S(1)} collective-permute-done((bf16[144,192]{0,1:T(8,128)(2,1)S(1)}, bf16[144,192]{0,1:T(8,128)(2,1)S(1)}, u32[]{:S(2)}, u32[]{:S(2)}) %collective-permute-start.34) | collective-permute-done | bytes 55328 | tf_op jit(solution)/shard_map/ppermute | solution.py:159
  310.5 7.0 %collective-permute-done.41 = bf16[144,192]{0,1:T(8,128)(2,1)S(1)} collective-permute-done((bf16[144,192]{0,1:T(8,128)(2,1)S(1)}, bf16[144,192]{0,1:T(8,128)(2,1)S(1)}, u32[]{:S(2)}, u32[]{:S(2)}) %collective-permute-start.41) | collective-permute-done | bytes 55328 | tf_op jit(solution)/shard_map/ppermute | solution.py:159
  317.7 5.4 collective-permute-done.35
  324.1 4.1 collective-permute-done.42
  328.5 4.9 collective-permute-done.36
  336.1 6.1 %collective-permute-done.43 = bf16[576,192]{0,1:T(8,128)(2,1)S(1)} collective-permute-done((bf16[576,192]{0,1:T(8,128)(2,1)S(1)}, bf16[576,192]{0,1:T(8,128)(2,1)S(1)}, u32[]{:S(2)}, u32[]{:S(2)}) %collective-permute-start.43) | collective-permute-done | bytes 221216 | tf_op jit(solution)/shard_map/ppermute | solution.py:159
  343.2 6.0 %collective-permute-done.37 = bf16[576,192]{0,1:T(8,128)(2,1)S(1)} collective-permute-done((bf16[576,192]{0,1:T(8,128)(2,1)S(1)}, bf16[576,192]{0,1:T(8,128)(2,1)S(1)}, u32[]{:S(2)}, u32[]{:S(2)}) %collective-permute-start.37) | collective-permute-done | bytes 221216 | tf_op jit(solution)/shard_map/ppermute | solution.py:159
  360.5 3.5 collective-permute-done.48
  365.2 3.0 collective-permute-done.54
  369.3 4.2 collective-permute-done.49
  374.3 4.2 collective-permute-done.55
  379.1 4.2 collective-permute-done.50
  384.0 4.2 collective-permute-done.56
  388.4 3.9 collective-permute-done.51
  393.5 3.0 collective-permute-done.57
  397.2 3.1 add_convert_fusion
  401.1 3.1 add_convert_fusion.1
  405.9 4.5 collective-permute-done.58
  412.6 4.4 collective-permute-done.26
  417.0 2.5 fusion.19
  424.0 3.2 dynamic_update_slice.12
  430.3 3.7 dynamic_update_slice.13
  435.7 2.9 dynamic_update_slice.14
  441.1 3.6 dynamic_update_slice.15
  447.1 4.7 collective-permute-done.29
  452.1 5.0 collective-permute-done.30
  458.5 3.2 fusion.18
  461.7 3.2 collective-permute-done.31
  466.2 2.2 convert_add_fusion.1
  469.3 11.9 %collective-permute-done.66 = bf16[768,768]{1,0:T(8,128)(2,1)} collective-permute-done((bf16[768,768]{1,0:T(8,128)(2,1)}, bf16[768,768]{1,0:T(8,128)(2,1)}, u32[]{:S(2)}, u32[]{:S(2)}) %collective-permute-start.66) | collective-permute-done | bytes 1179680 | tf_op jit(solution)/shard_map/ppermute | solution.py:159
  487.6 5.5 %collective-permute-done.67 = bf16[192,768]{1,0:T(8,128)(2,1)S(1)} collective-permute-done((bf16[192,768]{1,0:T(8,128)(2,1)S(1)}, bf16[192,768]{1,0:T(8,128)(2,1)S(1)}, u32[]{:S(2)}, u32[]{:S(2)}) %collective-permute-start.67) | collective-permute-done | bytes 294944 | tf_op jit(solution)/shard_map/ppermute | solution.py:159
  504.2 4.8 collective-permute-done.90
  513.6 3.3 collective-permute-done.75
  517.1 2.2 collective-permute-done.91
  531.7 6.0 %collective-permute-done.93 = bf16[192,768]{1,0:T(8,128)(2,1)S(1)} collective-permute-done((bf16[192,768]{1,0:T(8,128)(2,1)S(1)}, bf16[192,768]{1,0:T(8,128)(2,1)S(1)}, u32[]{:S(2)}, u32[]{:S(2)}) %collective-permute-start.93) | collective-permute-done | bytes 294944 | tf_op jit(solution)/shard_map/ppermute | solution.py:159
  (586 shorter events, 194.7 us)
Async XLA Ops:
  5.6 20.6 %collective-permute-start = (bf16[512,768]{1,0:T(8,128)(2,1)S(1)}, bf16[512,768]{1,0:T(8,128)(2,1)S(1)}, u32[]{:S(2)}, u32[]{:S(2)}) collective-permute-start(bf16[512,768]{1,0:T(8,128)(2,1)S(1)} %fusion.14), channel_id=1, source_target_pairs={{0,2},{1,3},{2,0},{3,1},{4,6},{5,7},{6,4},{7,5},{8,10},{9,11},{10,... | collective-permute-start | bytes 2359304 | tf_op jit(solution)/shard_map/ppermute | solution.py:159
  8.6 31.9 %collective-permute-start.2 = (bf16[512,768]{1,0:T(8,128)(2,1)S(1)}, bf16[512,768]{1,0:T(8,128)(2,1)}, u32[]{:S(2)}, u32[]{:S(2)}) collective-permute-start(bf16[512,768]{1,0:T(8,128)(2,1)S(1)} %fusion.14), channel_id=1, source_target_pairs={{0,1},{1,0},{2,3},{3,2},{4,5},{5,4},{6,7},{7,6},{8,9},{9,8},{10,11... | collective-permute-start | bytes 2359304 | tf_op jit(solution)/shard_map/ppermute | solution.py:159
  8.6 68.0 %collective-permute-start.15 = (f32[768]{0:T(1024)S(1)}, f32[768]{0:T(1024)S(1)}, u32[]{:S(2)}, u32[]{:S(2)}) collective-permute-start(f32[768]{0:T(1024)S(1)} %copy-done.89), channel_id=1, source_target_pairs={{0,2},{1,3},{2,0},{3,1},{4,6},{5,7},{6,4},{7,5},{8,10},{9,11},{10,... | collective-permute-start | bytes 9224 | tf_op jit(solution)/shard_map/ppermute | solution.py:159
  26.2 12.1 %collective-permute-start.1 = (bf16[512,768]{1,0:T(8,128)(2,1)S(1)}, bf16[512,768]{1,0:T(8,128)(2,1)}, u32[]{:S(2)}, u32[]{:S(2)}) collective-permute-start(bf16[512,768]{1,0:T(8,128)(2,1)S(1)} %collective-permute-done), channel_id=1, source_target_pairs={{0,1},{1,0},{2,3},{3,2},{4,5},{5,4},{6,7},{7,6},{8,9},{9,8},{10,11... | collective-permute-start | bytes 2359304 | tf_op jit(solution)/shard_map/ppermute | solution.py:159
  38.3 33.4 %collective-permute-start.6 = (bf16[192,768]{1,0:T(8,128)(2,1)S(1)}, bf16[192,768]{1,0:T(8,128)(2,1)S(1)}, u32[]{:S(2)}, u32[]{:S(2)}) collective-permute-start(bf16[192,768]{1,0:T(8,128)(2,1)S(1)} %copy-done.32), channel_id=1, source_target_pairs={{0,1},{1,0},{2,3},{3,2},{4,5},{5,4},{6,7},{7,6},{8,9},{9,8},{10,11... | collective-permute-start | bytes 884744 | tf_op jit(solution)/shard_map/ppermute | solution.py:159
  38.7 30.7 %collective-permute-start.7 = (bf16[96,768]{1,0:T(8,128)(2,1)S(1)}, bf16[96,768]{1,0:T(8,128)(2,1)S(1)}, u32[]{:S(2)}, u32[]{:S(2)}) collective-permute-start(bf16[96,768]{1,0:T(8,128)(2,1)S(1)} %slice_select_fusion.2), channel_id=1, source_target_pairs={{0,2},{1,3},{2,0},{3,1},{4,6},{5,7},{6,4},{7,5},{8,10},{9,11},{10,... | collective-permute-start | bytes 442376 | tf_op jit(solution)/shard_map/ppermute | solution.py:159
  71.1 7.8 %collective-permute-start.4 = (bf16[192,512]{1,0:T(8,128)(2,1)S(1)}, bf16[192,512]{1,0:T(8,128)(2,1)S(1)}, u32[]{:S(2)}, u32[]{:S(2)}) collective-permute-start(bf16[192,512]{1,0:T(8,128)(2,1)S(1)} %get-tuple-element.135), channel_id=1, source_target_pairs={{0,2},{1,3},{2,0},{3,1},{4,6},{5,7},{6,4},{7,5},{8,10},{9,11},{10,... | collective-permute-start | bytes 589832 | tf_op jit(solution)/shard_map/ppermute | solution.py:159
  71.7 10.5 %collective-permute-start.5 = (bf16[192,512]{1,0:T(8,128)(2,1)S(1)}, bf16[192,512]{1,0:T(8,128)(2,1)S(1)}, u32[]{:S(2)}, u32[]{:S(2)}) collective-permute-start(bf16[192,512]{1,0:T(8,128)(2,1)S(1)} %get-tuple-element.134), channel_id=1, source_target_pairs={{0,3},{1,2},{2,1},{3,0},{4,7},{5,6},{6,5},{7,4},{8,11},{9,10},{10,... | collective-permute-start | bytes 589832 | tf_op jit(solution)/shard_map/ppermute | solution.py:159
  76.6 46.5 %collective-permute-start.11 = (f32[768]{0:T(1024)S(1)}, f32[768]{0:T(1024)S(1)}, u32[]{:S(2)}, u32[]{:S(2)}) collective-permute-start(f32[768]{0:T(1024)S(1)} %copy-done.89), channel_id=1, source_target_pairs={{0,1},{1,0},{2,3},{3,2},{4,5},{5,4},{6,7},{7,6},{8,9},{9,8},{10,11... | collective-permute-start | bytes 9224 | tf_op jit(solution)/shard_map/ppermute | solution.py:159
  76.9 54.6 %collective-permute-start.19 = (f32[768]{0:T(1024)S(1)}, f32[768]{0:T(1024)S(1)}, u32[]{:S(2)}, u32[]{:S(2)}) collective-permute-start(f32[768]{0:T(1024)S(1)} %collective-permute-done.15), channel_id=1, source_target_pairs={{0,1},{1,0},{2,3},{3,2},{4,5},{5,4},{6,7},{7,6},{8,9},{9,8},{10,11... | collective-permute-start | bytes 9224 | tf_op jit(solution)/shard_map/ppermute | solution.py:159
  77.2 46.4 %collective-permute-start.10 = (bf16[768,768]{1,0:T(8,128)(2,1)S(1)}, bf16[768,768]{1,0:T(8,128)(2,1)S(1)}, u32[]{:S(2)}, u32[]{:S(2)}) collective-permute-start(bf16[768,768]{1,0:T(8,128)(2,1)S(1)} %copy-done.30), channel_id=1, source_target_pairs={{0,1},{1,0},{2,3},{3,2},{4,5},{5,4},{6,7},{7,6},{8,9},{9,8},{10,11... | collective-permute-start | bytes 3538952 | tf_op jit(solution)/shard_map/ppermute | solution.py:159
  78.8 16.9 %collective-permute-start.13 = (bf16[384,768]{1,0:T(8,128)(2,1)S(1)}, bf16[384,768]{1,0:T(8,128)(2,1)S(1)}, u32[]{:S(2)}, u32[]{:S(2)}) collective-permute-start(bf16[384,768]{1,0:T(8,128)(2,1)S(1)} %slice_select_fusion.1), channel_id=1, source_target_pairs={{0,2},{1,3},{2,0},{3,1},{4,6},{5,7},{6,4},{7,5},{8,10},{9,11},{10,... | collective-permute-start | bytes 1769480 | tf_op jit(solution)/shard_map/ppermute | solution.py:159
  82.1 25.7 %collective-permute-start.16 = (bf16[384,768]{1,0:T(8,128)(2,1)S(1)}, bf16[384,768]{1,0:T(8,128)(2,1)S(1)}, u32[]{:S(2)}, u32[]{:S(2)}) collective-permute-start(bf16[384,768]{1,0:T(8,128)(2,1)S(1)} %slice_select_fusion), channel_id=1, source_target_pairs={{0,2},{1,3},{2,0},{3,1},{4,6},{5,7},{6,4},{7,5},{8,10},{9,11},{10,... | collective-permute-start | bytes 1769480 | tf_op jit(solution)/shard_map/ppermute | solution.py:159
  95.7 14.4 %collective-permute-start.14 = (bf16[384,768]{1,0:T(8,128)(2,1)S(1)}, bf16[384,768]{1,0:T(8,128)(2,1)S(1)}, u32[]{:S(2)}, u32[]{:S(2)}) collective-permute-start(bf16[384,768]{1,0:T(8,128)(2,1)S(1)} %collective-permute-done.13), channel_id=1, source_target_pairs={{0,4},{4,0},{8,12},{12,8},{16,20},{20,16},{24,28},{28,24},{1,5},{5... | collective-permute-start | bytes 1769480 | tf_op jit(solution)/shard_map/ppermute | solution.py:159
  107.9 14.9 %collective-permute-start.17 = (bf16[384,768]{1,0:T(8,128)(2,1)S(1)}, bf16[384,768]{1,0:T(8,128)(2,1)S(1)}, u32[]{:S(2)}, u32[]{:S(2)}) collective-permute-start(bf16[384,768]{1,0:T(8,128)(2,1)S(1)} %collective-permute-done.16), channel_id=1, source_target_pairs={{0,4},{4,0},{8,12},{12,8},{16,20},{20,16},{24,28},{28,24},{1,5},{5... | collective-permute-start | bytes 1769480 | tf_op jit(solution)/shard_map/ppermute | solution.py:159
  110.1 20.3 %collective-permute-start.12 = (bf16[768,768]{1,0:T(8,128)(2,1)S(1)}, bf16[768,768]{1,0:T(8,128)(2,1)S(1)}, u32[]{:S(2)}, u32[]{:S(2)}) collective-permute-start(bf16[768,768]{1,0:T(8,128)(2,1)S(1)} %copy-done.28), channel_id=1, source_target_pairs={{0,1},{1,0},{2,3},{3,2},{4,5},{5,4},{6,7},{7,6},{8,9},{9,8},{10,11... | collective-permute-start | bytes 3538952 | tf_op jit(solution)/shard_map/ppermute | solution.py:159
  122.8 8.8 %collective-permute-start.18 = (bf16[768,768]{1,0:T(8,128)(2,1)S(1)}, bf16[768,768]{1,0:T(8,128)(2,1)S(1)}, u32[]{:S(2)}, u32[]{:S(2)}) collective-permute-start(bf16[768,768]{1,0:T(8,128)(2,1)S(1)} %pad_maximum_fusion.1), channel_id=1, source_target_pairs={{0,1},{1,0},{2,3},{3,2},{4,5},{5,4},{6,7},{7,6},{8,9},{9,8},{10,11... | collective-permute-start | bytes 3538952 | tf_op jit(solution)/shard_map/ppermute | solution.py:159
  123.0 11.3 %collective-permute-start.20 = (bf16[768,768]{1,0:T(8,128)(2,1)S(1)}, bf16[768,768]{1,0:T(8,128)(2,1)S(1)}, u32[]{:S(2)}, u32[]{:S(2)}) collective-permute-start(bf16[768,768]{1,0:T(8,128)(2,1)S(1)} %pad_maximum_fusion.2), channel_id=1, source_target_pairs={{0,1},{1,0},{2,3},{3,2},{4,5},{5,4},{6,7},{7,6},{8,9},{9,8},{10,11... | collective-permute-start | bytes 3538952 | tf_op jit(solution)/shard_map/ppermute | solution.py:159
  190.6 98.5 %collective-permute-start.45 = (bf16[192,1152]{1,0:T(8,128)(2,1)}, bf16[192,1152]{1,0:T(8,128)(2,1)}, u32[]{:S(2)}, u32[]{:S(2)}) collective-permute-start(bf16[192,1152]{1,0:T(8,128)(2,1)} %pad_maximum_fusion.7), channel_id=1, source_target_pairs={{0,1},{1,0},{2,3},{3,2},{4,5},{5,4},{6,7},{7,6},{8,9},{9,8},{10,11... | collective-permute-start | bytes 1327112 | tf_op jit(solution)/shard_map/ppermute | solution.py:159
  192.8 17.2 %collective-permute-start.79 = (f32[768]{0:T(1024)}, f32[768]{0:T(1024)}, u32[]{:S(2)}, u32[]{:S(2)}) collective-permute-start(f32[768]{0:T(1024)} %get-tuple-element.210), channel_id=1, source_target_pairs={{0,1},{1,0},{2,3},{3,2},{4,5},{5,4},{6,7},{7,6},{8,9},{9,8},{10,11... | collective-permute-start | bytes 9224 | tf_op jit(solution)/shard_map/ppermute | solution.py:159
  194.4 14.1 %collective-permute-start.59 = (f32[5,768]{1,0:T(8,128)S(1)}, f32[5,768]{1,0:T(8,128)S(1)}, u32[]{:S(2)}, u32[]{:S(2)}) collective-permute-start(f32[5,768]{1,0:T(8,128)S(1)} %stack.67), channel_id=1, source_target_pairs={{0,1},{1,0},{2,3},{3,2},{4,5},{5,4},{6,7},{7,6},{8,9},{9,8},{10,11... | collective-permute-start | bytes 46088 | tf_op jit(solution)/shard_map/ppermute | solution.py:159
  196.9 32.5 %collective-permute-start.21 = (bf16[192,512]{1,0:T(8,128)(2,1)}, bf16[192,512]{1,0:T(8,128)(2,1)}, u32[]{:S(2)}, u32[]{:S(2)}) collective-permute-start(bf16[192,512]{1,0:T(8,128)(2,1)} %get-tuple-element.132), channel_id=1, source_target_pairs={{0,1},{1,0},{2,3},{3,2},{4,5},{5,4},{6,7},{7,6},{8,9},{9,8},{10,11... | collective-permute-start | bytes 589832 | tf_op jit(solution)/shard_map/ppermute | solution.py:159
  198.9 11.2 %collective-permute-start.81 = (f32[768]{0:T(1024)S(1)}, f32[768]{0:T(1024)S(1)}, u32[]{:S(2)}, u32[]{:S(2)}) collective-permute-start(f32[768]{0:T(1024)S(1)} %add.513), channel_id=1, source_target_pairs={{0,2},{1,3},{2,0},{3,1},{4,6},{5,7},{6,4},{7,5},{8,10},{9,11},{10,... | collective-permute-start | bytes 9224 | tf_op jit(solution)/shard_map/ppermute | solution.py:159
  223.0 110.6 %collective-permute-start.44 = (bf16[192,1152]{1,0:T(8,128)(2,1)S(1)}, bf16[192,1152]{1,0:T(8,128)(2,1)}, u32[]{:S(2)}, u32[]{:S(2)}) collective-permute-start(bf16[192,1152]{1,0:T(8,128)(2,1)S(1)} %pad_maximum_fusion.6), channel_id=1, source_target_pairs={{0,1},{1,0},{2,3},{3,2},{4,5},{5,4},{6,7},{7,6},{8,9},{9,8},{10,11... | collective-permute-start | bytes 1327112 | tf_op jit(solution)/shard_map/ppermute | solution.py:159
  227.6 7.5 %collective-permute-start.23 = (bf16[192,512]{1,0:T(8,128)(2,1)}, bf16[192,512]{1,0:T(8,128)(2,1)S(1)}, u32[]{:S(2)}, u32[]{:S(2)}) collective-permute-start(bf16[192,512]{1,0:T(8,128)(2,1)} %get-tuple-element.130), channel_id=1, source_target_pairs={{0,3},{1,2},{2,1},{3,0},{4,7},{5,6},{6,5},{7,4},{8,11},{9,10},{10,... | collective-permute-start | bytes 589832 | tf_op jit(solution)/shard_map/ppermute | solution.py:159
  229.3 167.2 %collective-permute-start.86 = (bf16[768,768]{1,0:T(8,128)(2,1)}, bf16[768,768]{1,0:T(8,128)(2,1)}, u32[]{:S(2)}, u32[]{:S(2)}) collective-permute-start(bf16[768,768]{1,0:T(8,128)(2,1)} %convolution_convert_fusion.1), channel_id=1, source_target_pairs={{0,1},{1,0},{2,3},{3,2},{4,5},{5,4},{6,7},{7,6},{8,9},{9,8},{10,11... | collective-permute-start | bytes 3538952 | tf_op jit(solution)/shard_map/ppermute | solution.py:159
  278.8 8.1 %collective-permute-start.32 = (bf16[576,192]{0,1:T(8,128)(2,1)S(1)}, bf16[576,192]{0,1:T(8,128)(2,1)S(1)}, u32[]{:S(2)}, u32[]{:S(2)}) collective-permute-start(bf16[576,192]{0,1:T(8,128)(2,1)S(1)} %get-tuple-element.115), channel_id=1, source_target_pairs={{0,4},{4,0},{8,12},{12,8},{16,20},{20,16},{24,28},{28,24},{1,5},{5... | collective-permute-start | bytes 663560 | tf_op jit(solution)/shard_map/ppermute | solution.py:159
  279.8 7.9 %collective-permute-start.38 = (bf16[576,192]{0,1:T(8,128)(2,1)S(1)}, bf16[576,192]{0,1:T(8,128)(2,1)S(1)}, u32[]{:S(2)}, u32[]{:S(2)}) collective-permute-start(bf16[576,192]{0,1:T(8,128)(2,1)S(1)} %get-tuple-element.114), channel_id=1, source_target_pairs={{0,8},{4,12},{8,0},{12,4},{16,24},{20,28},{24,16},{28,20},{1,9},{5... | collective-permute-start | bytes 663560 | tf_op jit(solution)/shard_map/ppermute | solution.py:159
  286.8 179.4 %collective-permute-start.85 = (bf16[768,768]{1,0:T(8,128)(2,1)}, bf16[768,768]{1,0:T(8,128)(2,1)}, u32[]{:S(2)}, u32[]{:S(2)}) collective-permute-start(bf16[768,768]{1,0:T(8,128)(2,1)} %convolution_convert_fusion.3), channel_id=1, source_target_pairs={{0,1},{1,0},{2,3},{3,2},{4,5},{5,4},{6,7},{7,6},{8,9},{9,8},{10,11... | collective-permute-start | bytes 3538952 | tf_op jit(solution)/shard_map/ppermute | solution.py:159
  293.6 40.6 %collective-permute-start.46 = (bf16[192,1152]{1,0:T(8,128)(2,1)S(1)}, bf16[192,1152]{1,0:T(8,128)(2,1)S(1)}, u32[]{:S(2)}, u32[]{:S(2)}) collective-permute-start(bf16[192,1152]{1,0:T(8,128)(2,1)S(1)} %add_convert_fusion.4), channel_id=1, source_target_pairs={{0,2},{1,3},{2,0},{3,1},{4,6},{5,7},{6,4},{7,5},{8,10},{9,11},{10,... | collective-permute-start | bytes 1327112 | tf_op jit(solution)/shard_map/ppermute | solution.py:159
  302.1 8.3 %collective-permute-start.34 = (bf16[144,192]{0,1:T(8,128)(2,1)S(1)}, bf16[144,192]{0,1:T(8,128)(2,1)S(1)}, u32[]{:S(2)}, u32[]{:S(2)}) collective-permute-start(bf16[144,192]{0,1:T(8,128)(2,1)S(1)} %select_convert_fusion.15), channel_id=1, source_target_pairs={{0,16},{4,20},{8,24},{12,28},{16,0},{20,4},{24,8},{28,12},{1,17},{... | collective-permute-start | bytes 165896 | tf_op jit(solution)/shard_map/ppermute | solution.py:159
  333.4 66.9 %collective-permute-start.65 = (bf16[768,768]{1,0:T(8,128)(2,1)}, bf16[768,768]{1,0:T(8,128)(2,1)}, u32[]{:S(2)}, u32[]{:S(2)}) collective-permute-start(bf16[768,768]{1,0:T(8,128)(2,1)} %convolution_convert_fusion.5), channel_id=1, source_target_pairs={{0,1},{1,0},{2,3},{3,2},{4,5},{5,4},{6,7},{7,6},{8,9},{9,8},{10,11... | collective-permute-start | bytes 3538952 | tf_op jit(solution)/shard_map/ppermute | solution.py:159
  333.6 20.4 %collective-permute-start.25 = (bf16[512,768]{1,0:T(8,128)(2,1)}, bf16[512,768]{1,0:T(8,128)(2,1)}, u32[]{:S(2)}, u32[]{:S(2)}) collective-permute-start(bf16[512,768]{1,0:T(8,128)(2,1)} %bitcast_convert_fusion), channel_id=1, source_target_pairs={{0,1},{1,0},{2,3},{3,2},{4,5},{5,4},{6,7},{7,6},{8,9},{9,8},{10,11... | collective-permute-start | bytes 2359304 | tf_op jit(solution)/shard_map/ppermute | solution.py:159
  334.2 7.9 %collective-permute-start.43 = (bf16[576,192]{0,1:T(8,128)(2,1)S(1)}, bf16[576,192]{0,1:T(8,128)(2,1)S(1)}, u32[]{:S(2)}, u32[]{:S(2)}) collective-permute-start(bf16[576,192]{0,1:T(8,128)(2,1)S(1)} %pad_maximum_fusion.16), channel_id=1, source_target_pairs={{0,8},{4,12},{8,0},{12,4},{16,24},{20,28},{24,16},{28,20},{1,9},{5... | collective-permute-start | bytes 663560 | tf_op jit(solution)/shard_map/ppermute | solution.py:159
  349.3 7.7 %collective-permute-start.47 = (bf16[48,1152]{1,0:T(8,128)(2,1)}, bf16[48,1152]{1,0:T(8,128)(2,1)}, u32[]{:S(2)}, u32[]{:S(2)}) collective-permute-start(bf16[48,1152]{1,0:T(8,128)(2,1)} %get-tuple-element.127), channel_id=1, source_target_pairs={{0,4},{4,0},{8,12},{12,8},{16,20},{20,16},{24,28},{28,24},{1,5},{5... | collective-permute-start | bytes 331784 | tf_op jit(solution)/shard_map/ppermute | solution.py:159
  357.0 112.4 %collective-permute-start.64 = (bf16[768,768]{1,0:T(8,128)(2,1)}, bf16[768,768]{1,0:T(8,128)(2,1)S(1)}, u32[]{:S(2)}, u32[]{:S(2)}) collective-permute-start(bf16[768,768]{1,0:T(8,128)(2,1)} %convolution_convert_fusion.7), channel_id=1, source_target_pairs={{0,1},{1,0},{2,3},{3,2},{4,5},{5,4},{6,7},{7,6},{8,9},{9,8},{10,11... | collective-permute-start | bytes 3538952 | tf_op jit(solution)/shard_map/ppermute | solution.py:159
  396.5 14.7 %collective-permute-start.24 = (bf16[512,768]{1,0:T(8,128)(2,1)S(1)}, bf16[512,768]{1,0:T(8,128)(2,1)S(1)}, u32[]{:S(2)}, u32[]{:S(2)}) collective-permute-start(bf16[512,768]{1,0:T(8,128)(2,1)S(1)} %copy-done.81), channel_id=1, source_target_pairs={{0,1},{1,0},{2,3},{3,2},{4,5},{5,4},{6,7},{7,6},{8,9},{9,8},{10,11... | collective-permute-start | bytes 2359304 | tf_op jit(solution)/shard_map/ppermute | solution.py:159
  396.6 20.4 %collective-permute-start.26 = (bf16[512,768]{1,0:T(8,128)(2,1)S(1)}, bf16[512,768]{1,0:T(8,128)(2,1)S(1)}, u32[]{:S(2)}, u32[]{:S(2)}) collective-permute-start(bf16[512,768]{1,0:T(8,128)(2,1)S(1)} %fusion.50), channel_id=1, source_target_pairs={{0,2},{1,3},{2,0},{3,1},{4,6},{5,7},{6,4},{7,5},{8,10},{9,11},{10,... | collective-permute-start | bytes 2359304 | tf_op jit(solution)/shard_map/ppermute | solution.py:159
  411.2 16.0 %collective-permute-start.100 = (bf16[192,384]{1,0:T(8,128)(2,1)}, bf16[192,384]{1,0:T(8,128)(2,1)}, u32[]{:S(2)}, u32[]{:S(2)}) collective-permute-start(bf16[192,384]{1,0:T(8,128)(2,1)} %pad_maximum_fusion.17), channel_id=1, source_target_pairs={{0,1},{1,0},{2,3},{3,2},{4,5},{5,4},{6,7},{7,6},{8,9},{9,8},{10,11... | collective-permute-start | bytes 442376 | tf_op jit(solution)/shard_map/ppermute | solution.py:159
  411.2 8.7 %collective-permute-start.101 = (bf16[192,384]{1,0:T(8,128)(2,1)}, bf16[192,384]{1,0:T(8,128)(2,1)}, u32[]{:S(2)}, u32[]{:S(2)}) collective-permute-start(bf16[192,384]{1,0:T(8,128)(2,1)} %pad_maximum_fusion.17), channel_id=1, source_target_pairs={{0,2},{1,3},{2,0},{3,1},{4,6},{5,7},{6,4},{7,5},{8,10},{9,11},{10,... | collective-permute-start | bytes 442376 | tf_op jit(solution)/shard_map/ppermute | solution.py:159
  419.8 18.8 %collective-permute-start.102 = (bf16[192,384]{1,0:T(8,128)(2,1)}, bf16[192,384]{1,0:T(8,128)(2,1)}, u32[]{:S(2)}, u32[]{:S(2)}) collective-permute-start(bf16[192,384]{1,0:T(8,128)(2,1)} %collective-permute-done.101), channel_id=1, source_target_pairs={{0,1},{1,0},{2,3},{3,2},{4,5},{5,4},{6,7},{7,6},{8,9},{9,8},{10,11... | collective-permute-start | bytes 442376 | tf_op jit(solution)/shard_map/ppermute | solution.py:159
  420.8 25.5 %collective-permute-start.28 = (f32[2,768]{1,0:T(2,128)S(1)}, f32[2,768]{1,0:T(2,128)S(1)}, u32[]{:S(2)}, u32[]{:S(2)}) collective-permute-start(f32[2,768]{1,0:T(2,128)S(1)} %fusion.74), channel_id=1, source_target_pairs={{0,2},{1,3},{2,0},{3,1},{4,6},{5,7},{6,4},{7,5},{8,10},{9,11},{10,... | collective-permute-start | bytes 18440 | tf_op jit(solution)/shard_map/ppermute | solution.py:159
  427.2 39.0 %collective-permute-start.87 = (bf16[768,768]{1,0:T(8,128)(2,1)}, bf16[768,768]{1,0:T(8,128)(2,1)}, u32[]{:S(2)}, u32[]{:S(2)}) collective-permute-start(bf16[768,768]{1,0:T(8,128)(2,1)} %add_convert_fusion), channel_id=1, source_target_pairs={{0,2},{1,3},{2,0},{3,1},{4,6},{5,7},{6,4},{7,5},{8,10},{9,11},{10,... | collective-permute-start | bytes 3538952 | tf_op jit(solution)/shard_map/ppermute | solution.py:159
  438.7 42.5 %collective-permute-start.66 = (bf16[768,768]{1,0:T(8,128)(2,1)}, bf16[768,768]{1,0:T(8,128)(2,1)}, u32[]{:S(2)}, u32[]{:S(2)}) collective-permute-start(bf16[768,768]{1,0:T(8,128)(2,1)} %add_convert_fusion.1), channel_id=1, source_target_pairs={{0,2},{1,3},{2,0},{3,1},{4,6},{5,7},{6,4},{7,5},{8,10},{9,11},{10,... | collective-permute-start | bytes 3538952 | tf_op jit(solution)/shard_map/ppermute | solution.py:159
  457.0 7.9 %collective-permute-start.31 = (f32[42,768]{1,0:T(8,128)S(1)}, f32[42,768]{1,0:T(8,128)S(1)}, u32[]{:S(2)}, u32[]{:S(2)}) collective-permute-start(f32[42,768]{1,0:T(8,128)S(1)} %add.477), channel_id=1, source_target_pairs={{0,16},{4,20},{8,24},{12,28},{16,0},{20,4},{24,8},{28,12},{1,17},{... | collective-permute-start | bytes 387080 | tf_op jit(solution)/shard_map/ppermute | solution.py:159
  468.5 15.7 %collective-permute-start.88 = (bf16[192,768]{1,0:T(8,128)(2,1)S(1)}, bf16[192,768]{1,0:T(8,128)(2,1)S(1)}, u32[]{:S(2)}, u32[]{:S(2)}) collective-permute-start(bf16[192,768]{1,0:T(8,128)(2,1)S(1)} %get-tuple-element.106), channel_id=1, source_target_pairs={{0,4},{4,0},{8,12},{12,8},{16,20},{20,16},{24,28},{28,24},{1,5},{5... | collective-permute-start | bytes 884744 | tf_op jit(solution)/shard_map/ppermute | solution.py:159
  469.3 14.9 %collective-permute-start.94 = (bf16[192,768]{1,0:T(8,128)(2,1)S(1)}, bf16[192,768]{1,0:T(8,128)(2,1)S(1)}, u32[]{:S(2)}, u32[]{:S(2)}) collective-permute-start(bf16[192,768]{1,0:T(8,128)(2,1)S(1)} %get-tuple-element.107), channel_id=1, source_target_pairs={{0,8},{4,12},{8,0},{12,4},{16,24},{20,28},{24,16},{28,20},{1,9},{5... | collective-permute-start | bytes 884744 | tf_op jit(solution)/shard_map/ppermute | solution.py:159
  483.1 10.0 %collective-permute-start.67 = (bf16[192,768]{1,0:T(8,128)(2,1)S(1)}, bf16[192,768]{1,0:T(8,128)(2,1)S(1)}, u32[]{:S(2)}, u32[]{:S(2)}) collective-permute-start(bf16[192,768]{1,0:T(8,128)(2,1)S(1)} %get-tuple-element.110), channel_id=1, source_target_pairs={{0,4},{4,0},{8,12},{12,8},{16,20},{20,16},{24,28},{28,24},{1,5},{5... | collective-permute-start | bytes 884744 | tf_op jit(solution)/shard_map/ppermute | solution.py:159
  484.0 9.9 %collective-permute-start.73 = (bf16[192,768]{1,0:T(8,128)(2,1)S(1)}, bf16[192,768]{1,0:T(8,128)(2,1)S(1)}, u32[]{:S(2)}, u32[]{:S(2)}) collective-permute-start(bf16[192,768]{1,0:T(8,128)(2,1)S(1)} %get-tuple-element.111), channel_id=1, source_target_pairs={{0,8},{4,12},{8,0},{12,4},{16,24},{20,28},{24,16},{28,20},{1,9},{5... | collective-permute-start | bytes 884744 | tf_op jit(solution)/shard_map/ppermute | solution.py:159
  484.4 12.7 %collective-permute-start.89 = (bf16[96,768]{1,0:T(8,128)(2,1)S(1)}, bf16[96,768]{1,0:T(8,128)(2,1)S(1)}, u32[]{:S(2)}, u32[]{:S(2)}) collective-permute-start(bf16[96,768]{1,0:T(8,128)(2,1)S(1)} %select_convert_fusion.7), channel_id=1, source_target_pairs={{0,8},{4,12},{8,0},{12,4},{16,24},{20,28},{24,16},{28,20},{1,9},{5... | collective-permute-start | bytes 442376 | tf_op jit(solution)/shard_map/ppermute | solution.py:159
  486.3 12.6 %collective-permute-start.95 = (bf16[96,768]{1,0:T(8,128)(2,1)S(1)}, bf16[96,768]{1,0:T(8,128)(2,1)S(1)}, u32[]{:S(2)}, u32[]{:S(2)}) collective-permute-start(bf16[96,768]{1,0:T(8,128)(2,1)S(1)} %select_convert_fusion.6), channel_id=1, source_target_pairs={{0,4},{4,0},{8,12},{12,8},{16,20},{20,16},{24,28},{28,24},{1,5},{5... | collective-permute-start | bytes 442376 | tf_op jit(solution)/shard_map/ppermute | solution.py:159
  494.4 7.7 %collective-permute-start.74 = (bf16[96,768]{1,0:T(8,128)(2,1)S(1)}, bf16[96,768]{1,0:T(8,128)(2,1)S(1)}, u32[]{:S(2)}, u32[]{:S(2)}) collective-permute-start(bf16[96,768]{1,0:T(8,128)(2,1)S(1)} %select_convert_fusion.8), channel_id=1, source_target_pairs={{0,4},{4,0},{8,12},{12,8},{16,20},{20,16},{24,28},{28,24},{1,5},{5... | collective-permute-start | bytes 442376 | tf_op jit(solution)/shard_map/ppermute | solution.py:159
  497.2 11.8 %collective-permute-start.90 = (bf16[48,768]{1,0:T(8,128)(2,1)S(1)}, bf16[48,768]{1,0:T(8,128)(2,1)S(1)}, u32[]{:S(2)}, u32[]{:S(2)}) collective-permute-start(bf16[48,768]{1,0:T(8,128)(2,1)S(1)} %select_convert_fusion.17), channel_id=1, source_target_pairs={{0,16},{4,20},{8,24},{12,28},{16,0},{20,4},{24,8},{28,12},{1,17},{... | collective-permute-start | bytes 221192 | tf_op jit(solution)/shard_map/ppermute | solution.py:159
  499.0 11.5 %collective-permute-start.96 = (bf16[48,768]{1,0:T(8,128)(2,1)S(1)}, bf16[48,768]{1,0:T(8,128)(2,1)S(1)}, u32[]{:S(2)}, u32[]{:S(2)}) collective-permute-start(bf16[48,768]{1,0:T(8,128)(2,1)S(1)} %select_convert_fusion.16), channel_id=1, source_target_pairs={{0,16},{4,20},{8,24},{12,28},{16,0},{20,4},{24,8},{28,12},{1,17},{... | collective-permute-start | bytes 221192 | tf_op jit(solution)/shard_map/ppermute | solution.py:159
  501.0 11.1 %collective-permute-start.69 = (bf16[48,768]{1,0:T(8,128)(2,1)S(1)}, bf16[48,768]{1,0:T(8,128)(2,1)S(1)}, u32[]{:S(2)}, u32[]{:S(2)}) collective-permute-start(bf16[48,768]{1,0:T(8,128)(2,1)S(1)} %select_convert_fusion.19), channel_id=1, source_target_pairs={{0,16},{4,20},{8,24},{12,28},{16,0},{20,4},{24,8},{28,12},{1,17},{... | collective-permute-start | bytes 221192 | tf_op jit(solution)/shard_map/ppermute | solution.py:159
  502.2 14.7 %collective-permute-start.75 = (bf16[48,768]{1,0:T(8,128)(2,1)S(1)}, bf16[48,768]{1,0:T(8,128)(2,1)S(1)}, u32[]{:S(2)}, u32[]{:S(2)}) collective-permute-start(bf16[48,768]{1,0:T(8,128)(2,1)S(1)} %select_convert_fusion.18), channel_id=1, source_target_pairs={{0,16},{4,20},{8,24},{12,28},{16,0},{20,4},{24,8},{28,12},{1,17},{... | collective-permute-start | bytes 221192 | tf_op jit(solution)/shard_map/ppermute | solution.py:159
  509.0 10.2 %collective-permute-start.91 = (bf16[48,768]{1,0:T(8,128)(2,1)S(1)}, bf16[48,768]{1,0:T(8,128)(2,1)S(1)}, u32[]{:S(2)}, u32[]{:S(2)}) collective-permute-start(bf16[48,768]{1,0:T(8,128)(2,1)S(1)} %add_convert_fusion.8), channel_id=1, source_target_pairs={{0,16},{4,20},{8,24},{12,28},{16,0},{20,4},{24,8},{28,12},{1,17},{... | collective-permute-start | bytes 221192 | tf_op jit(solution)/shard_map/ppermute | solution.py:159
  510.6 11.0 %collective-permute-start.97 = (bf16[48,768]{1,0:T(8,128)(2,1)S(1)}, bf16[48,768]{1,0:T(8,128)(2,1)S(1)}, u32[]{:S(2)}, u32[]{:S(2)}) collective-permute-start(bf16[48,768]{1,0:T(8,128)(2,1)S(1)} %add_convert_fusion.7), channel_id=1, source_target_pairs={{0,16},{4,20},{8,24},{12,28},{16,0},{20,4},{24,8},{28,12},{1,17},{... | collective-permute-start | bytes 221192 | tf_op jit(solution)/shard_map/ppermute | solution.py:159
  512.1 10.2 %collective-permute-start.70 = (bf16[48,768]{1,0:T(8,128)(2,1)S(1)}, bf16[48,768]{1,0:T(8,128)(2,1)S(1)}, u32[]{:S(2)}, u32[]{:S(2)}) collective-permute-start(bf16[48,768]{1,0:T(8,128)(2,1)S(1)} %add_convert_fusion.10), channel_id=1, source_target_pairs={{0,16},{4,20},{8,24},{12,28},{16,0},{20,4},{24,8},{28,12},{1,17},{... | collective-permute-start | bytes 221192 | tf_op jit(solution)/shard_map/ppermute | solution.py:159
  523.3 8.3 %collective-permute-start.77 = (bf16[96,768]{1,0:T(8,128)(2,1)S(1)}, bf16[96,768]{1,0:T(8,128)(2,1)S(1)}, u32[]{:S(2)}, u32[]{:S(2)}) collective-permute-start(bf16[96,768]{1,0:T(8,128)(2,1)S(1)} %pad_maximum_fusion.22), channel_id=1, source_target_pairs={{0,4},{4,0},{8,12},{12,8},{16,20},{20,16},{24,28},{28,24},{1,5},{5... | collective-permute-start | bytes 442376 | tf_op jit(solution)/shard_map/ppermute | solution.py:159
  526.4 11.3 %collective-permute-start.93 = (bf16[192,768]{1,0:T(8,128)(2,1)S(1)}, bf16[192,768]{1,0:T(8,128)(2,1)S(1)}, u32[]{:S(2)}, u32[]{:S(2)}) collective-permute-start(bf16[192,768]{1,0:T(8,128)(2,1)S(1)} %pad_maximum_fusion.12), channel_id=1, source_target_pairs={{0,4},{4,0},{8,12},{12,8},{16,20},{20,16},{24,28},{28,24},{1,5},{5... | collective-permute-start | bytes 884744 | tf_op jit(solution)/shard_map/ppermute | solution.py:159
  528.5 9.3 %collective-permute-start.99 = (bf16[192,768]{1,0:T(8,128)(2,1)S(1)}, bf16[192,768]{1,0:T(8,128)(2,1)S(1)}, u32[]{:S(2)}, u32[]{:S(2)}) collective-permute-start(bf16[192,768]{1,0:T(8,128)(2,1)S(1)} %pad_maximum_fusion.13), channel_id=1, source_target_pairs={{0,8},{4,12},{8,0},{12,4},{16,24},{20,28},{24,16},{28,20},{1,9},{5... | collective-permute-start | bytes 884744 | tf_op jit(solution)/shard_map/ppermute | solution.py:159
  529.6 11.3 %collective-permute-start.72 = (bf16[192,768]{1,0:T(8,128)(2,1)S(1)}, bf16[192,768]{1,0:T(8,128)(2,1)S(1)}, u32[]{:S(2)}, u32[]{:S(2)}) collective-permute-start(bf16[192,768]{1,0:T(8,128)(2,1)S(1)} %pad_maximum_fusion.10), channel_id=1, source_target_pairs={{0,4},{4,0},{8,12},{12,8},{16,20},{20,16},{24,28},{28,24},{1,5},{5... | collective-permute-start | bytes 884744 | tf_op jit(solution)/shard_map/ppermute | solution.py:159
  531.7 9.3 %collective-permute-start.78 = (bf16[192,768]{1,0:T(8,128)(2,1)S(1)}, bf16[192,768]{1,0:T(8,128)(2,1)S(1)}, u32[]{:S(2)}, u32[]{:S(2)}) collective-permute-start(bf16[192,768]{1,0:T(8,128)(2,1)S(1)} %pad_maximum_fusion.11), channel_id=1, source_target_pairs={{0,8},{4,12},{8,0},{12,4},{16,24},{20,28},{24,16},{28,20},{1,9},{5... | collective-permute-start | bytes 884744 | tf_op jit(solution)/shard_map/ppermute | solution.py:159
  (144 other events, 1120.0 us)

commit v2 on v1

--- a/solution.py
+++ b/solution.py
@@ -8,6 +8,7 @@
 
 HD = 64
 EXPERTS = 3
+HEAD_ROWS = 80
 EPSILON = 1e-05
 F32 = jnp.float32
 BF16 = jnp.bfloat16
@@ -59,68 +60,546 @@
     )(qkv, qkv, qkv)
 
 
+def partner(index, bit):
+    return index + bit - 2 * bit * lax.rem(lax.div(index, bit), 2)
+
+
+def rows_at(ref, start, size):
+    return ref.at[pl.ds(pl.multiple_of(start, 16), size)]
+
+
+def add_rows(dst, src, lead, dst_off, src_off, size):
+    step = 48 if size % 48 == 0 else 32
+
+    def one(r, carry):
+        here = pl.ds(pl.multiple_of(dst_off + r * step, 16), step)
+        there = pl.ds(pl.multiple_of(src_off + r * step, 16), step)
+        got = src[there] if lead is None else src[lead, there]
+        dst[here] = (dst[here].astype(F32) + got.astype(F32)).astype(BF16)
+        return carry
+
+    lax.fori_loop(0, size // step, one, 0)
+
+
 def bwd_kernel(
-    q_ref, k_ref, v_ref, o_ref, do_ref, lse_ref, dq_ref, dk_ref, dv_ref, ks, vs, dks, dvs, *, scale
+    qkv_ref, o_ref, lse_ref, do_ref, rows_ref, wt_ref, tiles_ref, gain_ref, onehot_ref, small_ref,
+    *rest, scale, chunks, dp_size, heads, tp_size, width
 ):
-    i = pl.program_id(1)
-
-    @pl.when(i == 0)
+    n_src = tp_size * sum(1 for c in chunks if c["tp"] and c["part"] == 0)
+    srcs = rest[:n_src]
+    tok_ref, sum_ref, last_ref, head_ref = rest[n_src : n_src + 4]
+    n_out = n_src + 4 + len(chunks)
+    outs = rest[n_src + 4 : n_out]
+    (
+        ks, vs, dks, dvs, dos, dqkv, da_far, da_core, da_across,
+        small_in, small_got, last_own, last_got, hg,
+    ) = rest[n_out : n_out + 14]
+    per = rest[n_out + 14 : -12]
+    (
+        send_sems, recv_sems, local_sems, do_send, do_recv, do_local, da_send, da_recv,
+        vec_send, vec_recv, hg_send, hg_recv,
+    ) = rest[-12:]
+    i, h = pl.program_id(0), pl.program_id(1)
+    steps = tp_size * heads
+    step = i * heads + h
+    dpi, tpi = lax.axis_index("dp"), lax.axis_index("tp")
+    rows_dev = dos.shape[3]
+    bits = [1 << b for b in range(dp_size.bit_length() - 1)]
+
+    def remote(src, dst, ssem, rsem, axis, bit):
+        dev = (partner(dpi, bit), tpi) if axis == "dp" else (dpi, partner_any(tpi, bit))
+        return pltpu.make_async_remote_copy(
+            src_ref=src, dst_ref=dst, send_sem=ssem, recv_sem=rsem,
+            device_id=dev, device_id_type=pl.DeviceIdType.MESH,
+        )
+
+    def bit_of(bit):
+        return lax.rem(lax.div(dpi, bit), 2)
+
+    bufs, at = [], 0
+    for c in chunks:
+        n = 8 if c["tp"] else 5
+        bufs.append(per[at : at + n])
+        at += n
+
+    class Chunk:
+        def __init__(self, k):
+            self.k, self.c = k, chunks[k]
+            self.rows, self.order = self.c["rows"], self.c["order"]
+            self.acc = bufs[k][0]
+            self.halves = bufs[k][1:4]
+            if self.c["tp"]:
+                self.mid, self.got, self.got_far, self.got_x = bufs[k][4:8]
+                self.fin = self.got
+            else:
+                self.fin = bufs[k][4]
+            self.stages = []
+            if self.c["tp"]:
+                self.stages.append(("C", 0, None))
+            size, seq, far = self.rows, [], self.c["tp"]
+            for name in self.order:
+                if name == "X":
+                    far = False
+                    self.stages.append(("X", size, list(seq)))
+                else:
+                    self.stages.append(("R", name, (list(seq), size, far)))
+                    size //= 2
+                    seq.append((name, size))
+            for name in bits[3:]:
+                self.stages.append(("B", name, (list(seq), size)))
+            while seq:
+                name, half = seq[-1]
+                self.stages.append(("G", name, (list(seq), half)))
+                seq.pop()
+
+        def off(self, seq):
+            total = 0
+            for name, half in seq:
+                total = total + bit_of(name) * half
+            return total
+
+        def copies(self, s):
+            kind, name, info = self.stages[s]
+            ss, rs = send_sems.at[self.k], recv_sems.at[self.k]
+            if kind == "C":
+                lo = self.c["part"] * self.rows
+                blk = [r.at[pl.ds(lo, self.rows)] for r in self.c_src]
+                return [
+                    remote(blk[1], self.got, ss.at[0], rs.at[0], "tp", 1),
+                    remote(blk[3], self.got_far, ss.at[1], rs.at[1], "tp", 1),
+                    pltpu.make_async_copy(blk[0], self.acc, local_sems.at[self.k, 0]),
+                    pltpu.make_async_copy(blk[2], self.mid, local_sems.at[self.k, 1]),
+                ]
+            if kind == "X":
+                off = self.off(info)
+                return [
+                    remote(
+                        rows_at(self.mid, off, name), rows_at(self.got_x, off, name),
+                        ss.at[2], rs.at[2], "tp", 2,
+                    )
+                ]
+            if kind == "R":
+                seq, size, far = info
+                half = size // 2
+                off = self.off(seq) + (1 - bit_of(name)) * half
+                slot = self.slot(s)
+                out = [
+                    remote(
+                        rows_at(self.acc, off, half), self.halves[slot].at[0, pl.ds(0, half)],
+                        ss.at[3 + s], rs.at[3 + s], "dp", name,
+                    )
+                ]
+                if far:
+                    out.append(
+                        remote(
+                            rows_at(self.mid, off, half),
+                            self.halves[slot].at[1, pl.ds(0, half)],
+                            ss.at[2 + 14], rs.at[2 + 14], "dp", name,
+                        )
+                    )
+                return out
+            if kind == "B":
+                seq, size = info
+                off = self.off(seq)
+                slot = 2
+                return [
+                    remote(
+                        rows_at(self.acc, off, size),
+                        self.halves[slot].at[2 + bits.index(name) - 3, pl.ds(0, size)],
+                        ss.at[3 + s], rs.at[3 + s], "dp", name,
+                    )
+                ]
+            seq, half = info
+            off = self.off(seq)
+            here = rows_at(self.fin, off, half)
+            return [remote(here, here, ss.at[3 + s], rs.at[3 + s], "dp", name)]
+
+        def slot(self, s):
+            return sum(1 for t in self.stages[:s] if t[0] == "R")
+
+        def start(self, s):
+            for cp in self.copies(s):
+                cp.start()
+
+        def finish(self, s):
+            kind, name, info = self.stages[s]
+            for cp in self.copies(s):
+                cp.wait()
+            if kind == "C":
+                add_rows(self.acc, self.got, None, 0, 0, self.rows)
+                add_rows(self.mid, self.got_far, None, 0, 0, self.rows)
+            if kind == "X":
+                off = self.off(info)
+                add_rows(self.acc, self.got_x, None, off, off, name)
+            if kind == "R":
+                seq, size, far = info
+                half = size // 2
+                off = self.off(seq) + bit_of(name) * half
+                got = self.halves[self.slot(s)]
+                add_rows(self.acc, got, 0, off, 0, half)
+                if far:
+                    add_rows(self.mid, got, 1, off, 0, half)
+            if kind == "B":
+                seq, size = info
+                add_rows(self.acc, self.halves[2], bits.index(name) - 1, self.off(seq), 0, size)
+
+        def event(self, s):
+            if s > 0:
+                self.finish(s - 1)
+            if s < len(self.stages):
+                if self.stages[s][0] == "G" and self.stages[s - 1][0] != "G":
+                    seq, size = self.stages[s][2]
+                    here = pl.ds(pl.multiple_of(self.off(seq), 16), size)
+                    self.fin[here] = self.acc[here]
+                self.start(s)
+            else:
+                self.out_copy().start()
+
+        def out_copy(self):
+            return pltpu.make_async_copy(self.fin, outs[self.k], local_sems.at[self.k, 2])
+
+        @property
+        def n(self):
+            return len(self.stages)
+
+    work, at = [], 0
+    for k, c in enumerate(chunks):
+        ch = Chunk(k)
+        if c["tp"]:
+            if c["part"] == 0:
+                at += tp_size
+            ch.c_src = srcs[at - tp_size : at]
+        work.append(ch)
+    done = [0] * len(work)
+
+    def go(k, upto=None):
+        if done[k] <= work[k].n:
+            work[k].event(done[k])
+            done[k] += 1
+
+    def turn(ks):
+        for k in ks:
+            go(k)
+
+    ladder = [("tp", 1), ("tp", 2)] + [("dp", b) for b in bits]
+
+    def small_copy(s):
+        return remote(
+            small_in, small_got.at[s], vec_send.at[0, s], vec_recv.at[0, s], *ladder[s]
+        )
+
+    def small_event(s):
+        if s > 0:
+            small_copy(s - 1).wait()
+            got = small_got[s - 1]
+            small_in[0:8] += got[0:8]
+            if s == 1:
+                small_in[8:9] += got[9:10]
+                small_in[10:11] += got[11:12]
+            elif s == 2:
+                small_in[8:9] += got[10:11]
+            else:
+                small_in[8:9] += got[8:9]
+        if s < len(ladder):
+            small_copy(s).start()
+
+    def do_copy(p):
+        if p == 0:
+            return pltpu.make_async_copy(do_ref.at[0], dos.at[0], do_local)
+        return remote(do_ref.at[p], dos.at[p], do_send.at[p], do_recv.at[p], "tp", p)
+
+    @pl.when(step == 0)
     def _():
-        ks[...] = k_ref[0, 0].T
-        vs[...] = v_ref[0, 0].T
+        barrier = pltpu.get_barrier_semaphore()
+        others = [("tp", 1), ("tp", 2), ("tp", 3)] + [("dp", b) for b in bits]
+        for axis, bit in others:
+            dev = (partner(dpi, bit), tpi) if axis == "dp" else (dpi, partner_any(tpi, bit))
+            pl.semaphore_signal(
+                barrier, inc=1, device_id=dev, device_id_type=pl.DeviceIdType.MESH
+            )
+        pl.semaphore_wait(barrier, len(others))
+        for p in (2, 3, 1, 0):
+            do_copy(p).start()
+        for k in range(len(work)):
+            if chunks[k]["tp"]:
+                work[k].event(0)
+        small_in[...] = small_ref[...]
+        small_event(0)
+        for hh in range(heads):
+            ks[hh] = qkv_ref[1, hh].T
+            vs[hh] = qkv_ref[2, hh].T
         dks[...] = jnp.zeros_like(dks)
         dvs[...] = jnp.zeros_like(dvs)
 
-    qt = q_ref[0, 0] * jnp.bfloat16(scale)
-    dot_t = do_ref[0]
-    dsum = jnp.sum(dot_t.astype(F32) * o_ref[0].astype(F32), axis=0, keepdims=True)
-    s = dot(ks[...], qt)
-    p = jnp.exp(s - lse_ref[0])
-    dp = dot(vs[...], dot_t)
+    for p in range(tp_size):
+
+        @pl.when(step == p * heads)
+        def _():
+            do_copy(p).wait()
+
+    lanes = pl.ds(pl.multiple_of(i * rows_dev, rows_dev), rows_dev)
+    qt = qkv_ref[0, h, :, lanes] * jnp.bfloat16(scale)
+    dot_t = dos[i, h]
+    dsum = jnp.sum(
+        dot_t.astype(F32) * o_ref[h, :, lanes].astype(F32), axis=0, keepdims=True
+    )
+    s = dot(ks[h], qt)
+    p = jnp.exp(s - lse_ref[h, :, lanes])
+    dp = dot(vs[h], dot_t)
     ds = (p * (dp - dsum)).astype(BF16)
-    dq_ref[0] = (dot(k_ref[0, 0], ds) * scale).astype(BF16)
-    dvs[...] += dot(p.astype(BF16), dot_t.T)
-    dks[...] += dot(ds, qt.T)
-
-    @pl.when(i == pl.num_programs(1) - 1)
+    dqkv[0, h, :, lanes] = (dot(qkv_ref[1, h], ds) * scale).astype(BF16)
+    dvs[h] += dot(p.astype(BF16), dot_t.T)
+    dks[h] += dot(ds, qt.T)
+
+    n_tp = [k for k in range(len(work)) if chunks[k]["tp"]]
+    for k in n_tp:
+        done[k] = 1
+    small_done = [1]
+    for st in range(steps):
+
+        @pl.when(step == st)
+        def _():
+            if st < len(PLAN_STEPS):
+                turn(PLAN_STEPS[st])
+            if small_done[0] <= len(ladder):
+                small_event(small_done[0])
+                small_done[0] += 1
+
+    @pl.when(step == steps - 1)
     def _():
-        dk_ref[0] = dks[...].astype(BF16).T
-        dv_ref[0] = dvs[...].astype(BF16).T
-
-
-def attn_bwd(qkv, o, do, lse, scale, bq):
-    _, heads, _, rows = qkv.shape
-
-    def blk(j):
-        return pl.BlockSpec((1, 1, HD, bq), lambda h, i: (j, h, 0, i))
-
-    def full(j):
-        return pl.BlockSpec((1, 1, HD, rows), lambda h, i: (j, h, 0, 0))
-
+        for hh in range(heads):
+            dqkv[1, hh] = dks[hh].astype(BF16).T
+            dqkv[2, hh] = dvs[hh].astype(BF16).T
+
+        blk = 128
+
+        def da_rows(p, store):
+            def one(r, carry):
+                lane = pl.ds(pl.multiple_of(p * rows_dev + r * blk, blk), blk)
+                lhs = dqkv[:, :, :, lane].reshape(3 * heads * HD, blk)
+                here = pl.ds(pl.multiple_of(r * blk, blk), blk)
+                store(here, dot(lhs, wt_ref[...], ((0,), (0,))))
+                return carry
+
+            lax.fori_loop(0, rows_dev // blk, one, 0)
+
+        def keep(slot):
+            def store(here, val):
+                da_far[slot, here] = val.astype(BF16)
+
+            return store
+
+        core3 = remote(da_far.at[0], da_core.at[0], da_send.at[0], da_recv.at[0], "tp", 1)
+        core1 = remote(da_far.at[1], da_core.at[1], da_send.at[1], da_recv.at[1], "tp", 1)
+        far = remote(da_far.at[2], da_across, da_send.at[2], da_recv.at[2], "tp", 2)
+        da_rows(3, keep(0))
+        core3.start()
+        turn(PLAN_TAIL[0])
+        da_rows(1, keep(1))
+        core1.start()
+        turn(PLAN_TAIL[1])
+        core3.wait()
+
+        def store2(here, val):
+            da_far[2, here] = (val + da_core[0, here].astype(F32)).astype(BF16)
+
+        da_rows(2, store2)
+        far.start()
+        turn(PLAN_TAIL[2])
+        kq = [k for k in range(len(work)) if not chunks[k]["tp"]]
+        nh = heads * HD
+        spots = [(k, r) for k in kq for r in range(0, chunks[k]["rows"], nh)]
+        for sec in range(3):
+            k, r = spots[sec]
+            lhs = dqkv[sec].reshape(nh, tp_size * rows_dev)
+            work[k].acc[r : r + nh] = dot(lhs, rows_ref[...]).astype(BF16)
+        k, r = spots[2]
+        rest_rows = chunks[k]["rows"] - r - nh
+        work[k].acc[r + nh :] = jnp.zeros((rest_rows, width), BF16)
+        turn(kq)
+        turn(PLAN_TAIL[3])
+        core1.wait()
+
+        def store0(here, val):
+            tok_ref[here] = val + da_core[1, here].astype(F32)
+
+        da_rows(0, store0)
+        turn(PLAN_TAIL[4])
+        turn(PLAN_WAIT)
+        far.wait()
+        last_own[...] = jnp.zeros_like(last_own)
+
+        def norm_rows(r, carry):
+            here = pl.ds(pl.multiple_of(r * blk, blk), blk)
+            da = tok_ref[here] + da_across[here].astype(F32)
+            hat, rstd = norm_parts(tiles_ref[here].astype(F32))
+            tok_ref[here] = norm_back(hat, rstd, gain_ref[...], da)
+            last_own[0:1] += jnp.sum(da * hat, axis=0, keepdims=True)
+            last_own[1:2] += jnp.sum(da, axis=0, keepdims=True)
+            return carry
+
+        lax.fori_loop(0, rows_dev // blk, norm_rows, 0)
+
+        def last_copy(s):
+            if s < 2:
+                return remote(
+                    last_own.at[pl.ds(0, 8)], last_got.at[s, pl.ds(0, 8)],
+                    vec_send.at[1, s], vec_recv.at[1, s], *ladder[s],
+                )
+            return remote(
+                last_own, last_got.at[s], vec_send.at[1, s], vec_recv.at[1, s], *ladder[s]
+            )
+
+        last_copy(0).start()
+        for st in range(len(ladder)):
+            if st < len(PLAN_LAST):
+                turn(PLAN_LAST[st])
+            last_copy(st).wait()
+            if st < 2:
+                last_own[0:8] += last_got[st, 0:8]
+                if st == 1:
+                    last_own[8:] = onehot_ref[...] * last_own[1:2]
+            else:
+                last_own[...] += last_got[st]
+            if st + 1 < len(ladder):
+                last_copy(st + 1).start()
+        while small_done[0] <= len(ladder):
+            small_event(small_done[0])
+            small_done[0] += 1
+        turn(PLAN_LAST[-1])
+        turn(PLAN_END)
+        while any(done[k] <= work[k].n for k in range(len(work))):
+            turn(range(len(work)))
+        last_ref[...] = last_own[...]
+        sum_ref[...] = small_in[...]
+        kp = [k for k in n_tp if chunks[k].get("head")][0]
+        nh, hr = chunks[kp]["head"]
+        mine = work[kp].fin.at[pl.ds(nh, hr)]
+        cps = [
+            remote(mine, hg.at[p - 1], hg_send.at[p - 1], hg_recv.at[p - 1], "tp", p)
+            for p in range(1, tp_size)
+        ]
+        for cp in cps:
+            cp.start()
+        head_out = [
+            pltpu.make_async_copy(
+                mine, rows_at(head_ref, tpi * hr, hr), do_local
+            )
+        ]
+        head_out[0].start()
+        for p, cp in enumerate(cps):
+            cp.wait()
+            out = pltpu.make_async_copy(
+                hg.at[p], rows_at(head_ref, partner_any(tpi, p + 1) * hr, hr),
+                local_sems.at[p, 3],
+            )
+            out.start()
+            head_out.append(out)
+        for out in head_out:
+            out.wait()
+        for ch in work:
+            ch.out_copy().wait()
+
+
+def partner_any(index, mask):
+    if mask & 1:
+        index = partner(index, 1)
+    if mask & 2:
+        index = partner(index, 2)
+    return index
+
+
+PLAN_STEPS = ((0, 1, 2), (3,), (4,), (), (0, 1, 2), (), (), (1,), (3, 4), (1,), (0,), (1, 2, 4))
+PLAN_TAIL = ((0,), (), (1, 2, 3, 4), (0,), (1, 3))
+PLAN_WAIT = (2, 6, 4, 5, 1)
+PLAN_LAST = ((0,), (3, 5), (2, 6), (0, 4), (2, 3, 5), (0, 4, 6))
+PLAN_END = (3, 2, 5, 4, 6, 5, 3, 6, 5, 6)
+
+
+def attn_bwd(qkv, o, lse, do, rows, wt, tiles, gain, onehot, small, parts, mesh, scale):
+    _, heads, _, frame = qkv.shape
+    rows_dev, width = tiles.shape
+    tp_size, dp_size = mesh.shape["tp"], mesh.shape["dp"]
+    nbits = dp_size.bit_length() - 1
+    half = width // 2
+    ph_rows = parts[2][0].shape[0]
+    chunks = [
+        dict(tp=True, rows=half, part=0, order=[1, "X", 2, 4]),
+        dict(tp=True, rows=half, part=1, order=["X", 1, 2, 4]),
+        dict(tp=True, rows=half, part=0, order=[2, "X", 1, 4]),
+        dict(tp=True, rows=half, part=1, order=[2, "X", 1, 4]),
+        dict(tp=True, rows=ph_rows, part=0, order=["X", 1, 2, 4], head=(heads * HD, HEAD_ROWS)),
+        dict(tp=False, rows=half, order=[2, 1, 4]),
+        dict(tp=False, rows=256, order=[1, 2, 4]),
+    ]
+    n_k = len(chunks)
+    scratch = [
+        pltpu.VMEM((heads, frame, HD), BF16),
+        pltpu.VMEM((heads, frame, HD), BF16),
+        pltpu.VMEM((heads, frame, HD), F32),
+        pltpu.VMEM((heads, frame, HD), F32),
+        pltpu.VMEM((tp_size, heads, HD, rows_dev), BF16),
+        pltpu.VMEM((3, heads, HD, frame), BF16),
+        pltpu.VMEM((3, rows_dev, width), BF16),
+        pltpu.VMEM((2, rows_dev, width), BF16),
+        pltpu.VMEM((rows_dev, width), BF16),
+        pltpu.VMEM((16, width), F32),
+        pltpu.VMEM((2 + nbits, 16, width), F32),
+        pltpu.VMEM((8 + onehot.shape[0], width), F32),
+        pltpu.VMEM((2 + nbits, 8 + onehot.shape[0], width), F32),
+        pltpu.VMEM((tp_size - 1, HEAD_ROWS, width), BF16),
+    ]
+    for c in chunks:
+        r = c["rows"]
+        scratch.append(pltpu.VMEM((r, width), BF16))
+        scratch.append(pltpu.VMEM((2, r // 2, width), BF16))
+        scratch.append(pltpu.VMEM((2, r // 4, width), BF16))
+        scratch.append(pltpu.VMEM((2 + max(nbits - 3, 0), r // 8, width), BF16))
+        if c["tp"]:
+            scratch += [pltpu.VMEM((r, width), BF16)] * 4
+        else:
+            scratch.append(pltpu.VMEM((r, width), BF16))
+    scratch += [
+        pltpu.SemaphoreType.DMA((n_k, 17)),
+        pltpu.SemaphoreType.DMA((n_k, 17)),
+        pltpu.SemaphoreType.DMA((n_k, 4)),
+        pltpu.SemaphoreType.DMA((tp_size,)),
+        pltpu.SemaphoreType.DMA((tp_size,)),
+        pltpu.SemaphoreType.DMA,
+        pltpu.SemaphoreType.DMA((3,)),
+        pltpu.SemaphoreType.DMA((3,)),
+        pltpu.SemaphoreType.DMA((2, 2 + nbits)),
+        pltpu.SemaphoreType.DMA((2, 2 + nbits)),
+        pltpu.SemaphoreType.DMA((tp_size - 1,)),
+        pltpu.SemaphoreType.DMA((tp_size - 1,)),
+    ]
+    any_spec = pl.BlockSpec(memory_space=pl.ANY)
+    vmem = pl.BlockSpec(memory_space=pltpu.VMEM)
+    flat = [x for group in parts for x in group]
     return pl.pallas_call(
-        functools.partial(bwd_kernel, scale=scale),
-        grid=(heads, rows // bq),
-        in_specs=[
-            blk(0),
-            full(1),
-            full(2),
-            pl.BlockSpec((1, HD, bq), lambda h, i: (h, 0, i)),
-            pl.BlockSpec((1, HD, bq), lambda h, i: (h, 0, i)),
-            pl.BlockSpec((1, 1, bq), lambda h, i: (h, 0, i)),
-        ],
-        out_specs=[
-            pl.BlockSpec((1, HD, bq), lambda h, i: (h, 0, i)),
-            pl.BlockSpec((1, HD, rows), lambda h, i: (h, 0, 0)),
-            pl.BlockSpec((1, HD, rows), lambda h, i: (h, 0, 0)),
-        ],
-        out_shape=[jax.ShapeDtypeStruct((heads, HD, rows), BF16)] * 3,
-        scratch_shapes=[pltpu.VMEM((rows, HD), BF16)] * 2 + [pltpu.VMEM((rows, HD), F32)] * 2,
-        compiler_params=pltpu.CompilerParams(vmem_limit_bytes=50 << 20),
+        functools.partial(
+            bwd_kernel, scale=scale, chunks=chunks, dp_size=dp_size, heads=heads,
+            tp_size=tp_size, width=width,
+        ),
+        grid=(tp_size, heads),
+        in_specs=[vmem, vmem, vmem, any_spec] + [vmem] * 6 + [any_spec] * len(flat),
+        out_specs=[vmem, vmem, vmem, any_spec] + [any_spec] * n_k,
+        out_shape=[
+            jax.ShapeDtypeStruct((rows_dev, width), F32),
+            jax.ShapeDtypeStruct((16, width), F32),
+            jax.ShapeDtypeStruct((8 + onehot.shape[0], width), F32),
+            jax.ShapeDtypeStruct((tp_size * HEAD_ROWS, width), BF16),
+        ]
+        + [jax.ShapeDtypeStruct((c["rows"], width), BF16) for c in chunks],
+        scratch_shapes=scratch,
+        compiler_params=pltpu.CompilerParams(
+            vmem_limit_bytes=60 << 20, collective_id=1, has_side_effects=True
+        ),
         cost_estimate=pl.CostEstimate(
-            flops=46_000_000_000, bytes_accessed=8 << 20, transcendentals=heads * rows * rows
+            flops=60_000_000_000, bytes_accessed=30 << 20, transcendentals=heads * frame * frame
         ),
         name="attn_bwd",
-    )(qkv, qkv, qkv, o, do, lse)
+    )(qkv, o, lse, do, rows, wt, tiles, gain, onehot, small, *flat)
 
 
 def norm_parts(values):
@@ -152,7 +631,6 @@
 
 def make_body(mesh):
     dp_size, tp_size = mesh.shape["dp"], mesh.shape["tp"]
-    dp_bits = [1 << b for b in range(dp_size.bit_length() - 1)]
 
     def swap(x, axis, bit):
         size = dp_size if axis == "dp" else tp_size
@@ -169,46 +647,6 @@
 
     def my_bit(bit):
         return (lax.axis_index("dp") & bit) != 0
-
-    def fold_tp(parts, cast=BF16):
-        got1 = core(parts[3].astype(cast))
-        got0 = core(parts[1].astype(cast))
-        mid = parts[2].astype(F32) + got1.astype(F32)
-        own = parts[0].astype(F32) + got0.astype(F32)
-        return own + across(mid.astype(cast)).astype(F32)
-
-    def dp_sum(x, bits):
-        for bit in bits:
-            n = x.shape[0] // 2
-            lo, hi = x[:n], x[n:]
-            mine = my_bit(bit)
-            send = jnp.where(mine, lo, hi).astype(BF16)
-            keep = jnp.where(mine, hi, lo).astype(F32)
-            x = keep + swap(send, "dp", bit).astype(F32)
-        x = x.astype(BF16)
-        for bit in reversed(bits):
-            got = swap(x, "dp", bit)
-            mine = my_bit(bit)
-            x = jnp.concatenate([jnp.where(mine, got, x), jnp.where(mine, x, got)], axis=0)
-        return x
-
-    def dp_sum_halves(x):
-        n = x.shape[0] // 2
-        order = list(dp_bits)
-        if n % dp_size:
-            return dp_sum(x, order).astype(F32)
-        other = [order[1], order[0]] + order[2:]
-        return jnp.concatenate([dp_sum(x[:n], order), dp_sum(x[n:], other)], axis=0).astype(F32)
-
-    def butterfly_dp(x):
-        for bit in dp_bits:
-            x = x + swap(x, "dp", bit)
-        return x
-
-    def butterfly_all(x):
-        x = x + core(x)
-        x = x + across(x)
-        return butterfly_dp(x)
 
     def gather_tp(x):
         n = x.shape[0] // 2
@@ -329,43 +767,32 @@
         dy = dx1.astype(BF16)
         do_all = dot(proj_cat, dy, ((1,), (1,))).astype(BF16)
         nh = heads * HD
-        db = [do_all[p * nh : (p + 1) * nh] for p in range(tp_size)]
-        do = jnp.concatenate([db[0], core(db[1]), across(db[2]), diag(db[3])], axis=1)
-        do = do.reshape(heads, HD, rows_frame)
-        dqt, dkt, dvt = attn_bwd(qkv, o_heads, do, lse, scale_val, min(512, rows_frame))
-
+        do_all = do_all.reshape(tp_size, heads, HD, rows_dev)
         blended = (corr)[:, None, :]
         for e in range(EXPERTS):
             blended = blended + gates[e][:, None, :] * specialist_outlooks[e].astype(F32)
 
         d_proj = dot(o_own, dy, ((1,), (0,))).astype(BF16)
-        d_head = dot(h_low, head_grads, ((0,), (1,))).astype(BF16)
-        d_head = jnp.pad(d_head, ((0, 0), (0, (-d_head.shape[1]) % 128)))
+        d_head = dot(head_grads, h_low).astype(BF16)
+        d_head = jnp.pad(d_head, ((0, tp_size * HEAD_ROWS - d_head.shape[0]), (0, 0)))
         dproj_parts = []
+        ph_rows = -(-(nh + HEAD_ROWS) // 128) * 128
         for p in range(tp_size):
-            head_blk = lax.dynamic_slice_in_dim(d_head, (tp_index ^ p) * nh, nh, 0)
+            head_blk = lax.dynamic_slice_in_dim(d_head, (tp_index ^ p) * HEAD_ROWS, HEAD_ROWS, 0)
             dproj_parts.append(
-                jnp.concatenate([d_proj[p * nh : (p + 1) * nh], head_blk], axis=1)
+                jnp.concatenate(
+                    [
+                        d_proj[p * nh : (p + 1) * nh],
+                        head_blk,
+                        jnp.zeros((ph_rows - nh - HEAD_ROWS, width), BF16),
+                    ],
+                    axis=0,
+                )
             )
-
-        narrow_sum = dp_sum_halves(fold_tp(d_narrow))
-        wide_sum = dp_sum_halves(fold_tp(d_wide))
-        proj_sum = dp_sum_halves(fold_tp(dproj_parts))
-        proj_weight_grad = proj_sum[:, :width]
-        head_own = proj_sum[:, width:].astype(BF16)
-        h2 = across(head_own)
-        head_parts = [head_own, core(head_own), h2, core(h2)]
-        head_sum = jnp.zeros((width, head_own.shape[1]), BF16)
-        for p in range(tp_size):
-            head_sum = lax.dynamic_update_slice_in_dim(
-                head_sum, head_parts[p], (tp_index ^ p) * nh, 0
-            )
-        head_sum = head_sum.astype(F32)
-        gate_weight_grad = head_sum[:, : EXPERTS * fields]
-        correct_weight_grad = head_sum[:, EXPERTS * fields : (EXPERTS + 1) * fields]
 
         head_bias = jnp.sum(head_grads.astype(F32), axis=1)
         head_bias = jnp.pad(head_bias, (0, width - head_bias.shape[0]))
+        zero = jnp.zeros((width,), F32)
         small = jnp.stack(
             [
                 jnp.sum(dx2, axis=0),
@@ -373,41 +800,38 @@
                 jnp.sum(dc, axis=0),
                 jnp.sum(dx1, axis=0),
                 head_bias,
+                zero,
+                zero,
+                zero,
             ]
+            + [jnp.sum(dus[p].astype(F32), axis=0) for p in range(tp_size)]
+            + [zero] * 4
         )
-        small = butterfly_all(small)
-        in_parts = [jnp.sum(dus[p].astype(F32), axis=0) for p in range(tp_size)]
-        in_bias_grad = butterfly_dp(fold_tp(in_parts, F32))
-
-        dqkv = jnp.stack([dqt, dkt, dvt]).reshape(3, nh, rows_frame)
-        d_qkv = jnp.einsum("td,sht->sdh", attn_rows, dqkv, preferred_element_type=F32)
-        qkv_sum = dp_sum_halves(d_qkv.reshape(3 * width, nh)).reshape(3, width, nh)
-        da_parts = [
-            jnp.einsum(
-                "sht,sdh->td",
-                dqkv[:, :, p * rows_dev : (p + 1) * rows_dev],
-                triple_w,
-                preferred_element_type=F32,
-            )
-            for p in range(tp_size)
-        ]
-        da = fold_tp(da_parts)
-        tokens_grad = dx1 + norm_back(hat1, rstd1, early_layernorm_scale, da)
-        da_sum = jnp.sum(da, axis=0)
-        last = jnp.stack([jnp.sum(da * hat1, axis=0), da_sum])
-        last = last + core(last)
-        last = last + across(last)
         leads = horizon_vectors.shape[0]
-        onehot = (jnp.arange(leads, dtype=jnp.int32) == lead).astype(F32)
-        table = jnp.concatenate([last, onehot[:, None] * last[1][None, :]], axis=0)
-        table = butterfly_dp(table)
+        onehot = (jnp.arange(leads, dtype=jnp.int32) == lead).astype(F32)[:, None]
+        w_t = jnp.transpose(triple_head_matrix, (0, 2, 1)).reshape(3 * nh, width)
+        (token_part, small, table, head_sum, n0, n1, i0, i1, ph, q0, q1) = attn_bwd(
+            qkv, o_heads, lse, do_all, attn_rows, w_t, tile_vectors,
+            early_layernorm_scale[None, :], onehot, small,
+            [d_narrow, d_wide, dproj_parts], mesh, scale_val,
+        )
+        tokens_grad = dx1 + token_part
+        narrow_sum = jnp.concatenate([n0, n1], axis=0).astype(F32)
+        wide_sum = jnp.concatenate([i0, i1], axis=0).astype(F32)
+        proj_weight_grad = ph[:nh].astype(F32)
+        head_sum = head_sum.T.astype(F32)
+        gate_weight_grad = head_sum[:, : EXPERTS * fields]
+        correct_weight_grad = head_sum[:, EXPERTS * fields : (EXPERTS + 1) * fields]
+        q_all = jnp.concatenate([q0, q1], axis=0)[: 3 * nh]
+        qkv_sum = jnp.transpose(q_all.reshape(3, nh, width), (0, 2, 1)).astype(F32)
+        in_bias_grad = small[8]
 
         return (
             blended,
             tokens_grad,
             table[0],
             table[1],
-            table[2:],
+            table[8:],
             qkv_sum,
             proj_weight_grad,
             small[3],

time: 550 us -> 370 us (0.67)
  waiting for transfers between devices: 218 us -> 56.4 us
  Pallas kernels: 62.1 us -> 171 us
  starting transfers between devices: 73.4 us -> 12.4 us
  local copies, waits for them, and re-layouts: 59 us -> 25.7 us
  matrix products: 68 us -> 50.7 us
  other arithmetic: 57.7 us -> 43.4 us
    ppermute x103 -> x21, waiting for transfers between devices: 218 us -> 56.4 us  [swap(): return lax.ppermute(x, axis, [(i, i ^ bit) for i in range(size)])]
    pallas_call x1, Pallas kernels: 36.8 us -> 146 us  [attn_bwd(): pl.pallas_call(functools.partial(bwd_kernel, scale=scale, chunks=chunks,...]
    ppermute x103 -> x21, starting transfers between devices: 73.4 us -> 12.4 us  [swap(): return lax.ppermute(x, axis, [(i, i ^ bit) for i in range(size)])]
    dynamic_update_slice x4 -> x0, local copies, waits for them, and re-layouts: 13.4 us -> none  [body(): lax.dynamic_update_slice_in_dim(head_sum, head_parts[p], (tp_index ^ p) *...]
    dot_general x5 -> x0, matrix products: 12 us -> none  [the longest x4 7.83 us: body(): jnp.einsum('sht,sdh->td', dqkv[:, :, p * rows_dev:(p + 1) * rows_dev], tr...]
    add x31 -> x1, other arithmetic: 12.6 us -> 1.33 us  [body(): tokens_grad = dx1 + token_part]
    dot_general x31, matrix products: 52.6 us -> 47 us  [dot(): return lax.dot_general(a, b, (dims, ((), ())), preferred_element_type=F32)]
  transfers between devices with their start and end apart: 103 -> 21, of which waited for: 60 -> 9; matrix products, arithmetic and copies ran while one was open for 22% -> 9% of each run, Pallas kernels for 11% -> 7%
where the time goes in v2:
time: 370 us; the launch traced here: 363 us
  Pallas kernels  171 us (46%)
  waiting for transfers between devices  56.4 us (15%)
  matrix products  50.7 us (14%)
  other arithmetic  43.4 us (12%)
  local copies, waits for them, and re-layouts  25.7 us (7%)
  starting transfers between devices  12.4 us (3%)
    pallas_call x1, Pallas kernels, attn_bwd(): pl.pallas_call(functools.partial(bwd_kernel, scale=scale, chunks=chunks,...  146 us
    ppermute x21, waiting for transfers between devices, swap(): return lax.ppermute(x, axis, [(i, i ^ bit) for i in range(size)])  56.4 us
    dot_general x31, matrix products, dot(): return lax.dot_general(a, b, (dims, ((), ())), preferred_element_type=F32)  47 us
    pallas_call x1, Pallas kernels, attn_fwd(): pl.pallas_call(functools.partial(fwd_kernel, scale=scale), grid=(heads, r...  25 us
    ppermute x21, starting transfers between devices, swap(): return lax.ppermute(x, axis, [(i, i ^ bit) for i in range(size)])  12.4 us
    reduce_sum x1, other arithmetic, body(): jnp.sum(specialist_outlooks[e].astype(F32) * slope, axis=1)  9.98 us
    add x1, other arithmetic, body(): blended + gates[e][:, None, :] * specialist_outlooks[e].astype(F32)  9.05 us
  transfers between devices with their start and end apart: 21, of which 9 were waited for; matrix products, arithmetic and copies ran while one was open for 9% of the time, Pallas kernels for 7%

profile of v2, /device:TPU:0, one launch (start us, length us, event | category | flops | bytes accessed | tf_op | source)
XLA Modules:
  0.0 363.2 jit_solution(12694302831317384356)
XLA Ops:
  1.4 1.3 convert_reduce_fusion.1
  2.8 1.5 fusion.13
  4.8 3.0 collective-permute-start
  8.0 17.4 %collective-permute-done = bf16[512,768]{1,0:T(8,128)(2,1)S(1)} collective-permute-done((bf16[512,768]{1,0:T(8,128)(2,1)S(1)}, bf16[512,768]{1,0:T(8,128)(2,1)S(1)}, u32[]{:S(2)}, u32[]{:S(2)}) %collective-permute-start) | collective-permute-done | bytes 786464 | tf_op jit(solution)/shard_map/ppermute | solution.py:637
  25.4 10.0 %fusion.3 = (f32[69,512]{1,0:T(8,128)}, f32[69,512]{1,0:T(8,128)}, f32[69,512]{1,0:T(8,128)}, f32[69,512]{1,0:T(8,128)S(1)}) fusion(bf16[69,64,512]{2,1,0:T(8,128)(2,1)} %param.41, bf16[3,69,64,512]{3,2,1,0:T(8,128)(2,1)} %param.24), kind=kLoop, calls=%fused_computation.10 | loop fusion | flops 24729600 | bytes 18653184 | tf_op jit(solution)/shard_map/reduce_sum | solution.py:721
  38.6 1.8 collective-permute-start.7
  40.4 3.7 %fusion.8 = bf16[3,192,2048]{2,1,0:T(8,128)(2,1)S(1)} fusion(bf16[3,768,192]{1,2,0:T(8,128)(2,1)} %param.28, bf16[512,768]{1,0:T(8,128)(2,1)} %collective-permute-done.1, bf16[512,768]{1,0:T(8,128)(2,1)S(1)} %collective-permute-done, bf16[512,768]{1,0:T(8,128)(2,1)} %collective-permute-done.2, bf16[512,768]{1,0:T(8,128)(2,1)S(1)} %fusion.17), kind=kOutput, calls=%fused_computation.16 | convolution fusion | flops 1825701888 | bytes 6389760 | tf_op jit(solution)/shard_map/sdh,td->sht/dot_general | solution.py:712
  44.1 25.0 %attn_fwd.1 = (bf16[3,64,2048]{2,1,0:T(8,128)(2,1)S(1)}, f32[3,1,2048]{2,1,0:T(1,128)S(1)}) custom-call(bf16[3,3,64,2048]{3,2,1,0:T(8,128)(2,1)S(1)} %bitcast.104, bf16[3,3,64,2048]{3,2,1,0:T(8,128)(2,1)S(1)} %bitcast.105, bf16[3,3,64,2048]{3,2,1,0:T(8,128)(2,1)S(1)} %bitcast.106), custom_call_target="tpu_custom_call" | custom-call | flops 24000000000 | bytes 4194304 | tf_op jit(solution)/shard_map/attn_fwd/pallas_call | solution.py:38
  69.2 3.6 pad_maximum_fusion.rows_ref
  72.8 1.6 collective-permute-start.8
  75.1 0.9 collective-permute-start.5
  75.9 3.0 collective-permute-done.8
  79.3 1.0 copy-done.23
  81.4 0.9 collective-permute-done.4
  82.8 1.8 collective-permute-done.5
  84.6 1.4 collective-permute-start.16
  86.1 0.9 fusion.71
  88.1 11.1 %collective-permute-done.13 = bf16[384,768]{1,0:T(8,128)(2,1)S(1)} collective-permute-done((bf16[384,768]{1,0:T(8,128)(2,1)S(1)}, bf16[384,768]{1,0:T(8,128)(2,1)S(1)}, u32[]{:S(2)}, u32[]{:S(2)}) %collective-permute-start.13) | collective-permute-done | bytes 589856 | tf_op jit(solution)/shard_map/ppermute | solution.py:637
  99.1 2.9 multiply_convert_fusion.3
  102.0 8.9 %collective-permute-done.16 = bf16[384,768]{1,0:T(8,128)(2,1)S(1)} collective-permute-done((bf16[384,768]{1,0:T(8,128)(2,1)S(1)}, bf16[384,768]{1,0:T(8,128)(2,1)S(1)}, u32[]{:S(2)}, u32[]{:S(2)}) %collective-permute-start.16) | collective-permute-done | bytes 589856 | tf_op jit(solution)/shard_map/ppermute | solution.py:637
  112.8 12.5 %collective-permute-done.17 = bf16[384,768]{1,0:T(8,128)(2,1)S(1)} collective-permute-done((bf16[384,768]{1,0:T(8,128)(2,1)S(1)}, bf16[384,768]{1,0:T(8,128)(2,1)S(1)}, u32[]{:S(2)}, u32[]{:S(2)}) %collective-permute-start.17) | collective-permute-done | bytes 589856 | tf_op jit(solution)/shard_map/ppermute | solution.py:637
  126.1 2.8 multiply_convert_fusion.2
  128.9 2.8 multiply_convert_fusion.1
  132.8 2.8 multiply_convert_fusion
  137.0 1.1 add_convert_fusion
  138.1 1.2 fusion.47
  139.3 1.1 reshape.129
  141.0 1.1 fusion.57
  142.1 2.1 multiply_reduce_fusion.4
  144.3 0.8 sub.78
  145.1 1.8 div.51
  146.8 1.8 div.53
  148.6 1.7 sub.72
  150.4 1.8 sub.74
  152.2 1.5 multiply_convert_fusion.4
  155.9 1.8 convert_reduce_fusion.5
  158.9 1.9 convolution_convert_fusion.4.rest_4_
  160.7 1.9 convolution_convert_fusion.5.rest_3_
  162.7 1.9 convolution_convert_fusion.6.rest_2_
  164.6 1.8 convolution_convert_fusion.7.rest_1_
  166.4 1.8 convolution_convert_fusion.8.rest_0_
  168.4 1.8 convert_reduce_fusion.3
  170.3 1.9 convolution_convert_fusion.2.rest_6_
  172.1 2.0 convert_reduce_fusion.4
  174.2 1.8 convolution_convert_fusion.3.rest_5_
  176.0 1.8 convert_reduce_fusion.2
  177.9 1.8 convolution_convert_fusion.1.rest_7_
  181.0 0.8 fusion.78
  182.0 1.5 multiply_reduce_fusion
  184.8 1.7 convolution_convert_fusion.9
  187.8 1.7 maximum_maximum_fusion.3
  189.4 1.3 stack.63.small_ref
  190.7 146.1 %attn_bwd.1 = (f32[512,768]{1,0:T(8,128)}, f32[16,768]{1,0:T(8,128)}, f32[48,768]{1,0:T(8,128)}, bf16[320,768]{1,0:T(8,128)(2,1)}, bf16[384,768]{1,0:T(8,128)(2,...) custom-call(bf16[3,3,64,2048]{3,2,1,0:T(8,128)(2,1)} %bitcast.107, ...), custom_call_target="tpu_custom_call" | custom-call | flops 60000002048 | bytes 31457280 | tf_op jit(solution)/shard_map/attn_bwd/pallas_call | solution.py:579
  336.8 1.2 convert_bitcast_fusion.1
  338.0 0.9 slice.150
  340.9 1.6 slice_reduce_fusion
  342.5 1.3 slice.136
  343.7 1.3 slice_bitcast_fusion.3
  345.1 1.4 convert_bitcast_fusion
  347.5 1.3 add.314
  348.9 0.9 slice_convert_fusion
  350.4 1.6 maximum_convert_fusion.1
  352.1 1.6 maximum_convert_fusion
  353.7 9.1 %fusion.2 = f32[69,64,512]{2,1,0:T(8,128)} fusion(f32[69,512]{1,0:T(8,128)S(1)} %get-tuple-element.95, f32[69,512]{1,0:T(8,128)S(1)} %get-tuple-element.96, f32[69,512]{1,0:T(8,128)S(1)} %get-tuple-element.94, f32[69,512]{1,0:T(8,128)S(1)} %fusion.49, bf16[3,69,64,512]{3,2,1,0:T(8,128)(2,1)} %param.24), kind=kLoop, calls=%fused_computation.9 | loop fusion | flops 20348928 | bytes 23175168 | tf_op jit(solution)/shard_map/add | solution.py:773
  (251 shorter events, 23.9 us)
Async XLA Ops:
  0.7 3.6 copy-start
  0.7 3.6 %copy-start.5 = (bf16[512,768]{1,0:T(8,128)(2,1)S(1)}, bf16[512,768]{1,0:T(8,128)(2,1)}, u32[]{:S(2)}) copy-start(bf16[512,768]{1,0:T(8,128)(2,1)} %tiles_ref.1) | copy-start | bytes 2359300
  0.7 3.6 %copy-start.47 = (f32[768]{0:T(1024)S(1)}, f32[768]{0:T(1024)}, u32[]{:S(2)}) copy-start(f32[768]{0:T(1024)} %param.25) | copy-start | bytes 9220
  0.7 3.6 %copy-start.48 = (f32[768]{0:T(1024)S(1)}, f32[768]{0:T(1024)}, u32[]{:S(2)}) copy-start(f32[768]{0:T(1024)} %param.26) | copy-start | bytes 9220
  1.4 6.4 %copy-start.68 = (f32[768]{0:T(1024)S(1)}, f32[768]{0:T(1024)}, u32[]{:S(2)}) copy-start(f32[768]{0:T(1024)} %param.34) | copy-start | bytes 9220
  4.8 31.2 %copy-start.69 = (s32[40]{0:T(128)S(1)}, s32[40]{0:T(128)}, u32[]{:S(2)}) copy-start(s32[40]{0:T(128)} %param.23) | copy-start | bytes 484
  4.8 33.2 %copy-start.27 = (bf16[192,768]{1,0:T(8,128)(2,1)S(1)}, bf16[192,768]{1,0:T(8,128)(2,1)}, u32[]{:S(2)}) copy-start(bf16[192,768]{1,0:T(8,128)(2,1)} %param.29) | copy-start | bytes 884740
  4.8 20.6 %collective-permute-start = (bf16[512,768]{1,0:T(8,128)(2,1)S(1)}, bf16[512,768]{1,0:T(8,128)(2,1)S(1)}, u32[]{:S(2)}, u32[]{:S(2)}) collective-permute-start(bf16[512,768]{1,0:T(8,128)(2,1)S(1)} %fusion.17), channel_id=1, source_target_pairs={{0,2},{1,3},{2,0},{3,1},{4,6},{5,7},{6,4},{7,5},{8,10},{9,11},{10,... | collective-permute-start | bytes 2359304 | tf_op jit(solution)/shard_map/ppermute | solution.py:637
  7.8 32.6 %collective-permute-start.2 = (bf16[512,768]{1,0:T(8,128)(2,1)S(1)}, bf16[512,768]{1,0:T(8,128)(2,1)}, u32[]{:S(2)}, u32[]{:S(2)}) collective-permute-start(bf16[512,768]{1,0:T(8,128)(2,1)S(1)} %fusion.17), channel_id=1, source_target_pairs={{0,1},{1,0},{2,3},{3,2},{4,5},{5,4},{6,7},{7,6},{8,9},{9,8},{10,11... | collective-permute-start | bytes 2359304 | tf_op jit(solution)/shard_map/ppermute | solution.py:637
  7.8 72.6 %collective-permute-start.15 = (f32[768]{0:T(1024)S(1)}, f32[768]{0:T(1024)S(1)}, u32[]{:S(2)}, u32[]{:S(2)}) collective-permute-start(f32[768]{0:T(1024)S(1)} %copy-done.68), channel_id=1, source_target_pairs={{0,2},{1,3},{2,0},{3,1},{4,6},{5,7},{6,4},{7,5},{8,10},{9,11},{10,... | collective-permute-start | bytes 9224 | tf_op jit(solution)/shard_map/ppermute | solution.py:637
  25.4 12.6 %collective-permute-start.1 = (bf16[512,768]{1,0:T(8,128)(2,1)S(1)}, bf16[512,768]{1,0:T(8,128)(2,1)}, u32[]{:S(2)}, u32[]{:S(2)}) collective-permute-start(bf16[512,768]{1,0:T(8,128)(2,1)S(1)} %collective-permute-done), channel_id=1, source_target_pairs={{0,1},{1,0},{2,3},{3,2},{4,5},{5,4},{6,7},{7,6},{8,9},{9,8},{10,11... | collective-permute-start | bytes 2359304 | tf_op jit(solution)/shard_map/ppermute | solution.py:637
  38.0 37.1 %collective-permute-start.6 = (bf16[192,768]{1,0:T(8,128)(2,1)S(1)}, bf16[192,768]{1,0:T(8,128)(2,1)S(1)}, u32[]{:S(2)}, u32[]{:S(2)}) collective-permute-start(bf16[192,768]{1,0:T(8,128)(2,1)S(1)} %copy-done.27), channel_id=1, source_target_pairs={{0,1},{1,0},{2,3},{3,2},{4,5},{5,4},{6,7},{7,6},{8,9},{9,8},{10,11... | collective-permute-start | bytes 884744 | tf_op jit(solution)/shard_map/ppermute | solution.py:637
  38.6 34.3 %collective-permute-start.7 = (bf16[96,768]{1,0:T(8,128)(2,1)S(1)}, bf16[96,768]{1,0:T(8,128)(2,1)S(1)}, u32[]{:S(2)}, u32[]{:S(2)}) collective-permute-start(bf16[96,768]{1,0:T(8,128)(2,1)S(1)} %slice_select_fusion.2), channel_id=1, source_target_pairs={{0,2},{1,3},{2,0},{3,1},{4,6},{5,7},{6,4},{7,5},{8,10},{9,11},{10,... | collective-permute-start | bytes 442376 | tf_op jit(solution)/shard_map/ppermute | solution.py:637
  44.0 25.0 %copy-start.3 = (bf16[3,192,2048]{2,1,0:T(8,128)(2,1)}, bf16[3,192,2048]{2,1,0:T(8,128)(2,1)S(1)}, u32[]{:S(2)}) copy-start(bf16[3,192,2048]{2,1,0:T(8,128)(2,1)S(1)} %fusion.8) | copy-start | bytes 7077892
  69.1 3.8 %copy-start.2 = (bf16[3,64,2048]{2,1,0:T(8,128)(2,1)}, bf16[3,64,2048]{2,1,0:T(8,128)(2,1)S(1)}, u32[]{:S(2)}) copy-start(bf16[3,64,2048]{2,1,0:T(8,128)(2,1)S(1)} %get-tuple-element.40.o_ref) | copy-start | bytes 2359300
  69.1 3.8 %copy-start.4 = (f32[3,1,2048]{2,1,0:T(1,128)}, f32[3,1,2048]{2,1,0:T(1,128)S(1)}, u32[]{:S(2)}) copy-start(f32[3,1,2048]{2,1,0:T(1,128)S(1)} %get-tuple-element.44.lse_ref) | copy-start | bytes 73732
  69.1 16.9 %copy-start.40 = (bf16[192,512]{1,0:T(8,128)(2,1)}, bf16[192,512]{1,0:T(8,128)(2,1)S(1)}, u32[]{:S(2)}) copy-start(bf16[192,512]{1,0:T(8,128)(2,1)S(1)} %get-tuple-element.90) | copy-start | bytes 589828
  69.2 11.8 %collective-permute-start.3 = (bf16[192,512]{1,0:T(8,128)(2,1)S(1)}, bf16[192,512]{1,0:T(8,128)(2,1)S(1)}, u32[]{:S(2)}, u32[]{:S(2)}) collective-permute-start(bf16[192,512]{1,0:T(8,128)(2,1)S(1)} %get-tuple-element.93), channel_id=1, source_target_pairs={{0,1},{1,0},{2,3},{3,2},{4,5},{5,4},{6,7},{7,6},{8,9},{9,8},{10,11... | collective-permute-start | bytes 589832 | tf_op jit(solution)/shard_map/ppermute | solution.py:637
  72.8 6.4 %copy-start.25 = (bf16[768,768]{1,0:T(8,128)(2,1)S(1)}, bf16[768,768]{1,0:T(8,128)(2,1)}, u32[]{:S(2)}) copy-start(bf16[768,768]{1,0:T(8,128)(2,1)} %param.33) | copy-start | bytes 3538948
  72.8 6.1 %collective-permute-start.8 = (bf16[96,768]{1,0:T(8,128)(2,1)S(1)}, bf16[96,768]{1,0:T(8,128)(2,1)S(1)}, u32[]{:S(2)}, u32[]{:S(2)}) collective-permute-start(bf16[96,768]{1,0:T(8,128)(2,1)S(1)} %collective-permute-done.7), channel_id=1, source_target_pairs={{0,4},{4,0},{8,12},{12,8},{16,20},{20,16},{24,28},{28,24},{1,5},{5... | collective-permute-start | bytes 442376 | tf_op jit(solution)/shard_map/ppermute | solution.py:637
  74.5 7.8 %collective-permute-start.4 = (bf16[192,512]{1,0:T(8,128)(2,1)S(1)}, bf16[192,512]{1,0:T(8,128)(2,1)S(1)}, u32[]{:S(2)}, u32[]{:S(2)}) collective-permute-start(bf16[192,512]{1,0:T(8,128)(2,1)S(1)} %get-tuple-element.92), channel_id=1, source_target_pairs={{0,2},{1,3},{2,0},{3,1},{4,6},{5,7},{6,4},{7,5},{8,10},{9,11},{10,... | collective-permute-start | bytes 589832 | tf_op jit(solution)/shard_map/ppermute | solution.py:637
  75.1 9.6 %collective-permute-start.5 = (bf16[192,512]{1,0:T(8,128)(2,1)S(1)}, bf16[192,512]{1,0:T(8,128)(2,1)S(1)}, u32[]{:S(2)}, u32[]{:S(2)}) collective-permute-start(bf16[192,512]{1,0:T(8,128)(2,1)S(1)} %get-tuple-element.91), channel_id=1, source_target_pairs={{0,3},{1,2},{2,1},{3,0},{4,7},{5,6},{6,5},{7,4},{8,11},{9,10},{10,... | collective-permute-start | bytes 589832 | tf_op jit(solution)/shard_map/ppermute | solution.py:637
  79.1 1.6 collective-permute-start.9
  80.3 5.8 %copy-start.67 = (f32[768]{0:T(1024)S(1)}, f32[768]{0:T(1024)}, u32[]{:S(2)}) copy-start(f32[768]{0:T(1024)} %param.30) | copy-start | bytes 9220
  80.4 45.1 %collective-permute-start.11 = (f32[768]{0:T(1024)S(1)}, f32[768]{0:T(1024)S(1)}, u32[]{:S(2)}, u32[]{:S(2)}) collective-permute-start(f32[768]{0:T(1024)S(1)} %copy-done.68), channel_id=1, source_target_pairs={{0,1},{1,0},{2,3},{3,2},{4,5},{5,4},{6,7},{7,6},{8,9},{9,8},{10,11... | collective-permute-start | bytes 9224 | tf_op jit(solution)/shard_map/ppermute | solution.py:637
  80.8 52.0 %collective-permute-start.19 = (f32[768]{0:T(1024)S(1)}, f32[768]{0:T(1024)S(1)}, u32[]{:S(2)}, u32[]{:S(2)}) collective-permute-start(f32[768]{0:T(1024)S(1)} %collective-permute-done.15), channel_id=1, source_target_pairs={{0,1},{1,0},{2,3},{3,2},{4,5},{5,4},{6,7},{7,6},{8,9},{9,8},{10,11... | collective-permute-start | bytes 9224 | tf_op jit(solution)/shard_map/ppermute | solution.py:637
  81.0 6.0 %copy-start.44 = (bf16[768,768]{1,0:T(8,128)(2,1)}, bf16[768,768]{1,0:T(8,128)(2,1)S(1)}, u32[]{:S(2)}) copy-start(bf16[768,768]{1,0:T(8,128)(2,1)S(1)} %constant_dynamic-update-slice_fusion) | copy-start | bytes 3538948
  81.0 6.0 %copy-start.61 = (bf16[192,512]{1,0:T(8,128)(2,1)}, bf16[192,512]{1,0:T(8,128)(2,1)S(1)}, u32[]{:S(2)}) copy-start(bf16[192,512]{1,0:T(8,128)(2,1)S(1)} %collective-permute-done.3) | copy-start | bytes 589828
  81.0 45.0 %collective-permute-start.10 = (bf16[768,768]{1,0:T(8,128)(2,1)S(1)}, bf16[768,768]{1,0:T(8,128)(2,1)S(1)}, u32[]{:S(2)}, u32[]{:S(2)}) collective-permute-start(bf16[768,768]{1,0:T(8,128)(2,1)S(1)} %copy-done.25), channel_id=1, source_target_pairs={{0,1},{1,0},{2,3},{3,2},{4,5},{5,4},{6,7},{7,6},{8,9},{9,8},{10,11... | collective-permute-start | bytes 3538952 | tf_op jit(solution)/shard_map/ppermute | solution.py:637
  82.3 4.7 %copy-start.63 = (bf16[192,512]{1,0:T(8,128)(2,1)}, bf16[192,512]{1,0:T(8,128)(2,1)S(1)}, u32[]{:S(2)}) copy-start(bf16[192,512]{1,0:T(8,128)(2,1)S(1)} %collective-permute-done.4) | copy-start | bytes 589828
  82.3 16.9 %collective-permute-start.13 = (bf16[384,768]{1,0:T(8,128)(2,1)S(1)}, bf16[384,768]{1,0:T(8,128)(2,1)S(1)}, u32[]{:S(2)}, u32[]{:S(2)}) collective-permute-start(bf16[384,768]{1,0:T(8,128)(2,1)S(1)} %slice_select_fusion.1), channel_id=1, source_target_pairs={{0,2},{1,3},{2,0},{3,1},{4,6},{5,7},{6,4},{7,5},{8,10},{9,11},{10,... | collective-permute-start | bytes 1769480 | tf_op jit(solution)/shard_map/ppermute | solution.py:637
  84.6 2.4 copy-start.65
  84.6 26.2 %collective-permute-start.16 = (bf16[384,768]{1,0:T(8,128)(2,1)S(1)}, bf16[384,768]{1,0:T(8,128)(2,1)S(1)}, u32[]{:S(2)}, u32[]{:S(2)}) collective-permute-start(bf16[384,768]{1,0:T(8,128)(2,1)S(1)} %slice_select_fusion), channel_id=1, source_target_pairs={{0,2},{1,3},{2,0},{3,1},{4,6},{5,7},{6,4},{7,5},{8,10},{9,11},{10,... | collective-permute-start | bytes 1769480 | tf_op jit(solution)/shard_map/ppermute | solution.py:637
  88.0 44.8 %copy-start.28 = (bf16[512,768]{1,0:T(8,128)(2,1)}, bf16[512,768]{1,0:T(8,128)(2,1)S(1)}, u32[]{:S(2)}) copy-start(bf16[512,768]{1,0:T(8,128)(2,1)S(1)} %add_convert_fusion.1) | copy-start | bytes 2359300
  99.1 13.5 %collective-permute-start.14 = (bf16[384,768]{1,0:T(8,128)(2,1)S(1)}, bf16[384,768]{1,0:T(8,128)(2,1)S(1)}, u32[]{:S(2)}, u32[]{:S(2)}) collective-permute-start(bf16[384,768]{1,0:T(8,128)(2,1)S(1)} %collective-permute-done.13), channel_id=1, source_target_pairs={{0,4},{4,0},{8,12},{12,8},{16,20},{20,16},{24,28},{28,24},{1,5},{5... | collective-permute-start | bytes 1769480 | tf_op jit(solution)/shard_map/ppermute | solution.py:637
  102.0 10.2 %copy-start.70 = (bf16[512,768]{1,0:T(8,128)(2,1)}, bf16[512,768]{1,0:T(8,128)(2,1)S(1)}, u32[]{:S(2)}) copy-start(bf16[512,768]{1,0:T(8,128)(2,1)S(1)} %get-tuple-element.109) | copy-start | bytes 2359300
  110.9 14.4 %collective-permute-start.17 = (bf16[384,768]{1,0:T(8,128)(2,1)S(1)}, bf16[384,768]{1,0:T(8,128)(2,1)S(1)}, u32[]{:S(2)}, u32[]{:S(2)}) collective-permute-start(bf16[384,768]{1,0:T(8,128)(2,1)S(1)} %collective-permute-done.16), channel_id=1, source_target_pairs={{0,4},{4,0},{8,12},{12,8},{16,20},{20,16},{24,28},{28,24},{1,5},{5... | collective-permute-start | bytes 1769480 | tf_op jit(solution)/shard_map/ppermute | solution.py:637
  112.6 19.1 %collective-permute-start.12 = (bf16[768,768]{1,0:T(8,128)(2,1)S(1)}, bf16[768,768]{1,0:T(8,128)(2,1)S(1)}, u32[]{:S(2)}, u32[]{:S(2)}) collective-permute-start(bf16[768,768]{1,0:T(8,128)(2,1)S(1)} %copy-done.23), channel_id=1, source_target_pairs={{0,1},{1,0},{2,3},{3,2},{4,5},{5,4},{6,7},{7,6},{8,9},{9,8},{10,11... | collective-permute-start | bytes 3538952 | tf_op jit(solution)/shard_map/ppermute | solution.py:637
  112.7 16.2 %copy-start.8 = (bf16[384,768]{1,0:T(8,128)(2,1)}, bf16[384,768]{1,0:T(8,128)(2,1)S(1)}, u32[]{:S(2)}) copy-start(bf16[384,768]{1,0:T(8,128)(2,1)S(1)} %get-tuple-element.89) | copy-start | bytes 1769476
  125.3 7.5 %collective-permute-start.18 = (bf16[768,768]{1,0:T(8,128)(2,1)S(1)}, bf16[768,768]{1,0:T(8,128)(2,1)S(1)}, u32[]{:S(2)}, u32[]{:S(2)}) collective-permute-start(bf16[768,768]{1,0:T(8,128)(2,1)S(1)} %pad_maximum_fusion.1), channel_id=1, source_target_pairs={{0,1},{1,0},{2,3},{3,2},{4,5},{5,4},{6,7},{7,6},{8,9},{9,8},{10,11... | collective-permute-start | bytes 3538952 | tf_op jit(solution)/shard_map/ppermute | solution.py:637
  125.4 11.6 %copy-start.10 = (bf16[384,768]{1,0:T(8,128)(2,1)}, bf16[384,768]{1,0:T(8,128)(2,1)S(1)}, u32[]{:S(2)}) copy-start(bf16[384,768]{1,0:T(8,128)(2,1)S(1)} %get-tuple-element.86) | copy-start | bytes 1769476
  125.4 11.6 %copy-start.12 = (bf16[384,768]{1,0:T(8,128)(2,1)}, bf16[384,768]{1,0:T(8,128)(2,1)S(1)}, u32[]{:S(2)}) copy-start(bf16[384,768]{1,0:T(8,128)(2,1)S(1)} %get-tuple-element.87) | copy-start | bytes 1769476
  125.5 10.1 %collective-permute-start.20 = (bf16[768,768]{1,0:T(8,128)(2,1)S(1)}, bf16[768,768]{1,0:T(8,128)(2,1)S(1)}, u32[]{:S(2)}, u32[]{:S(2)}) collective-permute-start(bf16[768,768]{1,0:T(8,128)(2,1)S(1)} %pad_maximum_fusion.2), channel_id=1, source_target_pairs={{0,1},{1,0},{2,3},{3,2},{4,5},{5,4},{6,7},{7,6},{8,9},{9,8},{10,11... | collective-permute-start | bytes 3538952 | tf_op jit(solution)/shard_map/ppermute | solution.py:637
  126.1 2.9 copy-start.53
  128.9 2.9 copy-start.72
  131.8 5.2 %copy-start.30 = (bf16[512,768]{1,0:T(8,128)(2,1)}, bf16[512,768]{1,0:T(8,128)(2,1)S(1)}, u32[]{:S(2)}) copy-start(bf16[512,768]{1,0:T(8,128)(2,1)S(1)} %get-tuple-element.113) | copy-start | bytes 2359300
  132.8 2.8 copy-start.55
  141.0 3.2 copy-start.17
  141.0 3.2 copy-start.18
  141.0 3.2 copy-start.19
  142.1 2.1 copy-start.20
  145.1 7.1 %copy-start.14 = (f32[207,512]{1,0:T(8,128)S(1)}, f32[207,512]{1,0:T(8,128)}, u32[]{:S(2)}) copy-start(f32[207,512]{1,0:T(8,128)} %fusion.47) | copy-start | bytes 1271812
  160.7 1.9 copy-start.31
  166.4 2.0 copy-start.11
  166.4 2.0 copy-start.13
  166.4 2.0 copy-start.79
  184.2 2.3 copy-start.6
  336.8 2.8 copy-start.43
  336.8 8.2 %copy-start.36 = (bf16[384,768]{1,0:T(8,128)(2,1)S(1)}, bf16[384,768]{1,0:T(8,128)(2,1)}, u32[]{:S(2)}) copy-start(bf16[384,768]{1,0:T(8,128)(2,1)} %get-tuple-element.47) | copy-start | bytes 1769476
  336.8 8.2 %copy-start.39 = (bf16[256,768]{1,0:T(8,128)(2,1)S(1)}, bf16[256,768]{1,0:T(8,128)(2,1)}, u32[]{:S(2)}) copy-start(bf16[256,768]{1,0:T(8,128)(2,1)} %get-tuple-element.48) | copy-start | bytes 1179652
  345.0 2.0 copy-start.16
  345.1 2.5 copy-start.7
  347.5 2.2 copy-start.15
  353.7 9.1 %copy-start.1 = (f32[40,768]{1,0:T(8,128)S(1)}, f32[40,768]{1,0:T(8,128)}, u32[]{:S(2)}) copy-start(f32[40,768]{1,0:T(8,128)} %param.27) | copy-start | bytes 368644
  (37 other events, 54.1 us)

commit v3 on v2

--- a/solution.py
+++ b/solution.py
@@ -18,46 +18,276 @@
     return lax.dot_general(a, b, (dims, ((), ())), preferred_element_type=F32)
 
 
-def fwd_kernel(q_ref, k_ref, v_ref, o_ref, lse_ref, ks, *, scale):
-    @pl.when(pl.program_id(1) == 0)
+def fwd_kernel(
+    tiles_ref, gain_ref, shift_ref, wt_ref, proj_ref, wide_ref, narrow_ref, exp_ref, slope_ref,
+    rows_out, qkv_ref, o_ref, lse_ref, own_out, dots_ref, proj_all, wide_all, narrow_all,
+    rows_ref, own_ref, out_sem, ks, stream, stream_g, stream_sem, row_send, row_recv, o_send, o_recv, o_local,
+    w_send, w_recv, *, scale, dp_size, tp_size, heads
+):
+    i, h = pl.program_id(0), pl.program_id(1)
+    steps = tp_size * heads
+    step = i * heads + h
+    dpi, tpi = lax.axis_index("dp"), lax.axis_index("tp")
+    rows_dev, width = tiles_ref.shape
+    piece = rows_dev // 2
+    mine = lax.rem(dpi, 2)
+
+    def remote(src, dst, ssem, rsem, axis, bit):
+        dev = (partner(dpi, bit), tpi) if axis == "dp" else (dpi, partner_any(tpi, bit))
+        return pltpu.make_async_remote_copy(
+            src_ref=src, dst_ref=dst, send_sem=ssem, recv_sem=rsem,
+            device_id=dev, device_id_type=pl.DeviceIdType.MESH,
+        )
+
+    def row_copy(kind, c):
+        a, b, bit = ((0, 1, 1), (0, 2, 2), (2, 3, 1))[kind]
+        here = pl.ds(c * piece, piece)
+        return remote(
+            rows_ref.at[a, here], rows_ref.at[b, here],
+            row_send.at[kind, c], row_recv.at[kind, c], "tp", bit,
+        )
+
+    parts = []
+    for src, dst, cuts in ((proj_ref, proj_all, 1), (wide_ref, wide_all, 2), (narrow_ref, narrow_all, 2)):
+        n = src.shape[0] // cuts
+        for c in range(cuts):
+            parts.append((src, dst, c * n, n // 2))
+
+    def w_half(part, whose):
+        return pl.ds(pl.multiple_of(part[2] + whose * part[3], 16), part[3])
+
+    def w_far(n):
+        src, dst, _, _ = parts[n]
+        rows = w_half(parts[n], mine)
+        return remote(
+            src.at[rows], dst.at[1, rows], w_send.at[n, 0], w_recv.at[n, 0], "tp", 2
+        )
+
+    def w_side(n):
+        dst = parts[n][1]
+        rows = w_half(parts[n], mine)
+        here = dst.at[1, rows]
+        return remote(here, here, w_send.at[n, 1], w_recv.at[n, 1], "dp", 1)
+
+    def w_fwd(n, second):
+        dst = parts[n][1]
+        rows = w_half(parts[n], 1 - mine if second else mine)
+        k = 3 if second else 2
+        return remote(
+            dst.at[1, rows], dst.at[2, rows], w_send.at[n, k], w_recv.at[n, k], "tp", 1
+        )
+
+    def w_near(n):
+        src, dst, lo, half = parts[n]
+        rows = pl.ds(lo, 2 * half)
+        return remote(src.at[rows], dst.at[0, rows], w_send.at[n, 4], w_recv.at[n, 4], "tp", 1)
+
+    def o_copy(p):
+        if p == 0:
+            return pltpu.make_async_copy(o_ref.at[0], own_ref.at[0], o_local)
+        return remote(o_ref.at[p], own_ref.at[p], o_send.at[p], o_recv.at[p], "tp", p)
+
+    fields, sites = slope_ref.shape[0], slope_ref.shape[1]
+    per = stream.shape[2]
+    groups = fields // per
+    depth = stream.shape[0]
+
+    def stream_copies(g):
+        slot = lax.rem(g, depth)
+        at = pl.ds(g * per, per)
+        return (
+            pltpu.make_async_copy(
+                exp_ref.at[:, at], stream.at[slot], stream_sem.at[slot, 0]
+            ),
+            pltpu.make_async_copy(
+                slope_ref.at[at], stream_g.at[slot], stream_sem.at[slot, 1]
+            ),
+        )
+
+    @pl.when(step == 0)
     def _():
-        ks[...] = k_ref[0, 0].T
-
-    q = q_ref[0, 0] * jnp.bfloat16(scale)
-    s = dot(ks[...], q)
+        barrier = pltpu.get_barrier_semaphore()
+        others = [("tp", 1), ("tp", 2), ("tp", 3), ("dp", 1)]
+        for axis, bit in others:
+            dev = (partner(dpi, bit), tpi) if axis == "dp" else (dpi, partner_any(tpi, bit))
+            pl.semaphore_signal(
+                barrier, inc=1, device_id=dev, device_id_type=pl.DeviceIdType.MESH
+            )
+        for g in range(min(depth - 1, groups)):
+            for cp in stream_copies(g):
+                cp.start()
+        blk = 64
+
+        def norm_rows(r, carry):
+            here = pl.ds(pl.multiple_of(r * blk, blk), blk)
+            hat, _ = norm_parts(tiles_ref[here].astype(F32))
+            rows_ref[0, here] = (hat * gain_ref[...] + shift_ref[...]).astype(BF16)
+            return carry
+
+        half = piece // blk
+        lax.fori_loop(0, half, norm_rows, 0)
+        pl.semaphore_wait(barrier, len(others))
+        row_copy(1, 0).start()
+        lax.fori_loop(half, 2 * half, norm_rows, 0)
+        row_copy(1, 1).start()
+        row_copy(0, 0).start()
+        row_copy(0, 1).start()
+
+        def contract(g, carry):
+            @pl.when(g + depth - 1 < groups)
+            def _():
+                for cp in stream_copies(g + depth - 1):
+                    cp.start()
+
+            for cp in stream_copies(g):
+                cp.wait()
+            slot = lax.rem(g, depth)
+            for j in range(per):
+                slope = stream_g[slot, j].astype(F32)
+                for e in range(EXPERTS):
+                    dots_ref[e, pl.ds(g * per + j, 1)] = jnp.sum(
+                        stream[slot, e, j].astype(F32) * slope, axis=0, keepdims=True
+                    )
+                dots_ref[EXPERTS, pl.ds(g * per + j, 1)] = jnp.sum(slope, axis=0, keepdims=True)
+            return carry
+
+        dots_ref[...] = jnp.zeros_like(dots_ref)
+        lax.fori_loop(0, groups, contract, 0)
+
+        def project(p):
+            lane = pl.ds(p * rows_dev, rows_dev)
+            for s in range(3):
+                part = dot(wt_ref[s], rows_ref[p], ((1,), (1,))).astype(BF16)
+                qkv_ref[s, :, :, lane] = part.reshape(heads, HD, rows_dev)
+            for hh in range(heads):
+                ks[hh, lane] = qkv_ref[1, hh, :, lane].T
+
+        project(0)
+        for c in range(2):
+            row_copy(0, c).wait()
+        project(1)
+        for c in range(2):
+            row_copy(1, c).wait()
+            row_copy(2, c).start()
+        w_far(0).start()
+        w_far(1).start()
+        project(2)
+        for c in range(2):
+            row_copy(2, c).wait()
+        for n in range(len(parts)):
+            w_near(n).start()
+        rows_copy = pltpu.make_async_copy(rows_ref, rows_out, out_sem.at[0])
+        rows_copy.start()
+        project(3)
+
+    p = lax.rem(i + 2, tp_size)
+    lanes = pl.ds(pl.multiple_of(p * rows_dev, rows_dev), rows_dev)
+    q = qkv_ref[0, h, :, lanes] * jnp.bfloat16(scale)
+    s = dot(ks[h], q)
     m = jnp.max(s, axis=0, keepdims=True)
-    p = jnp.exp(s - m)
-    l = jnp.sum(p, axis=0, keepdims=True)
-    o = dot(v_ref[0, 0], p.astype(BF16))
-    o_ref[0] = (o / l).astype(BF16)
-    lse_ref[0] = m + jnp.log(l)
-
-
-def attn_fwd(qkv, scale, bq):
-    _, heads, _, rows = qkv.shape
+    e = jnp.exp(s - m)
+    l = jnp.sum(e, axis=0, keepdims=True)
+    o_ref[p, h] = (dot(qkv_ref[2, h], e.astype(BF16)) / l).astype(BF16)
+    lse_ref[p, h] = m + jnp.log(l)
+
+    seq = {}
+
+    def after(st, *what):
+        seq.setdefault(min(st, steps - 1), []).extend(what)
+
+    arrive = (1, 3, 6, 9, 11)
+    side = (3, 7, 10, 11, 11)
+    for n in range(len(parts)):
+        after(arrive[n], ("far", n))
+    for n in range(len(parts)):
+        after(side[n], ("side", n))
+    for st, what in seq.items():
+
+        @pl.when(step == st)
+        def _():
+            for kind, n in what:
+                if kind == "far":
+                    w_far(n).wait()
+                    if n + 2 < len(parts):
+                        w_far(n + 2).start()
+                    w_side(n).start()
+                    w_fwd(n, False).start()
+                else:
+                    w_side(n).wait()
+                    w_fwd(n, True).start()
+
+    for k in range(tp_size):
+
+        @pl.when(step == k * heads + heads - 1)
+        def _():
+            o_copy((k + 2) % tp_size).start()
+
+    @pl.when(step == steps - 1)
+    def _():
+        for k in range(tp_size):
+            o_copy(k).wait()
+        own_copy = pltpu.make_async_copy(own_ref, own_out, out_sem.at[1])
+        own_copy.start()
+        for n in range(len(parts)):
+            w_near(n).wait()
+            w_fwd(n, False).wait()
+            w_fwd(n, True).wait()
+        own_copy.wait()
+        pltpu.make_async_copy(rows_ref, rows_out, out_sem.at[0]).wait()
+
+
+def attn_fwd(tiles, gain, shift, wt, proj, wide, narrow, experts, slope, mesh, scale):
+    rows_dev, width = tiles.shape
+    heads = proj.shape[0] // HD
+    tp_size, dp_size = mesh.shape["tp"], mesh.shape["dp"]
+    frame = tp_size * rows_dev
+    fields, sites = slope.shape[0], slope.shape[1]
+    per = 3 if fields % 3 == 0 else 1
+    depth = 4
+    any_spec = pl.BlockSpec(memory_space=pl.ANY)
+    vmem = pl.BlockSpec(memory_space=pltpu.VMEM)
     return pl.pallas_call(
-        functools.partial(fwd_kernel, scale=scale),
-        grid=(heads, rows // bq),
-        in_specs=[
-            pl.BlockSpec((1, 1, HD, bq), lambda h, i: (0, h, 0, i)),
-            pl.BlockSpec((1, 1, HD, rows), lambda h, i: (1, h, 0, 0)),
-            pl.BlockSpec((1, 1, HD, rows), lambda h, i: (2, h, 0, 0)),
+        functools.partial(
+            fwd_kernel, scale=scale, dp_size=dp_size, tp_size=tp_size, heads=heads
+        ),
+        grid=(tp_size, heads),
+        in_specs=[vmem] * 4 + [any_spec] * 5,
+        out_specs=[any_spec] + [vmem] * 3 + [any_spec, vmem] + [any_spec] * 3,
+        out_shape=[
+            jax.ShapeDtypeStruct((tp_size, rows_dev, width), BF16),
+            jax.ShapeDtypeStruct((3, heads, HD, frame), BF16),
+            jax.ShapeDtypeStruct((tp_size, heads, HD, rows_dev), BF16),
+            jax.ShapeDtypeStruct((tp_size, heads, 1, rows_dev), F32),
+            jax.ShapeDtypeStruct((tp_size, heads, HD, rows_dev), BF16),
+            jax.ShapeDtypeStruct((EXPERTS + 1, HEAD_ROWS, rows_dev), F32),
+            jax.ShapeDtypeStruct((tp_size - 1,) + proj.shape, BF16),
+            jax.ShapeDtypeStruct((tp_size - 1,) + wide.shape, BF16),
+            jax.ShapeDtypeStruct((tp_size - 1,) + narrow.shape, BF16),
         ],
-        out_specs=[
-            pl.BlockSpec((1, HD, bq), lambda h, i: (h, 0, i)),
-            pl.BlockSpec((1, 1, bq), lambda h, i: (h, 0, i)),
+        scratch_shapes=[
+            pltpu.VMEM((tp_size, rows_dev, width), BF16),
+            pltpu.VMEM((tp_size, heads, HD, rows_dev), BF16),
+            pltpu.SemaphoreType.DMA((2,)),
+            pltpu.VMEM((heads, frame, HD), BF16),
+            pltpu.VMEM((depth, EXPERTS, per, sites, rows_dev), BF16),
+            pltpu.VMEM((depth, per, sites, rows_dev), BF16),
+            pltpu.SemaphoreType.DMA((depth, 2)),
+            pltpu.SemaphoreType.DMA((3, 2)),
+            pltpu.SemaphoreType.DMA((3, 2)),
+            pltpu.SemaphoreType.DMA((tp_size,)),
+            pltpu.SemaphoreType.DMA((tp_size,)),
+            pltpu.SemaphoreType.DMA,
+            pltpu.SemaphoreType.DMA((5, 5)),
+            pltpu.SemaphoreType.DMA((5, 5)),
         ],
-        out_shape=[
-            jax.ShapeDtypeStruct((heads, HD, rows), BF16),
-            jax.ShapeDtypeStruct((heads, 1, rows), F32),
-        ],
-        scratch_shapes=[pltpu.VMEM((rows, HD), BF16)],
-        compiler_params=pltpu.CompilerParams(vmem_limit_bytes=50 << 20),
+        compiler_params=pltpu.CompilerParams(
+            vmem_limit_bytes=56 << 20, collective_id=0, has_side_effects=True
+        ),
         cost_estimate=pl.CostEstimate(
-            flops=24_000_000_000, bytes_accessed=4 << 20, transcendentals=heads * rows * rows
+            flops=30_000_000_000, bytes_accessed=40 << 20, transcendentals=heads * frame * frame
         ),
         name="attn_fwd",
-    )(qkv, qkv, qkv)
+    )(tiles, gain, shift, wt, proj, wide, narrow, experts, slope)
 
 
 def partner(index, bit):
@@ -85,7 +315,7 @@
     qkv_ref, o_ref, lse_ref, do_ref, rows_ref, wt_ref, tiles_ref, gain_ref, onehot_ref, small_ref,
     *rest, scale, chunks, dp_size, heads, tp_size, width
 ):
-    n_src = tp_size * sum(1 for c in chunks if c["tp"] and c["part"] == 0)
+    n_src = sum(1 for c in chunks if c["tp"] and c["part"] == 0)
     srcs = rest[:n_src]
     tok_ref, sum_ref, last_ref, head_ref = rest[n_src : n_src + 4]
     n_out = n_src + 4 + len(chunks)
@@ -163,7 +393,7 @@
             ss, rs = send_sems.at[self.k], recv_sems.at[self.k]
             if kind == "C":
                 lo = self.c["part"] * self.rows
-                blk = [r.at[pl.ds(lo, self.rows)] for r in self.c_src]
+                blk = [self.c_src.at[p, pl.ds(lo, self.rows)] for p in range(tp_size)]
                 return [
                     remote(blk[1], self.got, ss.at[0], rs.at[0], "tp", 1),
                     remote(blk[3], self.got_far, ss.at[1], rs.at[1], "tp", 1),
@@ -267,8 +497,8 @@
         ch = Chunk(k)
         if c["tp"]:
             if c["part"] == 0:
-                at += tp_size
-            ch.c_src = srcs[at - tp_size : at]
+                at += 1
+            ch.c_src = srcs[at - 1]
         work.append(ch)
     done = [0] * len(work)
 
@@ -341,10 +571,10 @@
     qt = qkv_ref[0, h, :, lanes] * jnp.bfloat16(scale)
     dot_t = dos[i, h]
     dsum = jnp.sum(
-        dot_t.astype(F32) * o_ref[h, :, lanes].astype(F32), axis=0, keepdims=True
+        dot_t.astype(F32) * o_ref[i, h].astype(F32), axis=0, keepdims=True
     )
     s = dot(ks[h], qt)
-    p = jnp.exp(s - lse_ref[h, :, lanes])
+    p = jnp.exp(s - lse_ref[i, h])
     dp = dot(vs[h], dot_t)
     ds = (p * (dp - dsum)).astype(BF16)
     dqkv[0, h, :, lanes] = (dot(qkv_ref[1, h], ds) * scale).astype(BF16)
@@ -522,7 +752,7 @@
     tp_size, dp_size = mesh.shape["tp"], mesh.shape["dp"]
     nbits = dp_size.bit_length() - 1
     half = width // 2
-    ph_rows = parts[2][0].shape[0]
+    ph_rows = parts[2].shape[1]
     chunks = [
         dict(tp=True, rows=half, part=0, order=[1, "X", 2, 4]),
         dict(tp=True, rows=half, part=1, order=["X", 1, 2, 4]),
@@ -575,14 +805,13 @@
     ]
     any_spec = pl.BlockSpec(memory_space=pl.ANY)
     vmem = pl.BlockSpec(memory_space=pltpu.VMEM)
-    flat = [x for group in parts for x in group]
     return pl.pallas_call(
         functools.partial(
             bwd_kernel, scale=scale, chunks=chunks, dp_size=dp_size, heads=heads,
             tp_size=tp_size, width=width,
         ),
         grid=(tp_size, heads),
-        in_specs=[vmem, vmem, vmem, any_spec] + [vmem] * 6 + [any_spec] * len(flat),
+        in_specs=[vmem, vmem, vmem, any_spec] + [vmem] * 6 + [any_spec] * len(parts),
         out_specs=[vmem, vmem, vmem, any_spec] + [any_spec] * n_k,
         out_shape=[
             jax.ShapeDtypeStruct((rows_dev, width), F32),
@@ -599,7 +828,178 @@
             flops=60_000_000_000, bytes_accessed=30 << 20, transcendentals=heads * frame * frame
         ),
         name="attn_bwd",
-    )(qkv, o, lse, do, rows, wt, tiles, gain, onehot, small, *flat)
+    )(qkv, o, lse, do, rows, wt, tiles, gain, onehot, small, *parts)
+
+
+def mid_kernel(
+    tiles_ref, o_ref, dots_ref, off_ref, vec_ref, hw_ref, hb_ref, scale_ref,
+    pj_own, pj_far, wi_own, wi_far, na_own, na_far,
+    dn_ref, dw_ref, ph_ref, do_ref, dx1_ref, small_ref, gates_ref, corr_ref,
+    pj, wi, na, x1, hat, rstd, c_low, act, slope, h_low, hg, dx2, dz, du, dc, dy, hd, dn, dw, ph, dos,
+    in_sem, out_sem, *, tp_size, heads
+):
+    tpi = lax.axis_index("tp")
+    rows_dev, width = tiles_ref.shape
+    nh = heads * HD
+    half = rows_dev // 2
+    blocks = [pl.ds(r * half, half) for r in range(2)]
+
+    def loads(k, own, far, dst):
+        out = []
+        for p in range(tp_size):
+            src = own if p == 0 else far.at[p - 1]
+            n = src.shape[0]
+            to = dst.at[pl.ds(p * n, n)] if len(dst.shape) == 2 else dst.at[p]
+            out.append(pltpu.make_async_copy(src, to, in_sem.at[k, p]))
+        return out
+
+    load_pj = loads(0, pj_own, pj_far, pj)
+    load_wi = loads(1, wi_own, wi_far, wi)
+    load_na = loads(2, na_own, na_far, na)
+    for cp in load_pj + load_wi + load_na:
+        cp.start()
+    small_ref[...] = jnp.zeros_like(small_ref)
+    proj_bias, gain2, shift2, out_bias = (vec_ref[k : k + 1] for k in range(4))
+    for cp in load_pj:
+        cp.wait()
+    for r in blocks:
+        v = tiles_ref[r].astype(F32) + dot(o_ref[:, r], pj[...], ((0,), (0,))) + proj_bias
+        x1[r] = v
+        hv, rs = norm_parts(v)
+        hat[r] = hv
+        rstd[r] = rs
+        c_low[r] = (hv * gain2 + shift2).astype(BF16)
+    for p in range(tp_size):
+        load_wi[p].wait()
+        cols = pl.ds(p * width, width)
+        for r in blocks:
+            m, d = gelu_parts(dot(c_low[r], wi[p]) + off_ref[p : p + 1])
+            act[r, cols] = m.astype(BF16)
+            slope[r, cols] = d
+    for cp in load_na:
+        cp.wait()
+    for r in blocks:
+        h_low[r] = (x1[r] + dot(act[r], na[...]) + out_bias).astype(BF16)
+
+    logits = dot(hw_ref[...], h_low[...], ((1,), (1,))) + hb_ref[...]
+    row_scale = scale_ref[0:1, 0:1]
+    lg = [logits[e * HEAD_ROWS : (e + 1) * HEAD_ROWS] for e in range(EXPERTS)]
+    top = jnp.maximum(jnp.maximum(lg[0], lg[1]), lg[2])
+    ex = [jnp.exp(v - top) for v in lg]
+    inv = 1.0 / (ex[0] + ex[1] + ex[2])
+    gt = [v * inv for v in ex]
+    mixed = gt[0] * dots_ref[0] + gt[1] * dots_ref[1] + gt[2] * dots_ref[2]
+    for e in range(EXPERTS):
+        gates_ref[e] = gt[e]
+        hg[e * HEAD_ROWS : (e + 1) * HEAD_ROWS] = (gt[e] * (dots_ref[e] - mixed)).astype(BF16)
+    hg[EXPERTS * HEAD_ROWS :] = (dots_ref[EXPERTS] * row_scale).astype(BF16)
+    corr_ref[...] = logits[EXPERTS * HEAD_ROWS :] * row_scale
+    d2 = dot(hg[...], hw_ref[...], ((0,), (0,)))
+    dx2[...] = d2
+    dz[...] = d2.astype(BF16)
+    small_ref[0:1] = jnp.sum(d2, axis=0, keepdims=True)
+    ones = jnp.ones((8, rows_dev), BF16)
+    small_ref[4:5, : tp_size * HEAD_ROWS] = dot(ones, hg[...], ((1,), (1,)))[0:1]
+
+    def send_out(k, p, src, dst):
+        cp = pltpu.make_async_copy(src, dst, out_sem.at[k, p])
+        cp.start()
+        return cp
+
+    outs = []
+    for p in range(tp_size):
+        cols = pl.ds(p * width, width)
+        dn[p] = dot(act[:, cols], dz[...], ((0,), (0,))).astype(BF16)
+        outs.append(send_out(0, p, dn.at[p], dn_ref.at[p]))
+    for p in range(tp_size):
+        cols = pl.ds(p * width, width)
+        for r in blocks:
+            v = dot(dz[r], na[cols], ((1,), (1,))) * slope[r, cols]
+            low = v.astype(BF16)
+            du[p, r] = low
+            small_ref[8 + p : 9 + p] += jnp.sum(low.astype(F32), axis=0, keepdims=True)
+    for p in range(tp_size):
+        dw[p] = dot(c_low[...], du[p], ((0,), (0,))).astype(BF16)
+        outs.append(send_out(1, p, dw.at[p], dw_ref.at[p]))
+    for r in blocks:
+        g = dot(du[0, r], wi[0], ((1,), (1,)))
+        for p in range(1, tp_size):
+            g = g + dot(du[p, r], wi[p], ((1,), (1,)))
+        hv = hat[r]
+        d1 = dx2[r] + norm_back(hv, rstd[r], gain2, g)
+        dx1_ref[r] = d1
+        dy[r] = d1.astype(BF16)
+        small_ref[1:2] += jnp.sum(g * hv, axis=0, keepdims=True)
+        small_ref[2:3] += jnp.sum(g, axis=0, keepdims=True)
+        small_ref[3:4] += jnp.sum(d1, axis=0, keepdims=True)
+    dos[...] = dot(pj[...], dy[...], ((1,), (1,))).astype(BF16).reshape(dos.shape)
+    outs.append(send_out(2, 0, dos, do_ref))
+    dp = dot(o_ref[...], dy[...]).astype(BF16)
+    hd[...] = dot(hg[...], h_low[...]).astype(BF16)
+    for p in range(tp_size):
+        ph[p, 0:nh] = dp[p * nh : (p + 1) * nh]
+        at = pl.ds(pl.multiple_of(partner_any(tpi, p) * HEAD_ROWS, 16), HEAD_ROWS)
+        ph[p, nh : nh + HEAD_ROWS] = hd[at]
+        ph[p, nh + HEAD_ROWS :] = jnp.zeros((ph.shape[1] - nh - HEAD_ROWS, width), BF16)
+        outs.append(send_out(3, p, ph.at[p], ph_ref.at[p]))
+    for cp in outs:
+        cp.wait()
+
+
+def mid(tiles, o_own, dots, off, vec, hw, hb, row_scale, weights, mesh, heads):
+    rows_dev, width = tiles.shape
+    tp_size = mesh.shape["tp"]
+    nh = heads * HD
+    ph_rows = -(-(nh + HEAD_ROWS) // 128) * 128
+    n_head = hw.shape[0]
+    any_spec = pl.BlockSpec(memory_space=pl.ANY)
+    vmem = pl.BlockSpec(memory_space=pltpu.VMEM)
+    big = (tp_size, width, width)
+    return pl.pallas_call(
+        functools.partial(mid_kernel, tp_size=tp_size, heads=heads),
+        in_specs=[vmem] * 8 + [any_spec] * 6,
+        out_specs=[any_spec] * 4 + [vmem] * 4,
+        out_shape=[
+            jax.ShapeDtypeStruct(big, BF16),
+            jax.ShapeDtypeStruct(big, BF16),
+            jax.ShapeDtypeStruct((tp_size, ph_rows, width), BF16),
+            jax.ShapeDtypeStruct((tp_size, heads, HD, rows_dev), BF16),
+            jax.ShapeDtypeStruct((rows_dev, width), F32),
+            jax.ShapeDtypeStruct((16, width), F32),
+            jax.ShapeDtypeStruct((EXPERTS, HEAD_ROWS, rows_dev), F32),
+            jax.ShapeDtypeStruct((HEAD_ROWS, rows_dev), F32),
+        ],
+        scratch_shapes=[
+            pltpu.VMEM((tp_size * nh, width), BF16),
+            pltpu.VMEM(big, BF16),
+            pltpu.VMEM((tp_size * width, width), BF16),
+            pltpu.VMEM((rows_dev, width), F32),
+            pltpu.VMEM((rows_dev, width), F32),
+            pltpu.VMEM((rows_dev, 1), F32),
+            pltpu.VMEM((rows_dev, width), BF16),
+            pltpu.VMEM((rows_dev, tp_size * width), BF16),
+            pltpu.VMEM((rows_dev, tp_size * width), F32),
+            pltpu.VMEM((rows_dev, width), BF16),
+            pltpu.VMEM((n_head, rows_dev), BF16),
+            pltpu.VMEM((rows_dev, width), F32),
+            pltpu.VMEM((rows_dev, width), BF16),
+            pltpu.VMEM((tp_size, rows_dev, width), BF16),
+            pltpu.VMEM((8, width), F32),
+            pltpu.VMEM((rows_dev, width), BF16),
+            pltpu.VMEM((n_head, width), BF16),
+            pltpu.VMEM(big, BF16),
+            pltpu.VMEM(big, BF16),
+            pltpu.VMEM((tp_size, ph_rows, width), BF16),
+            pltpu.VMEM((tp_size, heads, HD, rows_dev), BF16),
+            pltpu.SemaphoreType.DMA((3, tp_size)),
+            pltpu.SemaphoreType.DMA((4, tp_size)),
+        ],
+        compiler_params=pltpu.CompilerParams(vmem_limit_bytes=60 << 20),
+        cost_estimate=pl.CostEstimate(
+            flops=18_000_000_000, bytes_accessed=30 << 20, transcendentals=2_000_000
+        ),
+        name="mid",
+    )(tiles, o_own, dots, off, vec, hw, hb, row_scale, *weights)
 
 
 def norm_parts(values):
@@ -641,20 +1041,6 @@
 
     def across(x):
         return swap(x, "tp", 2)
-
-    def diag(x):
-        return swap(x, "tp", 3)
-
-    def my_bit(bit):
-        return (lax.axis_index("dp") & bit) != 0
-
-    def gather_tp(x):
-        n = x.shape[0] // 2
-        mine = my_bit(1)
-        half = across(jnp.where(mine, x[n:], x[:n]))
-        other = swap(half, "dp", 1)
-        far = jnp.concatenate([jnp.where(mine, other, half), jnp.where(mine, half, other)], axis=0)
-        return [x, core(x), far, core(far)]
 
     def body(
         tile_vectors,
@@ -691,137 +1077,73 @@
         row_scale = lax.rsqrt(
             lax.dynamic_slice_in_dim(horizon_sample_tally, lead, 1, 0).astype(F32)
         )[0]
-        residual = tile_vectors.astype(F32)
-
-        hat1, rstd1 = norm_parts(residual)
-        attn_own = (hat1 * early_layernorm_scale + early_layernorm_shift + embed).astype(BF16)
-        rows2 = across(attn_own)
-        rows1 = core(attn_own)
-        rows3 = core(rows2)
-        rows2, rows3, triple_w, proj_w, wide_w, narrow_w = lax.optimization_barrier(
-            (rows2, rows3, triple_head_matrix, attending_matrix, widening_matrix, narrowing_matrix)
+        nh = heads * HD
+        w_t = jnp.transpose(triple_head_matrix, (0, 2, 1))
+        (attn_rows, qkv, o_heads, lse, o_own, dots, proj_all, wide_all, narrow_all) = attn_fwd(
+            tile_vectors,
+            early_layernorm_scale[None, :],
+            early_layernorm_shift[None, :] + embed,
+            w_t,
+            attending_matrix,
+            widening_matrix,
+            narrowing_matrix,
+            specialist_outlooks,
+            combined_loss_slope,
+            mesh,
+            scale_val,
         )
-        attn_rows = jnp.concatenate([attn_own, rows1, rows2, rows3], axis=0)
-
-        proj_all = gather_tp(proj_w)
-        wide_all = gather_tp(wide_w)
-        narrow_all = gather_tp(narrow_w)
         off2 = across(widening_offset)
-        off_all = [widening_offset, core(widening_offset), off2, core(off2)]
-
-        qkv = jnp.einsum(
-            "sdh,td->sht", triple_w, attn_rows, preferred_element_type=F32
-        ).astype(BF16)
-        qkv = qkv.reshape(3, heads, HD, rows_frame)
-        o_heads, lse = attn_fwd(qkv, scale_val, min(512, rows_frame))
-
-        slope = combined_loss_slope.astype(F32)
-        expert_dot = jnp.stack(
+        off_all = jnp.stack([widening_offset, core(widening_offset), off2, core(off2)])
+
+        def head_pad(x):
+            x = x.reshape((EXPERTS + 1, fields) + x.shape[1:])
+            x = jnp.pad(x, ((0, 0), (0, HEAD_ROWS - fields)) + ((0, 0),) * (x.ndim - 2))
+            return x.reshape((-1,) + x.shape[2:])
+
+        hw = head_pad(jnp.concatenate([router_matrix, adjuster_matrix], axis=1).T)
+        hb = head_pad(jnp.concatenate([router_offset, adjuster_offset])[:, None])
+        vec = jnp.stack(
+            [attending_offset, later_layernorm_scale, later_layernorm_shift, narrowing_offset]
+        )
+        (d_narrow, d_wide, d_ph, do_all, dx1, small, gates, corr) = mid(
+            tile_vectors,
+            o_own.reshape(tp_size * nh, rows_dev),
+            dots,
+            off_all,
+            vec,
+            hw,
+            hb,
+            row_scale[None, None],
             [
-                jnp.sum(specialist_outlooks[e].astype(F32) * slope, axis=1)
-                for e in range(EXPERTS)
-            ]
+                attending_matrix, proj_all, widening_matrix, wide_all,
+                narrowing_matrix, narrow_all,
+            ],
+            mesh,
+            heads,
         )
-        slope_sum = jnp.sum(slope, axis=1)
-
-        o_flat = o_heads.reshape(heads * HD, rows_frame)
-        ob = [o_flat[:, p * rows_dev : (p + 1) * rows_dev] for p in range(tp_size)]
-        o_own = jnp.concatenate([ob[0], core(ob[1]), across(ob[2]), diag(ob[3])], axis=0)
-        proj_cat = jnp.concatenate(proj_all, axis=0)
-        x1 = residual + dot(o_own, proj_cat, ((0,), (0,))) + attending_offset
-        hat2, rstd2 = norm_parts(x1)
-        c_low = (hat2 * later_layernorm_scale + later_layernorm_shift).astype(BF16)
-        acts, slopes = [], []
-        for p in range(tp_size):
-            m, d = gelu_parts(dot(c_low, wide_all[p]) + off_all[p])
-            acts.append(m.astype(BF16))
-            slopes.append(d)
-        mlp = dot(acts[0], narrow_all[0])
-        for p in range(1, tp_size):
-            mlp = mlp + dot(acts[p], narrow_all[p])
-        x2 = x1 + mlp + narrowing_offset
-        h_low = x2.astype(BF16)
-        logits = dot(router_matrix, h_low, ((0,), (1,))) + router_offset[:, None]
-        corr = (dot(adjuster_matrix, h_low, ((0,), (1,))) + adjuster_offset[:, None]) * row_scale
-        logits = logits.reshape(EXPERTS, fields, rows_dev)
-        top = jnp.max(logits, axis=0, keepdims=True)
-        raised = jnp.exp(logits - top)
-        gates = raised / jnp.sum(raised, axis=0, keepdims=True)
-        mixed = jnp.sum(gates * expert_dot, axis=0, keepdims=True)
-        dlog = (gates * (expert_dot - mixed)).astype(BF16).reshape(EXPERTS * fields, rows_dev)
-        dcorr = (slope_sum * row_scale).astype(BF16)
-
-        head_grads = jnp.concatenate([dlog, dcorr], axis=0)
-        head_w = jnp.concatenate([router_matrix, adjuster_matrix], axis=1)
-        dx2 = dot(head_grads, head_w, ((0,), (1,)))
-        dz = dx2.astype(BF16)
-        d_narrow = [dot(acts[p], dz, ((0,), (0,))).astype(BF16) for p in range(tp_size)]
-        dus = [
-            (dot(dz, narrow_all[p], ((1,), (1,))) * slopes[p]).astype(BF16) for p in range(tp_size)
-        ]
-        d_wide = [dot(c_low, dus[p], ((0,), (0,))).astype(BF16) for p in range(tp_size)]
-        dc = dot(dus[0], wide_all[0], ((1,), (1,)))
-        for p in range(1, tp_size):
-            dc = dc + dot(dus[p], wide_all[p], ((1,), (1,)))
-        dx1 = dx2 + norm_back(hat2, rstd2, later_layernorm_scale, dc)
-        dy = dx1.astype(BF16)
-        do_all = dot(proj_cat, dy, ((1,), (1,))).astype(BF16)
-        nh = heads * HD
-        do_all = do_all.reshape(tp_size, heads, HD, rows_dev)
+        gates = gates[:, :fields]
+        corr = corr[:fields]
+
         blended = (corr)[:, None, :]
         for e in range(EXPERTS):
             blended = blended + gates[e][:, None, :] * specialist_outlooks[e].astype(F32)
 
-        d_proj = dot(o_own, dy, ((1,), (0,))).astype(BF16)
-        d_head = dot(head_grads, h_low).astype(BF16)
-        d_head = jnp.pad(d_head, ((0, tp_size * HEAD_ROWS - d_head.shape[0]), (0, 0)))
-        dproj_parts = []
-        ph_rows = -(-(nh + HEAD_ROWS) // 128) * 128
-        for p in range(tp_size):
-            head_blk = lax.dynamic_slice_in_dim(d_head, (tp_index ^ p) * HEAD_ROWS, HEAD_ROWS, 0)
-            dproj_parts.append(
-                jnp.concatenate(
-                    [
-                        d_proj[p * nh : (p + 1) * nh],
-                        head_blk,
-                        jnp.zeros((ph_rows - nh - HEAD_ROWS, width), BF16),
-                    ],
-                    axis=0,
-                )
-            )
-
-        head_bias = jnp.sum(head_grads.astype(F32), axis=1)
-        head_bias = jnp.pad(head_bias, (0, width - head_bias.shape[0]))
-        zero = jnp.zeros((width,), F32)
-        small = jnp.stack(
-            [
-                jnp.sum(dx2, axis=0),
-                jnp.sum(dc * hat2, axis=0),
-                jnp.sum(dc, axis=0),
-                jnp.sum(dx1, axis=0),
-                head_bias,
-                zero,
-                zero,
-                zero,
-            ]
-            + [jnp.sum(dus[p].astype(F32), axis=0) for p in range(tp_size)]
-            + [zero] * 4
-        )
         leads = horizon_vectors.shape[0]
         onehot = (jnp.arange(leads, dtype=jnp.int32) == lead).astype(F32)[:, None]
-        w_t = jnp.transpose(triple_head_matrix, (0, 2, 1)).reshape(3 * nh, width)
         (token_part, small, table, head_sum, n0, n1, i0, i1, ph, q0, q1) = attn_bwd(
-            qkv, o_heads, lse, do_all, attn_rows, w_t, tile_vectors,
+            qkv, o_heads, lse, do_all, attn_rows.reshape(rows_frame, width), w_t.reshape(3 * nh, width), tile_vectors,
             early_layernorm_scale[None, :], onehot, small,
-            [d_narrow, d_wide, dproj_parts], mesh, scale_val,
+            [d_narrow, d_wide, d_ph], mesh, scale_val,
         )
         tokens_grad = dx1 + token_part
         narrow_sum = jnp.concatenate([n0, n1], axis=0).astype(F32)
         wide_sum = jnp.concatenate([i0, i1], axis=0).astype(F32)
         proj_weight_grad = ph[:nh].astype(F32)
-        head_sum = head_sum.T.astype(F32)
-        gate_weight_grad = head_sum[:, : EXPERTS * fields]
-        correct_weight_grad = head_sum[:, EXPERTS * fields : (EXPERTS + 1) * fields]
+        head_sum = head_sum.reshape(EXPERTS + 1, HEAD_ROWS, width)[:, :fields]
+        gate_weight_grad = head_sum[:EXPERTS].reshape(EXPERTS * fields, width).T.astype(F32)
+        correct_weight_grad = head_sum[EXPERTS].T.astype(F32)
+        head_bias = small[4, : (EXPERTS + 1) * HEAD_ROWS].reshape(EXPERTS + 1, HEAD_ROWS)
+        head_bias = head_bias[:, :fields]
         q_all = jnp.concatenate([q0, q1], axis=0)[: 3 * nh]
         qkv_sum = jnp.transpose(q_all.reshape(3, nh, width), (0, 2, 1)).astype(F32)
         in_bias_grad = small[8]
@@ -842,9 +1164,9 @@
             narrow_sum,
             small[0],
             gate_weight_grad,
-            small[4, : EXPERTS * fields],
+            head_bias[:EXPERTS].reshape(EXPERTS * fields),
             correct_weight_grad,
-            small[4, EXPERTS * fields : (EXPERTS + 1) * fields],
+            head_bias[EXPERTS],
         )
 
     return body

time: 370 us -> 301 us (0.81)
  Pallas kernels: 171 us -> 251 us
  waiting for transfers between devices: 56.4 us -> 0.01 us
  matrix products: 50.7 us -> 0 us
  other arithmetic: 43.4 us -> 24.3 us
  local copies, waits for them, and re-layouts: 25.7 us -> 14.4 us
  starting transfers between devices: 12.4 us -> 3.38 us
    pallas_call x1 -> x2, Pallas kernels: 25 us -> 106 us  [the longest x1 73.9 us: attn_fwd(): pl.pallas_call(functools.partial(fwd_kernel, scale=scale, dp_size=dp_size...]
    ppermute x21 -> x3, waiting for transfers between devices: 56.4 us -> 0.01 us  [swap(): return lax.ppermute(x, axis, [(i, i ^ bit) for i in range(size)])]
    dot_general x32 -> x0, matrix products: 50.7 us -> none  [the longest x31 47 us: dot(): return lax.dot_general(a, b, (dims, ((), ())), preferred_element_type=F32)]
    reduce_sum x8 -> x0, other arithmetic: 17.1 us -> none  [the longest x1 9.98 us: body(): jnp.sum(specialist_outlooks[e].astype(F32) * slope, axis=1)]
    ppermute x21 -> x3, starting transfers between devices: 12.4 us -> 3.38 us  [swap(): return lax.ppermute(x, axis, [(i, i ^ bit) for i in range(size)])]
    unnamed x162 -> x22, local copies, waits for them, and re-layouts: 6.69 us -> 0.84 us
    concatenate x5 -> x1, other arithmetic: 5.41 us -> 0.07 us  [body(): hb = head_pad(jnp.concatenate([router_offset, adjuster_offset])[:, None])]
    sub x3 -> x0, local copies, waits for them, and re-layouts: 4.36 us -> none  [the longest x2 3.55 us: body(): raised = jnp.exp(logits - top)]
  transfers between devices with their start and end apart: 21 -> 3, of which waited for: 9 -> 0; matrix products, arithmetic and copies ran while one was open for 9% -> 3% of each run, Pallas kernels for 7% -> 25%
where the time goes in v3:
time: 301 us; the launch traced here: 295 us
  Pallas kernels  251 us (83%)
  other arithmetic  24.3 us (8%)
  local copies, waits for them, and re-layouts  14.4 us (5%)
  starting transfers between devices  3.38 us (1%)
    pallas_call x1, Pallas kernels, attn_bwd(): pl.pallas_call(functools.partial(bwd_kernel, scale=scale, chunks=chunks,...  145 us
    pallas_call x1, Pallas kernels, attn_fwd(): pl.pallas_call(functools.partial(fwd_kernel, scale=scale, dp_size=dp_size...  73.9 us
    pallas_call x1, Pallas kernels, mid(): pl.pallas_call(functools.partial(mid_kernel, tp_size=tp_size, heads=heads...  31.8 us
    add x1, other arithmetic, body(): blended + gates[e][:, None, :] * specialist_outlooks[e].astype(F32)  9.03 us
  transfers between devices with their start and end apart: 3, of which 0 were waited for; matrix products, arithmetic and copies ran while one was open for 3% of the time, Pallas kernels for 25%

profile of v3, /device:TPU:0, one launch (start us, length us, event | category | flops | bytes accessed | tf_op | source)
XLA Modules:
  0.0 295.5 jit_solution(14046567515604420523)
XLA Ops:
  0.7 3.0 %collective-permute-start.1 = (f32[768]{0:T(1024)}, f32[768]{0:T(1024)S(1)}, u32[]{:S(2)}, u32[]{:S(2)}) collective-permute-start(f32[768]{0:T(1024)} %param.34), channel_id=1, source_target_pairs={{0,2},{1,3},{2,0},{3,1},{4,6},{5,7},{6,4},{7,5},{8,10},{9,11},{10,... | collective-permute-start | bytes 9224 | tf_op jit(solution)/shard_map/ppermute | solution.py:1037
  3.7 0.0 collective-permute-start
  4.3 1.3 broadcast_in_dim.4.gain_ref
  5.6 0.7 stack.35
  6.3 0.7 stack.36
  7.0 0.7 stack.37
  7.7 0.7 stack.38
  8.3 0.6 fusion.3.onehot_ref
  9.0 1.1 maximum_bitcast_fusion
  10.0 1.3 dynamic-slice_add_fusion.shift_ref
  11.4 0.0 copy-start.8
  11.4 0.0 copy-start.9
  11.4 0.0 copy-start.7
  11.4 0.0 copy-start.10
  11.4 73.9 %attn_fwd.1 = (bf16[4,512,768]{2,1,0:T(8,128)(2,1)}, bf16[3,3,64,2048]{3,2,1,0:T(8,128)(2,1)}, bf16[4,3,64,512]{3,2,1,0:T(8,128)(2,1)}, f32[4,3,1,512]{3,2,1,0:T...) custom-call(bf16[512,768]{1,0:T(8,128)(2,1)} %tiles_ref.5, ...), custom_call_target="tpu_custom_call" | custom-call | flops 30000001024 | bytes 41943040 | tf_op jit(solution)/shard_map/attn_fwd/pallas_call | solution.py:249
  85.3 0.6 pad_maximum_fusion.2.vec_ref
  85.9 0.0 collective-permute-done.1
  85.9 0.4 collective-permute-start.2
  86.2 0.0 copy-done.8
  86.3 0.0 copy-done.9
  86.3 0.1 pad_maximum_fusion.3
  86.3 0.0 copy-done.7
  86.3 0.0 copy-done.10
  86.3 0.6 dynamic_slice.7
  87.6 0.1 reshape.89
  87.8 0.1 reshape_broadcast_in_dim.3
  87.8 0.8 reshape.102.hb_ref
  88.7 0.8 pad.8
  89.5 0.0 collective-permute-done
  89.5 0.0 collective-permute-done.2
  89.5 0.6 pad_maximum_fusion.1.off_ref
  90.1 31.8 %mid.1 = (bf16[4,768,768]{2,1,0:T(8,128)(2,1)}, bf16[4,768,768]{2,1,0:T(8,128)(2,1)}, bf16[4,384,768]{2,1,0:T(8,128)(2,1)}, bf16[4,3,64,512]{3,2,1,0:T(8,128)(2,...) custom-call(bf16[512,768]{1,0:T(8,128)(2,1)} %tiles_ref.5, ...), custom_call_target="tpu_custom_call" | custom-call | flops 17999998976 | bytes 31457280 | tf_op jit(solution)/shard_map/mid/pallas_call | solution.py:958
  122.0 145.3 %attn_bwd.1 = (f32[512,768]{1,0:T(8,128)}, f32[16,768]{1,0:T(8,128)}, f32[48,768]{1,0:T(8,128)}, bf16[320,768]{1,0:T(8,128)(2,1)}, bf16[384,768]{1,0:T(8,128)(2,...) custom-call(bf16[3,3,64,2048]{3,2,1,0:T(8,128)(2,1)} %get-tuple-elem, ...), custom_call_target="tpu_custom_call" | custom-call | flops 60000002048 | bytes 31457280 | tf_op jit(solution)/shard_map/attn_bwd/pallas_call | solution.py:808
  267.3 1.0 slice_convert_fusion
  268.3 1.6 convert_bitcast_fusion.1
  269.9 1.6 slice.85
  271.4 1.6 slice_reduce_fusion
  273.0 0.7 slice_reduce_fusion.7
  273.7 1.2 pad_maximum_fusion
  274.9 0.0 copy-start.6
  275.0 0.0 copy-start
  275.0 1.4 convert_bitcast_fusion
  276.3 0.9 reshape.100
  277.2 0.0 copy-start.1
  277.2 1.9 slice_convert_fusion.1
  279.2 0.1 reshape_squeeze.3
  279.2 0.5 slice_bitcast_fusion.4
  279.8 0.6 reshape.95
  280.4 1.1 slice_bitcast_fusion.2
  281.5 0.0 copy-done.6
  281.5 0.0 copy-done
  281.5 0.0 copy-done.1
  281.5 0.0 copy-start.2
  281.5 0.0 copy-start.3
  281.6 0.0 copy-start.4
  281.6 0.0 copy-start.5
  281.6 1.3 add.34
  282.9 0.0 copy-done.2
  282.9 0.2 copy-done.3
  283.1 0.5 copy-done.4
  283.5 0.2 copy-done.5
  283.7 2.5 maximum_convert_fusion
  286.3 9.0 %fusion = f32[69,64,512]{2,1,0:T(8,128)} fusion(bf16[3,69,64,512]{3,2,1,0:T(8,128)(2,1)} %exp_ref.1, f32[69,512]{1,0:T(8,128)S(1)} %get-tuple-element.82, f32[69,512]{1,0:T(8,128)S(1)} %get-tuple-element.83, f32[69,512]{1,0:T(8,128)S(1)} %get-tuple-element.81, f32[69,512]{1,0:T(8,128)S(1)} %slice.76), kind=kLoop, calls=%fused_computation.1 | loop fusion | flops 20348928 | bytes 23175168 | tf_op jit(solution)/shard_map/add | solution.py:1129
  (6 shorter events, 0.0 us)
Async XLA Ops:
  0.7 85.2 %collective-permute-start.1 = (f32[768]{0:T(1024)}, f32[768]{0:T(1024)S(1)}, u32[]{:S(2)}, u32[]{:S(2)}) collective-permute-start(f32[768]{0:T(1024)} %param.34), channel_id=1, source_target_pairs={{0,2},{1,3},{2,0},{3,1},{4,6},{5,7},{6,4},{7,5},{8,10},{9,11},{10,... | collective-permute-start | bytes 9224 | tf_op jit(solution)/shard_map/ppermute | solution.py:1037
  3.7 85.8 %collective-permute-start = (f32[768]{0:T(1024)}, f32[768]{0:T(1024)S(1)}, u32[]{:S(2)}, u32[]{:S(2)}) collective-permute-start(f32[768]{0:T(1024)} %param.34), channel_id=1, source_target_pairs={{0,1},{1,0},{2,3},{3,2},{4,5},{5,4},{6,7},{7,6},{8,9},{9,8},{10,11... | collective-permute-start | bytes 9224 | tf_op jit(solution)/shard_map/ppermute | solution.py:1037
  11.4 74.9 %copy-start.8 = (f32[207]{0:T(256)S(1)}, f32[207]{0:T(256)}, u32[]{:S(2)}) copy-start(f32[207]{0:T(256)} %param.38) | copy-start | bytes 2488
  11.4 74.9 %copy-start.9 = (f32[69]{0:T(128)S(1)}, f32[69]{0:T(128)}, u32[]{:S(2)}) copy-start(f32[69]{0:T(128)} %param.40) | copy-start | bytes 832
  11.4 75.0 %copy-start.7 = (f32[768]{0:T(1024)S(1)}, f32[768]{0:T(1024)}, u32[]{:S(2)}) copy-start(f32[768]{0:T(1024)} %param.34) | copy-start | bytes 9220
  11.4 75.0 %copy-start.10 = (s32[40]{0:T(128)S(1)}, s32[40]{0:T(128)}, u32[]{:S(2)}) copy-start(s32[40]{0:T(128)} %param.23) | copy-start | bytes 484
  85.9 3.6 %collective-permute-start.2 = (f32[768]{0:T(1024)S(1)}, f32[768]{0:T(1024)S(1)}, u32[]{:S(2)}, u32[]{:S(2)}) collective-permute-start(f32[768]{0:T(1024)S(1)} %collective-permute-done.1), channel_id=1, source_target_pairs={{0,1},{1,0},{2,3},{3,2},{4,5},{5,4},{6,7},{7,6},{8,9},{9,8},{10,11... | collective-permute-start | bytes 9224 | tf_op jit(solution)/shard_map/ppermute | solution.py:1037
  274.9 6.5 %copy-start.6 = (f32[80,512]{1,0:T(8,128)S(1)}, f32[80,512]{1,0:T(8,128)}, u32[]{:S(2)}) copy-start(f32[80,512]{1,0:T(8,128)} %get-tuple-element.51) | copy-start | bytes 491524
  275.0 6.6 %copy-start = (f32[512,768]{1,0:T(8,128)S(1)}, f32[512,768]{1,0:T(8,128)}, u32[]{:S(2)}) copy-start(f32[512,768]{1,0:T(8,128)} %get-tuple-element.53) | copy-start | bytes 4718596
  277.2 4.3 %copy-start.1 = (f32[512,768]{1,0:T(8,128)S(1)}, f32[512,768]{1,0:T(8,128)}, u32[]{:S(2)}) copy-start(f32[512,768]{1,0:T(8,128)} %get-tuple-element.63) | copy-start | bytes 4718596
  281.5 1.4 copy-start.2
  281.5 1.5 copy-start.3
  281.6 2.0 copy-start.4
  281.6 2.1 copy-start.5

commit v4 on v3

--- a/solution.py
+++ b/solution.py
@@ -18,10 +18,15 @@
     return lax.dot_general(a, b, (dims, ((), ())), preferred_element_type=F32)
 
 
+def row_of(ref):
+    return ref[...].reshape(1, ref.shape[0])
+
+
 def fwd_kernel(
-    tiles_ref, gain_ref, shift_ref, wt_ref, proj_ref, wide_ref, narrow_ref, exp_ref, slope_ref,
-    rows_out, qkv_ref, o_ref, lse_ref, own_out, dots_ref, proj_all, wide_all, narrow_all,
-    rows_ref, own_ref, out_sem, ks, stream, stream_g, stream_sem, row_send, row_recv, o_send, o_recv, o_local,
+    lead_ref, tiles_ref, gain_ref, shift_ref, table_ref, off_ref, wt_ref, proj_ref, wide_ref,
+    narrow_ref, exp_ref, slope_ref,
+    rows_out, qkv_ref, o_ref, lse_ref, own_out, dots_ref, off_out, proj_all, wide_all, narrow_all,
+    offs, off_send, off_recv, rows_ref, own_ref, out_sem, ks, stream, stream_g, stream_sem, row_send, row_recv, o_send, o_recv, o_local,
     w_send, w_recv, *, scale, dp_size, tp_size, heads
 ):
     i, h = pl.program_id(0), pl.program_id(1)
@@ -46,6 +51,9 @@
             rows_ref.at[a, here], rows_ref.at[b, here],
             row_send.at[kind, c], row_recv.at[kind, c], "tp", bit,
         )
+
+    def off_copy(m):
+        return remote(offs.at[0], offs.at[m], off_send.at[m], off_recv.at[m], "tp", m)
 
     parts = []
     for src, dst, cuts in ((proj_ref, proj_all, 1), (wide_ref, wide_all, 2), (narrow_ref, narrow_all, 2)):
@@ -117,11 +125,14 @@
             for cp in stream_copies(g):
                 cp.start()
         blk = 64
+        gain = row_of(gain_ref)
+        shift = row_of(shift_ref) + table_ref[pl.ds(lead_ref[0], 1)]
+        offs[0, 0:1] = row_of(off_ref)
 
         def norm_rows(r, carry):
             here = pl.ds(pl.multiple_of(r * blk, blk), blk)
             hat, _ = norm_parts(tiles_ref[here].astype(F32))
-            rows_ref[0, here] = (hat * gain_ref[...] + shift_ref[...]).astype(BF16)
+            rows_ref[0, here] = (hat * gain + shift).astype(BF16)
             return carry
 
         half = piece // blk
@@ -132,6 +143,8 @@
         row_copy(1, 1).start()
         row_copy(0, 0).start()
         row_copy(0, 1).start()
+        for m in range(1, tp_size):
+            off_copy(m).start()
 
         def contract(g, carry):
             @pl.when(g + depth - 1 < groups)
@@ -226,6 +239,9 @@
     def _():
         for k in range(tp_size):
             o_copy(k).wait()
+        for m in range(1, tp_size):
+            off_copy(m).wait()
+        off_out[...] = offs[...]
         own_copy = pltpu.make_async_copy(own_ref, own_out, out_sem.at[1])
         own_copy.start()
         for n in range(len(parts)):
@@ -236,7 +252,9 @@
         pltpu.make_async_copy(rows_ref, rows_out, out_sem.at[0]).wait()
 
 
-def attn_fwd(tiles, gain, shift, wt, proj, wide, narrow, experts, slope, mesh, scale):
+def attn_fwd(
+    lead, tiles, gain, shift, table, off, wt, proj, wide, narrow, experts, slope, mesh, scale
+):
     rows_dev, width = tiles.shape
     heads = proj.shape[0] // HD
     tp_size, dp_size = mesh.shape["tp"], mesh.shape["dp"]
@@ -251,8 +269,8 @@
             fwd_kernel, scale=scale, dp_size=dp_size, tp_size=tp_size, heads=heads
         ),
         grid=(tp_size, heads),
-        in_specs=[vmem] * 4 + [any_spec] * 5,
-        out_specs=[any_spec] + [vmem] * 3 + [any_spec, vmem] + [any_spec] * 3,
+        in_specs=[pl.BlockSpec(memory_space=pltpu.SMEM)] + [vmem] * 6 + [any_spec] * 5,
+        out_specs=[any_spec] + [vmem] * 3 + [any_spec, vmem, vmem] + [any_spec] * 3,
         out_shape=[
             jax.ShapeDtypeStruct((tp_size, rows_dev, width), BF16),
             jax.ShapeDtypeStruct((3, heads, HD, frame), BF16),
@@ -260,11 +278,15 @@
             jax.ShapeDtypeStruct((tp_size, heads, 1, rows_dev), F32),
             jax.ShapeDtypeStruct((tp_size, heads, HD, rows_dev), BF16),
             jax.ShapeDtypeStruct((EXPERTS + 1, HEAD_ROWS, rows_dev), F32),
+            jax.ShapeDtypeStruct((tp_size, 8, width), F32),
             jax.ShapeDtypeStruct((tp_size - 1,) + proj.shape, BF16),
             jax.ShapeDtypeStruct((tp_size - 1,) + wide.shape, BF16),
             jax.ShapeDtypeStruct((tp_size - 1,) + narrow.shape, BF16),
         ],
         scratch_shapes=[
+            pltpu.VMEM((tp_size, 8, width), F32),
+            pltpu.SemaphoreType.DMA((tp_size,)),
+            pltpu.SemaphoreType.DMA((tp_size,)),
             pltpu.VMEM((tp_size, rows_dev, width), BF16),
             pltpu.VMEM((tp_size, heads, HD, rows_dev), BF16),
             pltpu.SemaphoreType.DMA((2,)),
@@ -287,7 +309,7 @@
             flops=30_000_000_000, bytes_accessed=40 << 20, transcendentals=heads * frame * frame
         ),
         name="attn_fwd",
-    )(tiles, gain, shift, wt, proj, wide, narrow, experts, slope)
+    )(lead, tiles, gain, shift, table, off, wt, proj, wide, narrow, experts, slope)
 
 
 def partner(index, bit):
@@ -318,26 +340,26 @@
     n_src = sum(1 for c in chunks if c["tp"] and c["part"] == 0)
     srcs = rest[:n_src]
     tok_ref, sum_ref, last_ref, head_ref = rest[n_src : n_src + 4]
-    n_out = n_src + 4 + len(chunks)
+    n_out = n_src + 4 + 4
     outs = rest[n_src + 4 : n_out]
     (
         ks, vs, dks, dvs, dos, dqkv, da_far, da_core, da_across,
-        small_in, small_got, last_own, last_got, hg,
+        small_in, small_got, last_tp, last_dp, hg,
     ) = rest[n_out : n_out + 14]
     per = rest[n_out + 14 : -12]
     (
         send_sems, recv_sems, local_sems, do_send, do_recv, do_local, da_send, da_recv,
         vec_send, vec_recv, hg_send, hg_recv,
     ) = rest[-12:]
-    i, h = pl.program_id(0), pl.program_id(1)
+    h, i = pl.program_id(0), pl.program_id(1)
     steps = tp_size * heads
-    step = i * heads + h
+    step = h * tp_size + i
     dpi, tpi = lax.axis_index("dp"), lax.axis_index("tp")
     rows_dev = dos.shape[3]
     bits = [1 << b for b in range(dp_size.bit_length() - 1)]
 
     def remote(src, dst, ssem, rsem, axis, bit):
-        dev = (partner(dpi, bit), tpi) if axis == "dp" else (dpi, partner_any(tpi, bit))
+        dev = (partner_any(dpi, bit), tpi) if axis == "dp" else (dpi, partner_any(tpi, bit))
         return pltpu.make_async_remote_copy(
             src_ref=src, dst_ref=dst, send_sem=ssem, recv_sem=rsem,
             device_id=dev, device_id_type=pl.DeviceIdType.MESH,
@@ -484,13 +506,35 @@
                 self.start(s)
             else:
                 self.out_copy().start()
+                if self.c.get("head"):
+                    head_start(self)
 
         def out_copy(self):
-            return pltpu.make_async_copy(self.fin, outs[self.k], local_sems.at[self.k, 2])
+            return pltpu.make_async_copy(
+                self.fin, outs[self.c["out"][0]].at[pl.ds(self.c["out"][1], self.rows)],
+                local_sems.at[self.k, 2],
+            )
 
         @property
         def n(self):
             return len(self.stages)
+
+    head_nh, hr = [c["head"] for c in chunks if c.get("head")][0]
+    head_chunk = []
+
+    def head_remote(ch, p):
+        mine = ch.fin.at[pl.ds(head_nh, hr)]
+        return remote(mine, hg.at[p - 1], hg_send.at[p - 1], hg_recv.at[p - 1], "tp", p)
+
+    def head_local(ch):
+        mine = ch.fin.at[pl.ds(head_nh, hr)]
+        return pltpu.make_async_copy(mine, rows_at(head_ref, tpi * hr, hr), local_sems.at[0, 3])
+
+    def head_start(ch):
+        head_chunk.append(ch)
+        for p in range(1, tp_size):
+            head_remote(ch, p).start()
+        head_local(ch).start()
 
     work, at = [], 0
     for k, c in enumerate(chunks):
@@ -541,31 +585,31 @@
     @pl.when(step == 0)
     def _():
         barrier = pltpu.get_barrier_semaphore()
-        others = [("tp", 1), ("tp", 2), ("tp", 3)] + [("dp", b) for b in bits]
+        others = [("tp", m) for m in range(1, tp_size)] + [("dp", m) for m in range(1, dp_size)]
         for axis, bit in others:
-            dev = (partner(dpi, bit), tpi) if axis == "dp" else (dpi, partner_any(tpi, bit))
+            dev = (partner_any(dpi, bit), tpi) if axis == "dp" else (dpi, partner_any(tpi, bit))
             pl.semaphore_signal(
                 barrier, inc=1, device_id=dev, device_id_type=pl.DeviceIdType.MESH
             )
         pl.semaphore_wait(barrier, len(others))
         for p in (2, 3, 1, 0):
             do_copy(p).start()
-        for k in range(len(work)):
-            if chunks[k]["tp"]:
-                work[k].event(0)
+        turn(PLAN_FIRST)
         small_in[...] = small_ref[...]
         small_event(0)
-        for hh in range(heads):
-            ks[hh] = qkv_ref[1, hh].T
-            vs[hh] = qkv_ref[2, hh].T
+
+    for p in range(tp_size):
+
+        @pl.when(step == p)
+        def _():
+            do_copy(p).wait()
+
+    @pl.when(i == 0)
+    def _():
+        ks[...] = qkv_ref[1, h].T
+        vs[...] = qkv_ref[2, h].T
         dks[...] = jnp.zeros_like(dks)
         dvs[...] = jnp.zeros_like(dvs)
-
-    for p in range(tp_size):
-
-        @pl.when(step == p * heads)
-        def _():
-            do_copy(p).wait()
 
     lanes = pl.ds(pl.multiple_of(i * rows_dev, rows_dev), rows_dev)
     qt = qkv_ref[0, h, :, lanes] * jnp.bfloat16(scale)
@@ -573,22 +617,47 @@
     dsum = jnp.sum(
         dot_t.astype(F32) * o_ref[i, h].astype(F32), axis=0, keepdims=True
     )
-    s = dot(ks[h], qt)
+    s = dot(ks[...], qt)
     p = jnp.exp(s - lse_ref[i, h])
-    dp = dot(vs[h], dot_t)
+    dp = dot(vs[...], dot_t)
     ds = (p * (dp - dsum)).astype(BF16)
     dqkv[0, h, :, lanes] = (dot(qkv_ref[1, h], ds) * scale).astype(BF16)
-    dvs[h] += dot(p.astype(BF16), dot_t.T)
-    dks[h] += dot(ds, qt.T)
-
-    n_tp = [k for k in range(len(work)) if chunks[k]["tp"]]
-    for k in n_tp:
-        done[k] = 1
+    dvs[...] += dot(p.astype(BF16), dot_t.T)
+    dks[...] += dot(ds, qt.T)
+
+    @pl.when(i == tp_size - 1)
+    def _():
+        dqkv[1, h] = dks[...].astype(BF16).T
+        dqkv[2, h] = dvs[...].astype(BF16).T
+
+    qk = 3 * HD
+    due = {}
+    spot = 0
+    for k in range(len(work)):
+        if not chunks[k]["tp"]:
+            n = min(chunks[k]["rows"] // qk, heads - spot)
+            due[k] = (spot, n)
+            spot += n
+
+    def weight_grad(k):
+        first, n = due[k]
+        for sec in range(3):
+            lhs = dqkv[sec, first : first + n].reshape(n * HD, tp_size * rows_dev)
+            work[k].acc[sec * n * HD : (sec + 1) * n * HD] = dot(lhs, rows_ref[...]).astype(BF16)
+        spare = chunks[k]["rows"] - n * qk
+        if spare:
+            work[k].acc[n * qk :] = jnp.zeros((spare, width), BF16)
+        go(k)
+
+    early = [k for k in due if sum(due[k]) < heads]
     small_done = [1]
     for st in range(steps):
 
         @pl.when(step == st)
         def _():
+            for k in early:
+                if st == sum(due[k]) * tp_size - 1:
+                    weight_grad(k)
             if st < len(PLAN_STEPS):
                 turn(PLAN_STEPS[st])
             if small_done[0] <= len(ladder):
@@ -597,10 +666,6 @@
 
     @pl.when(step == steps - 1)
     def _():
-        for hh in range(heads):
-            dqkv[1, hh] = dks[hh].astype(BF16).T
-            dqkv[2, hh] = dvs[hh].astype(BF16).T
-
         blk = 128
 
         def da_rows(p, store):
@@ -636,17 +701,9 @@
         da_rows(2, store2)
         far.start()
         turn(PLAN_TAIL[2])
-        kq = [k for k in range(len(work)) if not chunks[k]["tp"]]
-        nh = heads * HD
-        spots = [(k, r) for k in kq for r in range(0, chunks[k]["rows"], nh)]
-        for sec in range(3):
-            k, r = spots[sec]
-            lhs = dqkv[sec].reshape(nh, tp_size * rows_dev)
-            work[k].acc[r : r + nh] = dot(lhs, rows_ref[...]).astype(BF16)
-        k, r = spots[2]
-        rest_rows = chunks[k]["rows"] - r - nh
-        work[k].acc[r + nh :] = jnp.zeros((rest_rows, width), BF16)
-        turn(kq)
+        for k in due:
+            if k not in early:
+                weight_grad(k)
         turn(PLAN_TAIL[3])
         core1.wait()
 
@@ -657,70 +714,62 @@
         turn(PLAN_TAIL[4])
         turn(PLAN_WAIT)
         far.wait()
-        last_own[...] = jnp.zeros_like(last_own)
+        last_tp[tpi] = jnp.zeros((8, width), F32)
 
         def norm_rows(r, carry):
             here = pl.ds(pl.multiple_of(r * blk, blk), blk)
             da = tok_ref[here] + da_across[here].astype(F32)
             hat, rstd = norm_parts(tiles_ref[here].astype(F32))
-            tok_ref[here] = norm_back(hat, rstd, gain_ref[...], da)
-            last_own[0:1] += jnp.sum(da * hat, axis=0, keepdims=True)
-            last_own[1:2] += jnp.sum(da, axis=0, keepdims=True)
+            tok_ref[here] = norm_back(hat, rstd, row_of(gain_ref), da)
+            last_tp[tpi, 0:1] += jnp.sum(da * hat, axis=0, keepdims=True)
+            last_tp[tpi, 1:2] += jnp.sum(da, axis=0, keepdims=True)
             return carry
 
         lax.fori_loop(0, rows_dev // blk, norm_rows, 0)
 
-        def last_copy(s):
-            if s < 2:
-                return remote(
-                    last_own.at[pl.ds(0, 8)], last_got.at[s, pl.ds(0, 8)],
-                    vec_send.at[1, s], vec_recv.at[1, s], *ladder[s],
-                )
+        def last_copy(axis, m):
+            buf, me = (last_tp, tpi) if axis == "tp" else (last_dp, dpi)
+            at = 0 if axis == "tp" else tp_size
             return remote(
-                last_own, last_got.at[s], vec_send.at[1, s], vec_recv.at[1, s], *ladder[s]
+                buf.at[me], buf.at[me], vec_send.at[1, at + m], vec_recv.at[1, at + m], axis, m
             )
 
-        last_copy(0).start()
-        for st in range(len(ladder)):
-            if st < len(PLAN_LAST):
-                turn(PLAN_LAST[st])
-            last_copy(st).wait()
-            if st < 2:
-                last_own[0:8] += last_got[st, 0:8]
-                if st == 1:
-                    last_own[8:] = onehot_ref[...] * last_own[1:2]
-            else:
-                last_own[...] += last_got[st]
-            if st + 1 < len(ladder):
-                last_copy(st + 1).start()
+        for m in range(1, tp_size):
+            last_copy("tp", m).start()
+        turn(PLAN_LAST[0])
+        for m in range(1, tp_size):
+            last_copy("tp", m).wait()
+        total = last_tp[0]
+        for k in range(1, tp_size):
+            total = total + last_tp[k]
+        last_dp[dpi] = total
+        last_dp[dpi, 2:3] = onehot_ref[...]
+        for m in range(1, dp_size):
+            last_copy("dp", m).start()
+        turn(PLAN_LAST[1])
+        for m in range(1, dp_size):
+            last_copy("dp", m).wait()
+
+        last_ref[0:1] = jnp.sum(last_dp[:, 0, :], axis=0, keepdims=True)
+        shares = last_dp[:, 1, :]
+        last_ref[1:2] = jnp.sum(shares, axis=0, keepdims=True)
+        leads = last_ref.shape[0] - 8
+        hot = last_dp[:, 2, 0:128]
+        for k in range(leads):
+            last_ref[8 + k : 9 + k] = jnp.sum(hot[:, k : k + 1] * shares, axis=0, keepdims=True)
+        turn(PLAN_LAST[2])
         while small_done[0] <= len(ladder):
             small_event(small_done[0])
             small_done[0] += 1
-        turn(PLAN_LAST[-1])
         turn(PLAN_END)
         while any(done[k] <= work[k].n for k in range(len(work))):
             turn(range(len(work)))
-        last_ref[...] = last_own[...]
         sum_ref[...] = small_in[...]
-        kp = [k for k in n_tp if chunks[k].get("head")][0]
-        nh, hr = chunks[kp]["head"]
-        mine = work[kp].fin.at[pl.ds(nh, hr)]
-        cps = [
-            remote(mine, hg.at[p - 1], hg_send.at[p - 1], hg_recv.at[p - 1], "tp", p)
-            for p in range(1, tp_size)
-        ]
-        for cp in cps:
-            cp.start()
-        head_out = [
-            pltpu.make_async_copy(
-                mine, rows_at(head_ref, tpi * hr, hr), do_local
-            )
-        ]
-        head_out[0].start()
-        for p, cp in enumerate(cps):
-            cp.wait()
+        head_out = [head_local(head_chunk[0])]
+        for p in range(1, tp_size):
+            head_remote(head_chunk[0], p).wait()
             out = pltpu.make_async_copy(
-                hg.at[p], rows_at(head_ref, partner_any(tpi, p + 1) * hr, hr),
+                hg.at[p - 1], rows_at(head_ref, partner_any(tpi, p) * hr, hr),
                 local_sems.at[p, 3],
             )
             out.start()
@@ -732,21 +781,34 @@
 
 
 def partner_any(index, mask):
-    if mask & 1:
-        index = partner(index, 1)
-    if mask & 2:
-        index = partner(index, 2)
+    bit = 1
+    while bit <= mask:
+        if mask & bit:
+            index = partner(index, bit)
+        bit *= 2
     return index
 
 
-PLAN_STEPS = ((0, 1, 2), (3,), (4,), (), (0, 1, 2), (), (), (1,), (3, 4), (1,), (0,), (1, 2, 4))
-PLAN_TAIL = ((0,), (), (1, 2, 3, 4), (0,), (1, 3))
-PLAN_WAIT = (2, 6, 4, 5, 1)
-PLAN_LAST = ((0,), (3, 5), (2, 6), (0, 4), (2, 3, 5), (0, 4, 6))
-PLAN_END = (3, 2, 5, 4, 6, 5, 3, 6, 5, 6)
-
-
-def attn_bwd(qkv, o, lse, do, rows, wt, tiles, gain, onehot, small, parts, mesh, scale):
+PLAN_FIRST = (4, 2)
+PLAN_STEPS = ((0, 1), (4, 2, 0, 1, 3), (), (3,), (4, 2), (), (), (4,), (2, 0, 1, 4), (5, 3, 2), (4,), (2, 5),)
+PLAN_TAIL = ((), (4, 0), (), (3,), (2,),)
+PLAN_WAIT = (5, 4, 0, 6, 5, 1, 4, 3, 2, 0)
+PLAN_LAST = ((1, 6), (2, 5, 3), (6,),)
+PLAN_END = (1, 3, 0, 6, 5, 1, 0, 3, 1, 6, 3, 0, 1, 6)
+
+
+ORDERS = (
+    (2, "X", 1, 4),
+    (2, "X", 1, 4),
+    (1, "X", 2, 4),
+    ("X", 1, 2, 4),
+    ("X", 1, 2, 4),
+    (1, 2, 4),
+    (1, 4, 2),
+)
+
+
+def attn_bwd(qkv, o, lse, do, rows, wt, tiles, gain, onehot, leads, small, parts, mesh, scale):
     _, heads, _, frame = qkv.shape
     rows_dev, width = tiles.shape
     tp_size, dp_size = mesh.shape["tp"], mesh.shape["dp"]
@@ -754,20 +816,20 @@
     half = width // 2
     ph_rows = parts[2].shape[1]
     chunks = [
-        dict(tp=True, rows=half, part=0, order=[1, "X", 2, 4]),
-        dict(tp=True, rows=half, part=1, order=["X", 1, 2, 4]),
-        dict(tp=True, rows=half, part=0, order=[2, "X", 1, 4]),
-        dict(tp=True, rows=half, part=1, order=[2, "X", 1, 4]),
-        dict(tp=True, rows=ph_rows, part=0, order=["X", 1, 2, 4], head=(heads * HD, HEAD_ROWS)),
-        dict(tp=False, rows=half, order=[2, 1, 4]),
-        dict(tp=False, rows=256, order=[1, 2, 4]),
+        dict(tp=True, rows=half, part=0, order=ORDERS[0], out=(0, 0)),
+        dict(tp=True, rows=half, part=1, order=ORDERS[1], out=(0, half)),
+        dict(tp=True, rows=half, part=0, order=ORDERS[2], out=(1, 0)),
+        dict(tp=True, rows=half, part=1, order=ORDERS[3], out=(1, half)),
+        dict(tp=True, rows=ph_rows, part=0, order=ORDERS[4], out=(2, 0), head=(heads * HD, HEAD_ROWS)),
+        dict(tp=False, rows=half, order=ORDERS[5], out=(3, 0)),
+        dict(tp=False, rows=256, order=ORDERS[6], out=(3, half)),
     ]
     n_k = len(chunks)
     scratch = [
-        pltpu.VMEM((heads, frame, HD), BF16),
-        pltpu.VMEM((heads, frame, HD), BF16),
-        pltpu.VMEM((heads, frame, HD), F32),
-        pltpu.VMEM((heads, frame, HD), F32),
+        pltpu.VMEM((frame, HD), BF16),
+        pltpu.VMEM((frame, HD), BF16),
+        pltpu.VMEM((frame, HD), F32),
+        pltpu.VMEM((frame, HD), F32),
         pltpu.VMEM((tp_size, heads, HD, rows_dev), BF16),
         pltpu.VMEM((3, heads, HD, frame), BF16),
         pltpu.VMEM((3, rows_dev, width), BF16),
@@ -775,8 +837,8 @@
         pltpu.VMEM((rows_dev, width), BF16),
         pltpu.VMEM((16, width), F32),
         pltpu.VMEM((2 + nbits, 16, width), F32),
-        pltpu.VMEM((8 + onehot.shape[0], width), F32),
-        pltpu.VMEM((2 + nbits, 8 + onehot.shape[0], width), F32),
+        pltpu.VMEM((tp_size, 8, width), F32),
+        pltpu.VMEM((dp_size, 8, width), F32),
         pltpu.VMEM((tp_size - 1, HEAD_ROWS, width), BF16),
     ]
     for c in chunks:
@@ -798,8 +860,8 @@
         pltpu.SemaphoreType.DMA,
         pltpu.SemaphoreType.DMA((3,)),
         pltpu.SemaphoreType.DMA((3,)),
-        pltpu.SemaphoreType.DMA((2, 2 + nbits)),
-        pltpu.SemaphoreType.DMA((2, 2 + nbits)),
+        pltpu.SemaphoreType.DMA((2, tp_size + dp_size)),
+        pltpu.SemaphoreType.DMA((2, tp_size + dp_size)),
         pltpu.SemaphoreType.DMA((tp_size - 1,)),
         pltpu.SemaphoreType.DMA((tp_size - 1,)),
     ]
@@ -810,16 +872,19 @@
             bwd_kernel, scale=scale, chunks=chunks, dp_size=dp_size, heads=heads,
             tp_size=tp_size, width=width,
         ),
-        grid=(tp_size, heads),
+        grid=(heads, tp_size),
         in_specs=[vmem, vmem, vmem, any_spec] + [vmem] * 6 + [any_spec] * len(parts),
-        out_specs=[vmem, vmem, vmem, any_spec] + [any_spec] * n_k,
+        out_specs=[vmem, vmem, vmem, any_spec] + [any_spec] * 4,
         out_shape=[
             jax.ShapeDtypeStruct((rows_dev, width), F32),
             jax.ShapeDtypeStruct((16, width), F32),
-            jax.ShapeDtypeStruct((8 + onehot.shape[0], width), F32),
+            jax.ShapeDtypeStruct((8 + leads, width), F32),
             jax.ShapeDtypeStruct((tp_size * HEAD_ROWS, width), BF16),
         ]
-        + [jax.ShapeDtypeStruct((c["rows"], width), BF16) for c in chunks],
+        + [
+            jax.ShapeDtypeStruct((rows, width), BF16)
+            for rows in (width, width, ph_rows, half + chunks[-1]["rows"])
+        ],
         scratch_shapes=scratch,
         compiler_params=pltpu.CompilerParams(
             vmem_limit_bytes=60 << 20, collective_id=1, has_side_effects=True
@@ -832,7 +897,7 @@
 
 
 def mid_kernel(
-    tiles_ref, o_ref, dots_ref, off_ref, vec_ref, hw_ref, hb_ref, scale_ref,
+    tiles_ref, o_ref, dots_ref, off_ref, pb_ref, g2_ref, s2_ref, nb_ref, hw_ref, hb_ref, scale_ref,
     pj_own, pj_far, wi_own, wi_far, na_own, na_far,
     dn_ref, dw_ref, ph_ref, do_ref, dx1_ref, small_ref, gates_ref, corr_ref,
     pj, wi, na, x1, hat, rstd, c_low, act, slope, h_low, hg, dx2, dz, du, dc, dy, hd, dn, dw, ph, dos,
@@ -859,7 +924,7 @@
     for cp in load_pj + load_wi + load_na:
         cp.start()
     small_ref[...] = jnp.zeros_like(small_ref)
-    proj_bias, gain2, shift2, out_bias = (vec_ref[k : k + 1] for k in range(4))
+    proj_bias, gain2, shift2, out_bias = (row_of(v) for v in (pb_ref, g2_ref, s2_ref, nb_ref))
     for cp in load_pj:
         cp.wait()
     for r in blocks:
@@ -873,7 +938,7 @@
         load_wi[p].wait()
         cols = pl.ds(p * width, width)
         for r in blocks:
-            m, d = gelu_parts(dot(c_low[r], wi[p]) + off_ref[p : p + 1])
+            m, d = gelu_parts(dot(c_low[r], wi[p]) + off_ref[p, 0:1])
             act[r, cols] = m.astype(BF16)
             slope[r, cols] = d
     for cp in load_na:
@@ -946,7 +1011,7 @@
         cp.wait()
 
 
-def mid(tiles, o_own, dots, off, vec, hw, hb, row_scale, weights, mesh, heads):
+def mid(tiles, o_own, dots, off, vecs, hw, hb, row_scale, weights, mesh, heads):
     rows_dev, width = tiles.shape
     tp_size = mesh.shape["tp"]
     nh = heads * HD
@@ -957,7 +1022,7 @@
     big = (tp_size, width, width)
     return pl.pallas_call(
         functools.partial(mid_kernel, tp_size=tp_size, heads=heads),
-        in_specs=[vmem] * 8 + [any_spec] * 6,
+        in_specs=[vmem] * 11 + [any_spec] * 6,
         out_specs=[any_spec] * 4 + [vmem] * 4,
         out_shape=[
             jax.ShapeDtypeStruct(big, BF16),
@@ -999,7 +1064,79 @@
             flops=18_000_000_000, bytes_accessed=30 << 20, transcendentals=2_000_000
         ),
         name="mid",
-    )(tiles, o_own, dots, off, vec, hw, hb, row_scale, *weights)
+    )(tiles, o_own, dots, off, *vecs, hw, hb, row_scale, *weights)
+
+
+def finish_kernel(
+    n_ref, i_ref, ph_ref, qa_ref, qb_ref, hd_ref, tok_ref, dx_ref, table_ref,
+    no_ref, io_ref, po_ref, qo_ref, g_ref, c_ref, to_ref, lead_ref, *, fields
+):
+    no_ref[...] = n_ref[...].astype(F32)
+    io_ref[...] = i_ref[...].astype(F32)
+    po_ref[...] = ph_ref[...].astype(F32)
+    na = qa_ref.shape[0]
+    qo_ref[0, :na] = qa_ref[...].astype(F32)
+    qo_ref[0, na:] = qb_ref[...].astype(F32)
+    for e in range(EXPERTS):
+        g_ref[e * fields : (e + 1) * fields] = hd_ref[pl.ds(e * HEAD_ROWS, HEAD_ROWS)].astype(F32)[
+            :fields
+        ]
+    c_ref[...] = hd_ref[pl.ds(EXPERTS * HEAD_ROWS, HEAD_ROWS)].astype(F32)[:fields]
+    to_ref[...] = tok_ref[...] + dx_ref[...]
+    lead_ref[...] = table_ref[8:]
+
+
+def finish(n, i, ph, q, hd, tok, dx1, table, heads, fields):
+    width = n.shape[0]
+    nh = heads * HD
+    steps = 3
+    rows = width // steps
+    first = (width // 2) // (3 * HD) * HD
+    second = nh - first
+    base = 3 * first // second
+    tok_rows = tok.shape[0] // 2
+    leads = table.shape[0] - 8
+
+    def by_row(r):
+        return pl.BlockSpec((r, width), lambda g: (g, 0))
+
+    token = pl.BlockSpec((tok_rows, width), lambda g: (jnp.minimum(g, 1), 0))
+    return pl.pallas_call(
+        functools.partial(finish_kernel, fields=fields),
+        grid=(steps,),
+        in_specs=[
+            by_row(rows),
+            by_row(rows),
+            by_row(nh // steps),
+            by_row(first),
+            pl.BlockSpec((second, width), lambda g: (base + g, 0)),
+            pl.BlockSpec((hd.shape[0], rows), lambda g: (0, g)),
+            token,
+            token,
+            pl.BlockSpec(table.shape, lambda g: (0, 0)),
+        ],
+        out_specs=[
+            by_row(rows),
+            by_row(rows),
+            by_row(nh // steps),
+            pl.BlockSpec((1, nh, width), lambda g: (g, 0, 0)),
+            pl.BlockSpec((EXPERTS * fields, rows), lambda g: (0, g)),
+            pl.BlockSpec((fields, rows), lambda g: (0, g)),
+            token,
+            pl.BlockSpec((leads, width), lambda g: (0, 0)),
+        ],
+        out_shape=[
+            jax.ShapeDtypeStruct((width, width), F32),
+            jax.ShapeDtypeStruct((width, width), F32),
+            jax.ShapeDtypeStruct((nh, width), F32),
+            jax.ShapeDtypeStruct((3, nh, width), F32),
+            jax.ShapeDtypeStruct((EXPERTS * fields, width), F32),
+            jax.ShapeDtypeStruct((fields, width), F32),
+            jax.ShapeDtypeStruct(tok.shape, F32),
+            jax.ShapeDtypeStruct((leads, width), F32),
+        ],
+        name="finish",
+    )(n, i, ph, q, q, hd, tok, dx1, table)
 
 
 def norm_parts(values):
@@ -1030,17 +1167,7 @@
 
 
 def make_body(mesh):
-    dp_size, tp_size = mesh.shape["dp"], mesh.shape["tp"]
-
-    def swap(x, axis, bit):
-        size = dp_size if axis == "dp" else tp_size
-        return lax.ppermute(x, axis, [(i, i ^ bit) for i in range(size)])
-
-    def core(x):
-        return swap(x, "tp", 1)
-
-    def across(x):
-        return swap(x, "tp", 2)
+    tp_size = mesh.shape["tp"]
 
     def body(
         tile_vectors,
@@ -1073,16 +1200,18 @@
         scale_val = HD ** (-0.5)
         tp_index = lax.axis_index("tp")
         lead = snapshot_horizon_slot[0]
-        embed = lax.dynamic_slice_in_dim(horizon_vectors, lead, 1, 0)
         row_scale = lax.rsqrt(
             lax.dynamic_slice_in_dim(horizon_sample_tally, lead, 1, 0).astype(F32)
         )[0]
         nh = heads * HD
         w_t = jnp.transpose(triple_head_matrix, (0, 2, 1))
-        (attn_rows, qkv, o_heads, lse, o_own, dots, proj_all, wide_all, narrow_all) = attn_fwd(
+        (attn_rows, qkv, o_heads, lse, o_own, dots, off_all, proj_all, wide_all, narrow_all) = attn_fwd(
+            snapshot_horizon_slot,
             tile_vectors,
-            early_layernorm_scale[None, :],
-            early_layernorm_shift[None, :] + embed,
+            early_layernorm_scale,
+            early_layernorm_shift,
+            horizon_vectors,
+            widening_offset,
             w_t,
             attending_matrix,
             widening_matrix,
@@ -1092,8 +1221,6 @@
             mesh,
             scale_val,
         )
-        off2 = across(widening_offset)
-        off_all = jnp.stack([widening_offset, core(widening_offset), off2, core(off2)])
 
         def head_pad(x):
             x = x.reshape((EXPERTS + 1, fields) + x.shape[1:])
@@ -1102,9 +1229,7 @@
 
         hw = head_pad(jnp.concatenate([router_matrix, adjuster_matrix], axis=1).T)
         hb = head_pad(jnp.concatenate([router_offset, adjuster_offset])[:, None])
-        vec = jnp.stack(
-            [attending_offset, later_layernorm_scale, later_layernorm_shift, narrowing_offset]
-        )
+        vec = (attending_offset, later_layernorm_scale, later_layernorm_shift, narrowing_offset)
         (d_narrow, d_wide, d_ph, do_all, dx1, small, gates, corr) = mid(
             tile_vectors,
             o_own.reshape(tp_size * nh, rows_dev),
@@ -1129,23 +1254,23 @@
             blended = blended + gates[e][:, None, :] * specialist_outlooks[e].astype(F32)
 
         leads = horizon_vectors.shape[0]
-        onehot = (jnp.arange(leads, dtype=jnp.int32) == lead).astype(F32)[:, None]
-        (token_part, small, table, head_sum, n0, n1, i0, i1, ph, q0, q1) = attn_bwd(
+        onehot = (jnp.arange(width, dtype=jnp.int32) == lead).astype(F32)[None, :]
+        (token_part, small, table, head_sum, n_low, i_low, ph, q_low) = attn_bwd(
             qkv, o_heads, lse, do_all, attn_rows.reshape(rows_frame, width), w_t.reshape(3 * nh, width), tile_vectors,
-            early_layernorm_scale[None, :], onehot, small,
+            early_layernorm_scale, onehot, leads, small,
             [d_narrow, d_wide, d_ph], mesh, scale_val,
         )
-        tokens_grad = dx1 + token_part
-        narrow_sum = jnp.concatenate([n0, n1], axis=0).astype(F32)
-        wide_sum = jnp.concatenate([i0, i1], axis=0).astype(F32)
-        proj_weight_grad = ph[:nh].astype(F32)
-        head_sum = head_sum.reshape(EXPERTS + 1, HEAD_ROWS, width)[:, :fields]
-        gate_weight_grad = head_sum[:EXPERTS].reshape(EXPERTS * fields, width).T.astype(F32)
-        correct_weight_grad = head_sum[EXPERTS].T.astype(F32)
+        (
+            narrow_sum, wide_sum, proj_weight_grad, qkv_sum, gate_sum, correct_sum, tokens_grad,
+            lead_sum,
+        ) = finish(
+            n_low, i_low, ph, q_low, head_sum, token_part, dx1, table, heads, fields
+        )
+        qkv_sum = jnp.transpose(qkv_sum, (0, 2, 1))
+        gate_weight_grad = gate_sum.T
+        correct_weight_grad = correct_sum.T
         head_bias = small[4, : (EXPERTS + 1) * HEAD_ROWS].reshape(EXPERTS + 1, HEAD_ROWS)
         head_bias = head_bias[:, :fields]
-        q_all = jnp.concatenate([q0, q1], axis=0)[: 3 * nh]
-        qkv_sum = jnp.transpose(q_all.reshape(3, nh, width), (0, 2, 1)).astype(F32)
         in_bias_grad = small[8]
 
         return (
@@ -1153,7 +1278,7 @@
             tokens_grad,
             table[0],
             table[1],
-            table[8:],
+            lead_sum,
             qkv_sum,
             proj_weight_grad,
             small[3],

time: 301 us -> 275 us (0.914)
  other arithmetic: 24.3 us -> 9.74 us
  local copies, waits for them, and re-layouts: 14.4 us -> 6.11 us
  starting transfers between devices: 3.38 us -> 0 us
    convert_element_type x6 -> x1, other arithmetic: 9.06 us -> 0.59 us  [body(): onehot = (jnp.arange(width, dtype=jnp.int32) == lead).astype(F32)[None, :]]
    pallas_call x0 -> x1, Pallas kernels: none -> 6.89 us  [finish(): pl.pallas_call(functools.partial(finish_kernel, fields=fields), grid=(ste...]
    pallas_call x1, Pallas kernels: 145 us -> 139 us  [attn_bwd(): pl.pallas_call(functools.partial(bwd_kernel, scale=scale, chunks=chunks,...]
    ppermute x3 -> x0, starting transfers between devices: 3.38 us -> none  [swap(): return lax.ppermute(x, axis, [(i, i ^ bit) for i in range(size)])]
  transfers between devices with their start and end apart: 3 -> 0, of which waited for: 0 -> 0; matrix products, arithmetic and copies ran while one was open for 3% -> 0% of each run, Pallas kernels for 25% -> 0%
where the time goes in v4:
time: 275 us; the launch traced here: 271 us
  Pallas kernels  252 us (92%)
  other arithmetic  9.74 us (4%)
  local copies, waits for them, and re-layouts  6.11 us (2%)
    pallas_call x1, Pallas kernels, attn_bwd(): pl.pallas_call(functools.partial(bwd_kernel, scale=scale, chunks=chunks,...  139 us
    pallas_call x1, Pallas kernels, attn_fwd(): pl.pallas_call(functools.partial(fwd_kernel, scale=scale, dp_size=dp_size...  74.8 us
    pallas_call x1, Pallas kernels, mid(): pl.pallas_call(functools.partial(mid_kernel, tp_size=tp_size, heads=heads...  31.7 us
    add x1, other arithmetic, body(): blended + gates[e][:, None, :] * specialist_outlooks[e].astype(F32)  9.04 us
    pallas_call x1, Pallas kernels, finish(): pl.pallas_call(functools.partial(finish_kernel, fields=fields), grid=(ste...  6.89 us

profile of v4, /device:TPU:0, one launch (start us, length us, event | category | flops | bytes accessed | tf_op | source)
XLA Modules:
  0.0 270.5 jit_solution(12039959638290660347)
XLA Ops:
  1.3 0.0 copy-start.6
  1.3 0.0 copy-start.1
  1.3 0.0 copy-start.3
  1.3 0.0 copy-start.4
  1.3 0.0 copy-start.5
  1.4 74.8 %attn_fwd.1 = (bf16[4,512,768]{2,1,0:T(8,128)(2,1)}, bf16[3,3,64,2048]{3,2,1,0:T(8,128)(2,1)}, bf16[4,3,64,512]{3,2,1,0:T(8,128)(2,1)}, f32[4,3,1,512]{3,2,1,0:T...) custom-call(s32[1]{0:T(128)} %copy.40.lead_ref, ...), custom_call_target="tpu_custom_call" | custom-call | flops 30000001024 | bytes 41943040 | tf_op jit(solution)/shard_map/attn_fwd/pallas_call | solution.py:267
  76.1 0.0 copy-done.6
  76.1 0.6 dynamic_slice.3
  77.4 0.0 copy-done.1
  77.4 0.0 copy-done.3
  77.5 0.1 reshape.78
  77.6 0.8 pad.8
  78.4 0.0 copy-done.4
  78.4 0.0 copy-done.5
  78.4 0.1 pad_maximum_fusion
  78.5 0.1 reshape_broadcast_in_dim.3
  78.6 0.8 reshape.87.hb_ref
  79.4 31.7 %mid.1 = (bf16[4,768,768]{2,1,0:T(8,128)(2,1)}, bf16[4,768,768]{2,1,0:T(8,128)(2,1)}, bf16[4,384,768]{2,1,0:T(8,128)(2,1)}, bf16[4,3,64,512]{3,2,1,0:T(8,128)(2,...) custom-call(bf16[512,768]{1,0:T(8,128)(2,1)} %tiles_ref.5, ...), custom_call_target="tpu_custom_call" | custom-call | flops 17999998976 | bytes 31457280 | tf_op jit(solution)/shard_map/mid/pallas_call | solution.py:1023
  111.1 0.6 compare_convert_fusion.onehot_ref
  111.7 138.7 %attn_bwd.1 = (f32[512,768]{1,0:T(8,128)}, f32[16,768]{1,0:T(8,128)}, f32[48,768]{1,0:T(8,128)}, bf16[320,768]{1,0:T(8,128)(2,1)}, bf16[768,768]{1,0:T(8,128)(2,...) custom-call(bf16[3,3,64,2048]{3,2,1,0:T(8,128)(2,1)} %get-tuple-element.60.qkv_ref, ...), custom_call_target="tpu_custom_call" | custom-call | flops 60000002048 | bytes 31457280 | tf_op jit(solution)/shard_map/attn_bwd/pallas_call | solution.py:870
  250.4 0.0 copy-start
  250.5 1.6 slice_reduce_fusion
  252.1 0.0 copy-start.2
  252.1 6.9 %finish.1 = (f32[768,768]{1,0:T(8,128)}, f32[768,768]{1,0:T(8,128)}, f32[192,768]{1,0:T(8,128)}, f32[3,192,768]{2,1,0:T(8,128)}, f32[207,768]{1,0:T(8,128)}, /*i...) custom-call(bf16[768,768]{1,0:T(8,128)(2,1)} %get-tuple-element.69.n_ref, ...), custom_call_target="tpu_custom_call" | custom-call | tf_op jit(solution)/shard_map/finish/pallas_call | solution.py:1104
  259.0 0.7 slice_reduce_fusion.7
  259.7 0.1 reshape_squeeze.3
  259.8 0.6 reshape.83
  260.4 0.5 slice_bitcast_fusion.3
  261.0 0.0 copy-done
  261.0 0.0 copy-done.2
  261.0 9.0 %fusion = f32[69,64,512]{2,1,0:T(8,128)} fusion(bf16[3,69,64,512]{3,2,1,0:T(8,128)(2,1)} %exp_ref.1, f32[69,512]{1,0:T(8,128)S(1)} %get-tuple-element.94, f32[69,512]{1,0:T(8,128)S(1)} %get-tuple-element.95, f32[69,512]{1,0:T(8,128)S(1)} %get-tuple-element.93, f32[69,512]{1,0:T(8,128)S(1)} %slice.58), kind=kLoop, calls=%fused_computation.1 | loop fusion | flops 20348928 | bytes 23175168 | tf_op jit(solution)/shard_map/add | solution.py:1254
  (4 shorter events, 0.1 us)
Async XLA Ops:
  1.3 74.8 %copy-start.6 = (s32[40]{0:T(128)S(1)}, s32[40]{0:T(128)}, u32[]{:S(2)}) copy-start(s32[40]{0:T(128)} %param.23) | copy-start | bytes 484
  1.3 76.1 %copy-start.1 = (bf16[768,207]{0,1:T(8,128)(2,1)S(1)}, bf16[768,207]{0,1:T(8,128)(2,1)}, u32[]{:S(2)}) copy-start(bf16[768,207]{0,1:T(8,128)(2,1)} %param.37) | copy-start | bytes 953860
  1.3 76.1 %copy-start.3 = (bf16[768,69]{0,1:T(8,128)(2,1)S(1)}, bf16[768,69]{0,1:T(8,128)(2,1)}, u32[]{:S(2)}) copy-start(bf16[768,69]{0,1:T(8,128)(2,1)} %param.39) | copy-start | bytes 317956
  1.3 77.1 %copy-start.4 = (f32[207]{0:T(256)S(1)}, f32[207]{0:T(256)}, u32[]{:S(2)}) copy-start(f32[207]{0:T(256)} %param.38) | copy-start | bytes 2488
  1.3 77.1 %copy-start.5 = (f32[69]{0:T(128)S(1)}, f32[69]{0:T(128)}, u32[]{:S(2)}) copy-start(f32[69]{0:T(128)} %param.40) | copy-start | bytes 832
  250.4 10.5 %copy-start = (f32[3,80,512]{2,1,0:T(8,128)S(1)}, f32[3,80,512]{2,1,0:T(8,128)}, u32[]{:S(2)}) copy-start(f32[3,80,512]{2,1,0:T(8,128)} %get-tuple-element.59) | copy-start | bytes 1474564
  252.1 8.9 %copy-start.2 = (f32[80,512]{1,0:T(8,128)S(1)}, f32[80,512]{1,0:T(8,128)}, u32[]{:S(2)}) copy-start(f32[80,512]{1,0:T(8,128)} %get-tuple-element.58) | copy-start | bytes 491524

commit v5 on v4

--- a/solution.py
+++ b/solution.py
@@ -9,6 +9,8 @@
 HD = 64
 EXPERTS = 3
 HEAD_ROWS = 80
+MID_VMEM = 62 << 20
+PRE_BIT = 2
 EPSILON = 1e-05
 F32 = jnp.float32
 BF16 = jnp.bfloat16
@@ -20,6 +22,21 @@
 
 def row_of(ref):
     return ref[...].reshape(1, ref.shape[0])
+
+
+W_FLIGHT = 2
+W_PLAN = (
+    (0, (("far", 0),)),
+    (1, (("far", 1),)),
+    (3, (("far", 2), (0, 0))),
+    (4, ((0, 1),)),
+    (5, ((0, 2),)),
+    (6, (("far", 3),)),
+    (7, ((1, 1),)),
+    (9, (("far", 4),)),
+    (10, ((1, 2), (0, 3), ("far", 5))),
+    (11, ((0, 4), (0, 5))),
+)
 
 
 def fwd_kernel(
@@ -35,7 +52,6 @@
     dpi, tpi = lax.axis_index("dp"), lax.axis_index("tp")
     rows_dev, width = tiles_ref.shape
     piece = rows_dev // 2
-    mine = lax.rem(dpi, 2)
 
     def remote(src, dst, ssem, rsem, axis, bit):
         dev = (partner(dpi, bit), tpi) if axis == "dp" else (dpi, partner_any(tpi, bit))
@@ -56,39 +72,57 @@
         return remote(offs.at[0], offs.at[m], off_send.at[m], off_recv.at[m], "tp", m)
 
     parts = []
-    for src, dst, cuts in ((proj_ref, proj_all, 1), (wide_ref, wide_all, 2), (narrow_ref, narrow_all, 2)):
-        n = src.shape[0] // cuts
-        for c in range(cuts):
-            parts.append((src, dst, c * n, n // 2))
-
-    def w_half(part, whose):
-        return pl.ds(pl.multiple_of(part[2] + whose * part[3], 16), part[3])
+    for src, dst, cuts, share in (
+        (proj_ref, proj_all, (1,), (1,)),
+        (narrow_ref, narrow_all, (2, 2), (1, 2)),
+        (wide_ref, wide_all, (2, 3, 6), (1,)),
+    ):
+        lo = 0
+        for cut in cuts:
+            n = src.shape[0] // cut
+            parts.append((src, dst, lo, n, share))
+            lo += n
+
+    def w_rows(n, stage, theirs=False):
+        _, _, lo, size, share = parts[n]
+        size = size // (1 << len(share))
+        for bit in share[:stage]:
+            size *= 2
+        at = lo
+        step = size
+        for k, bit in enumerate(share[stage:]):
+            mine = lax.rem(lax.div(dpi, bit), 2)
+            if theirs and k == 0:
+                mine = 1 - mine
+            at = at + mine * step
+            step *= 2
+        return pl.ds(pl.multiple_of(at, 16), size)
 
     def w_far(n):
-        src, dst, _, _ = parts[n]
-        rows = w_half(parts[n], mine)
+        src, dst = parts[n][:2]
+        rows = w_rows(n, 0)
         return remote(
             src.at[rows], dst.at[1, rows], w_send.at[n, 0], w_recv.at[n, 0], "tp", 2
         )
 
-    def w_side(n):
+    def w_side(n, k):
+        rows = w_rows(n, k)
+        here = parts[n][1].at[1, rows]
+        return remote(
+            here, here, w_send.at[n, 1 + k], w_recv.at[n, 1 + k], "dp", parts[n][4][k]
+        )
+
+    def w_fwd(n, k):
         dst = parts[n][1]
-        rows = w_half(parts[n], mine)
-        here = dst.at[1, rows]
-        return remote(here, here, w_send.at[n, 1], w_recv.at[n, 1], "dp", 1)
-
-    def w_fwd(n, second):
-        dst = parts[n][1]
-        rows = w_half(parts[n], 1 - mine if second else mine)
-        k = 3 if second else 2
+        rows = w_rows(n, 0) if k == 0 else w_rows(n, k - 1, True)
         return remote(
-            dst.at[1, rows], dst.at[2, rows], w_send.at[n, k], w_recv.at[n, k], "tp", 1
+            dst.at[1, rows], dst.at[2, rows], w_send.at[n, 3 + k], w_recv.at[n, 3 + k], "tp", 1
         )
 
     def w_near(n):
-        src, dst, lo, half = parts[n]
-        rows = pl.ds(lo, 2 * half)
-        return remote(src.at[rows], dst.at[0, rows], w_send.at[n, 4], w_recv.at[n, 4], "tp", 1)
+        src, dst, lo, size, _ = parts[n]
+        rows = pl.ds(lo, size)
+        return remote(src.at[rows], dst.at[0, rows], w_send.at[n, 6], w_recv.at[n, 6], "tp", 1)
 
     def o_copy(p):
         if p == 0:
@@ -115,7 +149,7 @@
     @pl.when(step == 0)
     def _():
         barrier = pltpu.get_barrier_semaphore()
-        others = [("tp", 1), ("tp", 2), ("tp", 3), ("dp", 1)]
+        others = [("tp", 1), ("tp", 2), ("tp", 3), ("dp", 1), ("dp", 2)]
         for axis, bit in others:
             dev = (partner(dpi, bit), tpi) if axis == "dp" else (dpi, partner_any(tpi, bit))
             pl.semaphore_signal(
@@ -182,8 +216,8 @@
         for c in range(2):
             row_copy(1, c).wait()
             row_copy(2, c).start()
-        w_far(0).start()
-        w_far(1).start()
+        for n in range(W_FLIGHT):
+            w_far(n).start()
         project(2)
         for c in range(2):
             row_copy(2, c).wait()
@@ -208,12 +242,8 @@
     def after(st, *what):
         seq.setdefault(min(st, steps - 1), []).extend(what)
 
-    arrive = (1, 3, 6, 9, 11)
-    side = (3, 7, 10, 11, 11)
-    for n in range(len(parts)):
-        after(arrive[n], ("far", n))
-    for n in range(len(parts)):
-        after(side[n], ("side", n))
+    for st, what in W_PLAN:
+        after(st, *what)
     for st, what in seq.items():
 
         @pl.when(step == st)
@@ -221,13 +251,15 @@
             for kind, n in what:
                 if kind == "far":
                     w_far(n).wait()
-                    if n + 2 < len(parts):
-                        w_far(n + 2).start()
-                    w_side(n).start()
-                    w_fwd(n, False).start()
+                    if n + W_FLIGHT < len(parts):
+                        w_far(n + W_FLIGHT).start()
+                    w_side(n, 0).start()
+                    w_fwd(n, 0).start()
                 else:
-                    w_side(n).wait()
-                    w_fwd(n, True).start()
+                    w_side(n, kind).wait()
+                    if kind + 1 < len(parts[n][4]):
+                        w_side(n, kind + 1).start()
+                    w_fwd(n, kind + 1).start()
 
     for k in range(tp_size):
 
@@ -246,8 +278,8 @@
         own_copy.start()
         for n in range(len(parts)):
             w_near(n).wait()
-            w_fwd(n, False).wait()
-            w_fwd(n, True).wait()
+            for k in range(1 + len(parts[n][4])):
+                w_fwd(n, k).wait()
         own_copy.wait()
         pltpu.make_async_copy(rows_ref, rows_out, out_sem.at[0]).wait()
 
@@ -299,8 +331,8 @@
             pltpu.SemaphoreType.DMA((tp_size,)),
             pltpu.SemaphoreType.DMA((tp_size,)),
             pltpu.SemaphoreType.DMA,
-            pltpu.SemaphoreType.DMA((5, 5)),
-            pltpu.SemaphoreType.DMA((5, 5)),
+            pltpu.SemaphoreType.DMA((6, 7)),
+            pltpu.SemaphoreType.DMA((6, 7)),
         ],
         compiler_params=pltpu.CompilerParams(
             vmem_limit_bytes=56 << 20, collective_id=0, has_side_effects=True
@@ -370,7 +402,7 @@
 
     bufs, at = [], 0
     for c in chunks:
-        n = 8 if c["tp"] else 5
+        n = 7 if c["tp"] else 5
         bufs.append(per[at : at + n])
         at += n
 
@@ -381,8 +413,7 @@
             self.acc = bufs[k][0]
             self.halves = bufs[k][1:4]
             if self.c["tp"]:
-                self.mid, self.got, self.got_far, self.got_x = bufs[k][4:8]
-                self.fin = self.got
+                self.mid, self.fin, self.got_x = bufs[k][4:7]
             else:
                 self.fin = bufs[k][4]
             self.stages = []
@@ -399,6 +430,8 @@
                     seq.append((name, size))
             for name in bits[3:]:
                 self.stages.append(("B", name, (list(seq), size)))
+            if self.c.get("pre"):
+                self.stages.pop(1)
             while seq:
                 name, half = seq[-1]
                 self.stages.append(("G", name, (list(seq), half)))
@@ -415,12 +448,10 @@
             ss, rs = send_sems.at[self.k], recv_sems.at[self.k]
             if kind == "C":
                 lo = self.c["part"] * self.rows
-                blk = [self.c_src.at[p, pl.ds(lo, self.rows)] for p in range(tp_size)]
+                blk = [self.c_src.at[p, pl.ds(lo, self.rows)] for p in range(2)]
                 return [
-                    remote(blk[1], self.got, ss.at[0], rs.at[0], "tp", 1),
-                    remote(blk[3], self.got_far, ss.at[1], rs.at[1], "tp", 1),
                     pltpu.make_async_copy(blk[0], self.acc, local_sems.at[self.k, 0]),
-                    pltpu.make_async_copy(blk[2], self.mid, local_sems.at[self.k, 1]),
+                    pltpu.make_async_copy(blk[1], self.mid, local_sems.at[self.k, 1]),
                 ]
             if kind == "X":
                 off = self.off(info)
@@ -477,9 +508,6 @@
             kind, name, info = self.stages[s]
             for cp in self.copies(s):
                 cp.wait()
-            if kind == "C":
-                add_rows(self.acc, self.got, None, 0, 0, self.rows)
-                add_rows(self.mid, self.got_far, None, 0, 0, self.rows)
             if kind == "X":
                 off = self.off(info)
                 add_rows(self.acc, self.got_x, None, off, off, name)
@@ -789,22 +817,21 @@
     return index
 
 
-PLAN_FIRST = (4, 2)
-PLAN_STEPS = ((0, 1), (4, 2, 0, 1, 3), (), (3,), (4, 2), (), (), (4,), (2, 0, 1, 4), (5, 3, 2), (4,), (2, 5),)
-PLAN_TAIL = ((), (4, 0), (), (3,), (2,),)
-PLAN_WAIT = (5, 4, 0, 6, 5, 1, 4, 3, 2, 0)
-PLAN_LAST = ((1, 6), (2, 5, 3), (6,),)
-PLAN_END = (1, 3, 0, 6, 5, 1, 0, 3, 1, 6, 3, 0, 1, 6)
-
+PLAN_FIRST = (2, 0)
+PLAN_STEPS = ((2, 0, 4, 1), (4, 1, 3), (3,), (0,), (2, 1), (0,), (1,), (0, 4, 1), (2,), (0, 3, 5, 4, 1), (2,), (),)
+PLAN_TAIL = ((0,), (), (2,), (5,), (),)
+PLAN_WAIT = (3, 4, 2, 6, 5, 0, 4, 1, 3)
+PLAN_LAST = ((2,), (6, 5), (4, 3),)
+PLAN_END = (2, 6, 4, 3, 5, 1, 6, 3, 6, 5, 4, 6, 3)
 
 ORDERS = (
-    (2, "X", 1, 4),
+    ("X", 2, 1, 4),
     (2, "X", 1, 4),
     (1, "X", 2, 4),
-    ("X", 1, 2, 4),
-    ("X", 1, 2, 4),
+    ("X", 2, 1, 4),
+    (2, "X", 1, 4),
     (1, 2, 4),
-    (1, 4, 2),
+    (1, 2, 4),
 )
 
 
@@ -816,8 +843,8 @@
     half = width // 2
     ph_rows = parts[2].shape[1]
     chunks = [
-        dict(tp=True, rows=half, part=0, order=ORDERS[0], out=(0, 0)),
-        dict(tp=True, rows=half, part=1, order=ORDERS[1], out=(0, half)),
+        dict(tp=True, rows=half, part=0, pre=True, order=ORDERS[0], out=(0, 0)),
+        dict(tp=True, rows=half, part=1, pre=True, order=ORDERS[1], out=(0, half)),
         dict(tp=True, rows=half, part=0, order=ORDERS[2], out=(1, 0)),
         dict(tp=True, rows=half, part=1, order=ORDERS[3], out=(1, half)),
         dict(tp=True, rows=ph_rows, part=0, order=ORDERS[4], out=(2, 0), head=(heads * HD, HEAD_ROWS)),
@@ -848,7 +875,7 @@
         scratch.append(pltpu.VMEM((2, r // 4, width), BF16))
         scratch.append(pltpu.VMEM((2 + max(nbits - 3, 0), r // 8, width), BF16))
         if c["tp"]:
-            scratch += [pltpu.VMEM((r, width), BF16)] * 4
+            scratch += [pltpu.VMEM((r, width), BF16)] * 3
         else:
             scratch.append(pltpu.VMEM((r, width), BF16))
     scratch += [
@@ -901,8 +928,9 @@
     pj_own, pj_far, wi_own, wi_far, na_own, na_far,
     dn_ref, dw_ref, ph_ref, do_ref, dx1_ref, small_ref, gates_ref, corr_ref,
     pj, wi, na, x1, hat, rstd, c_low, act, slope, h_low, hg, dx2, dz, du, dc, dy, hd, dn, dw, ph, dos,
-    in_sem, out_sem, *, tp_size, heads
+    got_n, got_w, got_p, got_x, got_z, c_send, c_recv, x_send, x_recv, in_sem, out_sem, *, tp_size, heads
 ):
+    dpi = lax.axis_index("dp")
     tpi = lax.axis_index("tp")
     rows_dev, width = tiles_ref.shape
     nh = heads * HD
@@ -923,6 +951,39 @@
     load_na = loads(2, na_own, na_far, na)
     for cp in load_pj + load_wi + load_na:
         cp.start()
+    other = (dpi, partner(tpi, 1))
+    side = (partner(dpi, PRE_BIT), tpi)
+    far = (dpi, partner(tpi, 2))
+    barrier = pltpu.get_barrier_semaphore()
+    for dev in (other, side, far):
+        pl.semaphore_signal(
+            barrier, inc=1, device_id=dev, device_id_type=pl.DeviceIdType.MESH
+        )
+    mine = lax.rem(lax.div(dpi, PRE_BIT), 2)
+    top_rows, quarter = width // 2, width // 4
+
+    def far_copy():
+        return pltpu.make_async_remote_copy(
+            src_ref=dn.at[2, pl.ds(0, top_rows)], dst_ref=got_x,
+            send_sem=x_send.at[0], recv_sem=x_recv.at[0],
+            device_id=far, device_id_type=pl.DeviceIdType.MESH,
+        )
+
+    def side_copy(j):
+        rows = pl.ds(pl.multiple_of(top_rows + (1 - mine) * quarter, 16), quarter)
+        return pltpu.make_async_remote_copy(
+            src_ref=dn.at[2 * j, rows], dst_ref=got_z.at[j],
+            send_sem=x_send.at[1 + j], recv_sem=x_recv.at[1 + j],
+            device_id=side, device_id_type=pl.DeviceIdType.MESH,
+        )
+
+    def core_copy(k, j, src, got):
+        return pltpu.make_async_remote_copy(
+            src_ref=src.at[2 * j + 1], dst_ref=got.at[j],
+            send_sem=c_send.at[k, j], recv_sem=c_recv.at[k, j],
+            device_id=other, device_id_type=pl.DeviceIdType.MESH,
+        )
+
     small_ref[...] = jnp.zeros_like(small_ref)
     proj_bias, gain2, shift2, out_bias = (row_of(v) for v in (pb_ref, g2_ref, s2_ref, nb_ref))
     for cp in load_pj:
@@ -940,7 +1001,7 @@
         for r in blocks:
             m, d = gelu_parts(dot(c_low[r], wi[p]) + off_ref[p, 0:1])
             act[r, cols] = m.astype(BF16)
-            slope[r, cols] = d
+            slope[r, cols] = d.astype(BF16)
     for cp in load_na:
         cp.wait()
     for r in blocks:
@@ -972,20 +1033,38 @@
         return cp
 
     outs = []
-    for p in range(tp_size):
-        cols = pl.ds(p * width, width)
-        dn[p] = dot(act[:, cols], dz[...], ((0,), (0,))).astype(BF16)
-        outs.append(send_out(0, p, dn.at[p], dn_ref.at[p]))
-    for p in range(tp_size):
+    pairs = range(tp_size // 2)
+
+    def narrow_dot(p):
+        return dot(act[:, p * width : (p + 1) * width], dz[...], ((0,), (0,)))
+
+    def wide_dot(p):
+        return dot(c_low[...], du[p], ((0,), (0,)))
+
+    pl.semaphore_wait(barrier, 3)
+    for j in (1, 0):
+        dn[2 * j + 1] = narrow_dot(2 * j + 1).astype(BF16)
+        core_copy(0, j, dn, got_n).start()
+    def hidden_grad(p):
         cols = pl.ds(p * width, width)
         for r in blocks:
-            v = dot(dz[r], na[cols], ((1,), (1,))) * slope[r, cols]
+            v = dot(dz[r], na[cols], ((1,), (1,))) * slope[r, cols].astype(F32)
             low = v.astype(BF16)
             du[p, r] = low
             small_ref[8 + p : 9 + p] += jnp.sum(low.astype(F32), axis=0, keepdims=True)
-    for p in range(tp_size):
-        dw[p] = dot(c_low[...], du[p], ((0,), (0,))).astype(BF16)
-        outs.append(send_out(1, p, dw.at[p], dw_ref.at[p]))
+    hidden_grad(1)
+    hidden_grad(3)
+    for j in (1, 0):
+        core_copy(0, j, dn, got_n).wait()
+        dn[2 * j] = (narrow_dot(2 * j) + got_n[j].astype(F32)).astype(BF16)
+        if j == 1:
+            far_copy().start()
+        side_copy(j).start()
+    hidden_grad(0)
+    hidden_grad(2)
+    for j in pairs:
+        dw[2 * j + 1] = wide_dot(2 * j + 1).astype(BF16)
+        core_copy(1, j, dw, got_w).start()
     for r in blocks:
         g = dot(du[0, r], wi[0], ((1,), (1,)))
         for p in range(1, tp_size):
@@ -1006,7 +1085,22 @@
         at = pl.ds(pl.multiple_of(partner_any(tpi, p) * HEAD_ROWS, 16), HEAD_ROWS)
         ph[p, nh : nh + HEAD_ROWS] = hd[at]
         ph[p, nh + HEAD_ROWS :] = jnp.zeros((ph.shape[1] - nh - HEAD_ROWS, width), BF16)
-        outs.append(send_out(3, p, ph.at[p], ph_ref.at[p]))
+    for j in pairs:
+        core_copy(2, j, ph, got_p).start()
+    for j in pairs:
+        core_copy(1, j, dw, got_w).wait()
+        dw[2 * j] = (wide_dot(2 * j) + got_w[j].astype(F32)).astype(BF16)
+        outs.append(send_out(1, j, dw.at[2 * j], dw_ref.at[j]))
+    for j in pairs:
+        core_copy(2, j, ph, got_p).wait()
+        ph[2 * j] = (ph[2 * j].astype(F32) + got_p[j].astype(F32)).astype(BF16)
+        outs.append(send_out(3, j, ph.at[2 * j], ph_ref.at[j]))
+    far_copy().wait()
+    add_rows(dn.at[0], got_x, None, 0, 0, top_rows)
+    for j in (1, 0):
+        side_copy(j).wait()
+        add_rows(dn.at[2 * j], got_z, j, top_rows + mine * quarter, 0, quarter)
+        outs.append(send_out(0, j, dn.at[2 * j], dn_ref.at[j]))
     for cp in outs:
         cp.wait()
 
@@ -1020,14 +1114,15 @@
     any_spec = pl.BlockSpec(memory_space=pl.ANY)
     vmem = pl.BlockSpec(memory_space=pltpu.VMEM)
     big = (tp_size, width, width)
+    pair = (tp_size // 2,)
     return pl.pallas_call(
         functools.partial(mid_kernel, tp_size=tp_size, heads=heads),
         in_specs=[vmem] * 11 + [any_spec] * 6,
         out_specs=[any_spec] * 4 + [vmem] * 4,
         out_shape=[
-            jax.ShapeDtypeStruct(big, BF16),
-            jax.ShapeDtypeStruct(big, BF16),
-            jax.ShapeDtypeStruct((tp_size, ph_rows, width), BF16),
+            jax.ShapeDtypeStruct(pair + (width, width), BF16),
+            jax.ShapeDtypeStruct(pair + (width, width), BF16),
+            jax.ShapeDtypeStruct(pair + (ph_rows, width), BF16),
             jax.ShapeDtypeStruct((tp_size, heads, HD, rows_dev), BF16),
             jax.ShapeDtypeStruct((rows_dev, width), F32),
             jax.ShapeDtypeStruct((16, width), F32),
@@ -1043,7 +1138,7 @@
             pltpu.VMEM((rows_dev, 1), F32),
             pltpu.VMEM((rows_dev, width), BF16),
             pltpu.VMEM((rows_dev, tp_size * width), BF16),
-            pltpu.VMEM((rows_dev, tp_size * width), F32),
+            pltpu.VMEM((rows_dev, tp_size * width), BF16),
             pltpu.VMEM((rows_dev, width), BF16),
             pltpu.VMEM((n_head, rows_dev), BF16),
             pltpu.VMEM((rows_dev, width), F32),
@@ -1056,10 +1151,21 @@
             pltpu.VMEM(big, BF16),
             pltpu.VMEM((tp_size, ph_rows, width), BF16),
             pltpu.VMEM((tp_size, heads, HD, rows_dev), BF16),
+            pltpu.VMEM(pair + (width, width), BF16),
+            pltpu.VMEM(pair + (width, width), BF16),
+            pltpu.VMEM(pair + (ph_rows, width), BF16),
+            pltpu.VMEM((width // 2, width), BF16),
+            pltpu.VMEM(pair + (width // 4, width), BF16),
+            pltpu.SemaphoreType.DMA((3, tp_size // 2)),
+            pltpu.SemaphoreType.DMA((3, tp_size // 2)),
+            pltpu.SemaphoreType.DMA((3,)),
+            pltpu.SemaphoreType.DMA((3,)),
             pltpu.SemaphoreType.DMA((3, tp_size)),
             pltpu.SemaphoreType.DMA((4, tp_size)),
         ],
-        compiler_params=pltpu.CompilerParams(vmem_limit_bytes=60 << 20),
+        compiler_params=pltpu.CompilerParams(
+            vmem_limit_bytes=MID_VMEM, collective_id=2, has_side_effects=True
+        ),
         cost_estimate=pl.CostEstimate(
             flops=18_000_000_000, bytes_accessed=30 << 20, transcendentals=2_000_000
         ),

time: 275 us -> 260 us (0.945)
  Pallas kernels: 252 us -> 237 us
    pallas_call x1, Pallas kernels: 139 us -> 126 us  [attn_bwd(): pl.pallas_call(functools.partial(bwd_kernel, scale=scale, chunks=chunks,...]
    pallas_call x1, Pallas kernels: 74.8 us -> 66.6 us  [attn_fwd(): pl.pallas_call(functools.partial(fwd_kernel, scale=scale, dp_size=dp_size...]
    pallas_call x1, Pallas kernels: 31.7 us -> 38 us  [mid(): pl.pallas_call(functools.partial(mid_kernel, tp_size=tp_size, heads=heads...]
where the time goes in v5:
time: 260 us; the launch traced here: 256 us
  Pallas kernels  237 us (91%)
  other arithmetic  9.74 us (4%)
  local copies, waits for them, and re-layouts  6.06 us (2%)
    pallas_call x1, Pallas kernels, attn_bwd(): pl.pallas_call(functools.partial(bwd_kernel, scale=scale, chunks=chunks,...  126 us
    pallas_call x1, Pallas kernels, attn_fwd(): pl.pallas_call(functools.partial(fwd_kernel, scale=scale, dp_size=dp_size...  66.6 us
    pallas_call x1, Pallas kernels, mid(): pl.pallas_call(functools.partial(mid_kernel, tp_size=tp_size, heads=heads...  38 us
    add x1, other arithmetic, body(): blended + gates[e][:, None, :] * specialist_outlooks[e].astype(F32)  9.04 us
    pallas_call x1, Pallas kernels, finish(): pl.pallas_call(functools.partial(finish_kernel, fields=fields), grid=(ste...  6.89 us

profile of v5, /device:TPU:0, one launch (start us, length us, event | category | flops | bytes accessed | tf_op | source)
XLA Modules:
  0.0 255.6 jit_solution(14761775524423684603)
XLA Ops:
  1.3 0.0 copy-start.6
  1.3 0.0 copy-start.1
  1.3 0.0 copy-start.3
  1.3 0.0 copy-start.4
  1.3 0.0 copy-start.5
  1.4 66.6 %attn_fwd.1 = (bf16[4,512,768]{2,1,0:T(8,128)(2,1)}, bf16[3,3,64,2048]{3,2,1,0:T(8,128)(2,1)}, bf16[4,3,64,512]{3,2,1,0:T(8,128)(2,1)}, f32[4,3,1,512]{3,2,1,0:T...) custom-call(s32[1]{0:T(128)} %copy.40.lead_ref, ...), custom_call_target="tpu_custom_call" | custom-call | flops 30000001024 | bytes 41943040 | tf_op jit(solution)/shard_map/attn_fwd/pallas_call | solution.py:299
  68.0 0.0 copy-done.6
  68.0 0.6 dynamic_slice.3
  69.3 0.0 copy-done.1
  69.3 0.0 copy-done.3
  69.3 0.1 reshape.78
  69.4 0.8 pad.8
  70.3 0.0 copy-done.4
  70.3 0.0 copy-done.5
  70.3 0.1 pad_maximum_fusion
  70.3 0.1 reshape_broadcast_in_dim.3
  70.4 0.8 reshape.87.hb_ref
  71.3 38.0 %mid.1 = (bf16[2,768,768]{2,1,0:T(8,128)(2,1)}, bf16[2,768,768]{2,1,0:T(8,128)(2,1)}, bf16[2,384,768]{2,1,0:T(8,128)(2,1)}, bf16[4,3,64,512]{3,2,1,0:T(8,128)(2,...) custom-call(bf16[512,768]{1,0:T(8,128)(2,1)} %tiles_ref.5, ...), custom_call_target="tpu_custom_call" | custom-call | flops 17999998976 | bytes 31457280 | tf_op jit(solution)/shard_map/mid/pallas_call | solution.py:1118
  109.3 0.6 compare_convert_fusion.onehot_ref
  109.9 125.7 %attn_bwd.1 = (f32[512,768]{1,0:T(8,128)}, f32[16,768]{1,0:T(8,128)}, f32[48,768]{1,0:T(8,128)}, bf16[320,768]{1,0:T(8,128)(2,1)}, bf16[768,768]{1,0:T(8,128)(2,...) custom-call(bf16[3,3,64,2048]{3,2,1,0:T(8,128)(2,1)} %get-tuple-element.60.qkv_ref, ...), custom_call_target="tpu_custom_call" | custom-call | flops 60000002048 | bytes 31457280 | tf_op jit(solution)/shard_map/attn_bwd/pallas_call | solution.py:897
  235.6 0.0 copy-start
  235.6 1.6 slice_reduce_fusion
  237.2 0.0 copy-start.2
  237.2 6.9 %finish.1 = (f32[768,768]{1,0:T(8,128)}, f32[768,768]{1,0:T(8,128)}, f32[192,768]{1,0:T(8,128)}, f32[3,192,768]{2,1,0:T(8,128)}, f32[207,768]{1,0:T(8,128)}, /*i...) custom-call(bf16[768,768]{1,0:T(8,128)(2,1)} %get-tuple-element.69.n_ref, ...), custom_call_target="tpu_custom_call" | custom-call | tf_op jit(solution)/shard_map/finish/pallas_call | solution.py:1210
  244.1 0.7 slice_reduce_fusion.7
  244.8 0.1 reshape_squeeze.3
  244.9 0.6 reshape.83
  245.6 0.5 slice_bitcast_fusion.3
  246.1 0.0 copy-done
  246.1 0.0 copy-done.2
  246.1 9.0 %fusion = f32[69,64,512]{2,1,0:T(8,128)} fusion(bf16[3,69,64,512]{3,2,1,0:T(8,128)(2,1)} %exp_ref.1, f32[69,512]{1,0:T(8,128)S(1)} %get-tuple-element.94, f32[69,512]{1,0:T(8,128)S(1)} %get-tuple-element.95, f32[69,512]{1,0:T(8,128)S(1)} %get-tuple-element.93, f32[69,512]{1,0:T(8,128)S(1)} %slice.58), kind=kLoop, calls=%fused_computation.1 | loop fusion | flops 20348928 | bytes 23175168 | tf_op jit(solution)/shard_map/add | solution.py:1360
  (4 shorter events, 0.1 us)
Async XLA Ops:
  1.3 66.7 %copy-start.6 = (s32[40]{0:T(128)S(1)}, s32[40]{0:T(128)}, u32[]{:S(2)}) copy-start(s32[40]{0:T(128)} %param.23) | copy-start | bytes 484
  1.3 67.9 %copy-start.1 = (bf16[768,207]{0,1:T(8,128)(2,1)S(1)}, bf16[768,207]{0,1:T(8,128)(2,1)}, u32[]{:S(2)}) copy-start(bf16[768,207]{0,1:T(8,128)(2,1)} %param.37) | copy-start | bytes 953860
  1.3 67.9 %copy-start.3 = (bf16[768,69]{0,1:T(8,128)(2,1)S(1)}, bf16[768,69]{0,1:T(8,128)(2,1)}, u32[]{:S(2)}) copy-start(bf16[768,69]{0,1:T(8,128)(2,1)} %param.39) | copy-start | bytes 317956
  1.3 68.9 %copy-start.4 = (f32[207]{0:T(256)S(1)}, f32[207]{0:T(256)}, u32[]{:S(2)}) copy-start(f32[207]{0:T(256)} %param.38) | copy-start | bytes 2488
  1.3 68.9 %copy-start.5 = (f32[69]{0:T(128)S(1)}, f32[69]{0:T(128)}, u32[]{:S(2)}) copy-start(f32[69]{0:T(128)} %param.40) | copy-start | bytes 832
  235.6 10.5 %copy-start = (f32[3,80,512]{2,1,0:T(8,128)S(1)}, f32[3,80,512]{2,1,0:T(8,128)}, u32[]{:S(2)}) copy-start(f32[3,80,512]{2,1,0:T(8,128)} %get-tuple-element.59) | copy-start | bytes 1474564
  237.2 8.9 %copy-start.2 = (f32[80,512]{1,0:T(8,128)S(1)}, f32[80,512]{1,0:T(8,128)}, u32[]{:S(2)}) copy-start(f32[80,512]{1,0:T(8,128)} %get-tuple-element.58) | copy-start | bytes 491524

commit v6 on v5

--- a/solution.py
+++ b/solution.py
@@ -24,7 +24,7 @@
     return ref[...].reshape(1, ref.shape[0])
 
 
-W_FLIGHT = 2
+W_FLIGHT = 6
 W_PLAN = (
     (0, (("far", 0),)),
     (1, (("far", 1),)),
@@ -179,6 +179,8 @@
         row_copy(0, 1).start()
         for m in range(1, tp_size):
             off_copy(m).start()
+        for n in range(W_FLIGHT):
+            w_far(n).start()
 
         def contract(g, carry):
             @pl.when(g + depth - 1 < groups)
@@ -216,8 +218,6 @@
         for c in range(2):
             row_copy(1, c).wait()
             row_copy(2, c).start()
-        for n in range(W_FLIGHT):
-            w_far(n).start()
         project(2)
         for c in range(2):
             row_copy(2, c).wait()
@@ -1174,8 +1174,8 @@
 
 
 def finish_kernel(
-    n_ref, i_ref, ph_ref, qa_ref, qb_ref, hd_ref, tok_ref, dx_ref, table_ref,
-    no_ref, io_ref, po_ref, qo_ref, g_ref, c_ref, to_ref, lead_ref, *, fields
+    n_ref, i_ref, ph_ref, qa_ref, qb_ref, hd_ref, tok_ref, dx_ref, table_ref, small_ref,
+    no_ref, io_ref, po_ref, qo_ref, g_ref, c_ref, to_ref, lead_ref, *vec_refs, fields
 ):
     no_ref[...] = n_ref[...].astype(F32)
     io_ref[...] = i_ref[...].astype(F32)
@@ -1190,9 +1190,12 @@
     c_ref[...] = hd_ref[pl.ds(EXPERTS * HEAD_ROWS, HEAD_ROWS)].astype(F32)[:fields]
     to_ref[...] = tok_ref[...] + dx_ref[...]
     lead_ref[...] = table_ref[8:]
-
-
-def finish(n, i, ph, q, hd, tok, dx1, table, heads, fields):
+    rows = [table_ref[0:1], table_ref[1:2]] + [small_ref[k : k + 1] for k in (3, 1, 2, 8, 0)]
+    for ref, row in zip(vec_refs, rows):
+        ref[...] = row.reshape(row.shape[1])
+
+
+def finish(n, i, ph, q, hd, tok, dx1, table, small, heads, fields):
     width = n.shape[0]
     nh = heads * HD
     steps = 3
@@ -1220,6 +1223,7 @@
             token,
             token,
             pl.BlockSpec(table.shape, lambda g: (0, 0)),
+            pl.BlockSpec(small.shape, lambda g: (0, 0)),
         ],
         out_specs=[
             by_row(rows),
@@ -1230,7 +1234,8 @@
             pl.BlockSpec((fields, rows), lambda g: (0, g)),
             token,
             pl.BlockSpec((leads, width), lambda g: (0, 0)),
-        ],
+        ]
+        + [pl.BlockSpec((width,), lambda g: (0,))] * 7,
         out_shape=[
             jax.ShapeDtypeStruct((width, width), F32),
             jax.ShapeDtypeStruct((width, width), F32),
@@ -1240,9 +1245,10 @@
             jax.ShapeDtypeStruct((fields, width), F32),
             jax.ShapeDtypeStruct(tok.shape, F32),
             jax.ShapeDtypeStruct((leads, width), F32),
-        ],
+        ]
+        + [jax.ShapeDtypeStruct((width,), F32)] * 7,
         name="finish",
-    )(n, i, ph, q, q, hd, tok, dx1, table)
+    )(n, i, ph, q, q, hd, tok, dx1, table, small)
 
 
 def norm_parts(values):
@@ -1368,32 +1374,32 @@
         )
         (
             narrow_sum, wide_sum, proj_weight_grad, qkv_sum, gate_sum, correct_sum, tokens_grad,
-            lead_sum,
+            lead_sum, gain1_sum, shift1_sum, proj_bias_sum, gain2_sum, shift2_sum, in_bias_sum,
+            out_bias_sum,
         ) = finish(
-            n_low, i_low, ph, q_low, head_sum, token_part, dx1, table, heads, fields
+            n_low, i_low, ph, q_low, head_sum, token_part, dx1, table, small, heads, fields
         )
         qkv_sum = jnp.transpose(qkv_sum, (0, 2, 1))
         gate_weight_grad = gate_sum.T
         correct_weight_grad = correct_sum.T
         head_bias = small[4, : (EXPERTS + 1) * HEAD_ROWS].reshape(EXPERTS + 1, HEAD_ROWS)
         head_bias = head_bias[:, :fields]
-        in_bias_grad = small[8]
 
         return (
             blended,
             tokens_grad,
-            table[0],
-            table[1],
+            gain1_sum,
+            shift1_sum,
             lead_sum,
             qkv_sum,
             proj_weight_grad,
-            small[3],
-            small[1],
-            small[2],
+            proj_bias_sum,
+            gain2_sum,
+            shift2_sum,
             wide_sum,
-            in_bias_grad,
+            in_bias_sum,
             narrow_sum,
-            small[0],
+            out_bias_sum,
             gate_weight_grad,
             head_bias[:EXPERTS].reshape(EXPERTS * fields),
             correct_weight_grad,

time: 260 us -> 257 us (0.988)
  no operation moved by 1% of the time
where the time goes in v6:
time: 257 us; the launch traced here: 253 us
  Pallas kernels  236 us (92%)
  other arithmetic  9.74 us (4%)
  local copies, waits for them, and re-layouts  4.48 us (2%)
  between operations  2.6 us (1%)
    pallas_call x1, Pallas kernels, attn_bwd(): pl.pallas_call(functools.partial(bwd_kernel, scale=scale, chunks=chunks,...  125 us
    pallas_call x1, Pallas kernels, attn_fwd(): pl.pallas_call(functools.partial(fwd_kernel, scale=scale, dp_size=dp_size...  65.3 us
    pallas_call x1, Pallas kernels, mid(): pl.pallas_call(functools.partial(mid_kernel, tp_size=tp_size, heads=heads...  38.9 us
    add x1, other arithmetic, body(): blended + gates[e][:, None, :] * specialist_outlooks[e].astype(F32)  9.04 us
    pallas_call x1, Pallas kernels, finish(): pl.pallas_call(functools.partial(finish_kernel, fields=fields), grid=(ste...  6.93 us

profile of v6, /device:TPU:0, one launch (start us, length us, event | category | flops | bytes accessed | tf_op | source)
XLA Modules:
  0.0 252.7 jit_solution(1498798743649645705)
XLA Ops:
  1.3 0.0 copy-start.6
  1.3 0.0 copy-start.1
  1.3 0.0 copy-start.3
  1.3 0.0 copy-start.4
  1.3 0.0 copy-start.5
  1.4 65.3 %attn_fwd.1 = (bf16[4,512,768]{2,1,0:T(8,128)(2,1)}, bf16[3,3,64,2048]{3,2,1,0:T(8,128)(2,1)}, bf16[4,3,64,512]{3,2,1,0:T(8,128)(2,1)}, f32[4,3,1,512]{3,2,1,0:T...) custom-call(s32[1]{0:T(128)} %copy.40.lead_ref, ...), custom_call_target="tpu_custom_call" | custom-call | flops 30000001024 | bytes 41943040 | tf_op jit(solution)/shard_map/attn_fwd/pallas_call | solution.py:299
  66.6 0.0 copy-done.6
  66.7 0.6 dynamic_slice.3
  67.9 0.0 copy-done.1
  67.9 0.0 copy-done.3
  68.0 0.1 reshape.78
  68.1 0.8 pad.8
  68.9 0.0 copy-done.4
  68.9 0.0 copy-done.5
  68.9 0.1 pad_maximum_fusion
  69.0 0.1 reshape_broadcast_in_dim.3
  69.1 0.8 reshape.87.hb_ref
  69.9 38.9 %mid.1 = (bf16[2,768,768]{2,1,0:T(8,128)(2,1)}, bf16[2,768,768]{2,1,0:T(8,128)(2,1)}, bf16[2,384,768]{2,1,0:T(8,128)(2,1)}, bf16[4,3,64,512]{3,2,1,0:T(8,128)(2,...) custom-call(bf16[512,768]{1,0:T(8,128)(2,1)} %tiles_ref.5, ...), custom_call_target="tpu_custom_call" | custom-call | flops 17999998976 | bytes 31457280 | tf_op jit(solution)/shard_map/mid/pallas_call | solution.py:1118
  108.8 0.6 compare_convert_fusion.onehot_ref
  109.4 124.8 %attn_bwd.1 = (f32[512,768]{1,0:T(8,128)}, f32[16,768]{1,0:T(8,128)}, f32[48,768]{1,0:T(8,128)}, bf16[320,768]{1,0:T(8,128)(2,1)}, bf16[768,768]{1,0:T(8,128)(2,...) custom-call(bf16[3,3,64,2048]{3,2,1,0:T(8,128)(2,1)} %get-tuple-element.67.qkv_ref, ...), custom_call_target="tpu_custom_call" | custom-call | flops 60000002048 | bytes 31457280 | tf_op jit(solution)/shard_map/attn_bwd/pallas_call | solution.py:897
  234.2 0.0 copy-start
  234.2 0.0 copy-start.2
  234.2 6.9 %finish.1 = (f32[768,768]{1,0:T(8,128)}, f32[768,768]{1,0:T(8,128)}, f32[192,768]{1,0:T(8,128)}, f32[3,192,768]{2,1,0:T(8,128)}, f32[207,768]{1,0:T(8,128)}, /*i...) custom-call(bf16[768,768]{1,0:T(8,128)(2,1)} %get-tuple-element.76.n, ...), custom_call_target="tpu_custom_call" | custom-call | tf_op jit(solution)/shard_map/finish/pallas_call | solution.py:1213
  241.2 0.7 slice_reduce_fusion
  241.9 0.1 reshape_squeeze.3
  242.0 0.6 reshape.83
  242.6 0.5 slice_bitcast_fusion.3
  243.1 0.0 copy-done
  243.2 0.0 copy-done.2
  243.2 9.0 %fusion = f32[69,64,512]{2,1,0:T(8,128)} fusion(bf16[3,69,64,512]{3,2,1,0:T(8,128)(2,1)} %exp_ref.1, f32[69,512]{1,0:T(8,128)S(1)} %get-tuple-element.101, f32[69,512]{1,0:T(8,128)S(1)} %get-tuple-element.102, f32[69,512]{1,0:T(8,128)S(1)} %get-tuple-element.100, f32[69,512]{1,0:T(8,128)S(1)} %slice.37), kind=kLoop, calls=%fused_computation.1 | loop fusion | flops 20348928 | bytes 23175168 | tf_op jit(solution)/shard_map/add | solution.py:1366
  (4 shorter events, 0.1 us)
Async XLA Ops:
  1.3 65.3 %copy-start.6 = (s32[40]{0:T(128)S(1)}, s32[40]{0:T(128)}, u32[]{:S(2)}) copy-start(s32[40]{0:T(128)} %param.23) | copy-start | bytes 484
  1.3 66.6 %copy-start.1 = (bf16[768,207]{0,1:T(8,128)(2,1)S(1)}, bf16[768,207]{0,1:T(8,128)(2,1)}, u32[]{:S(2)}) copy-start(bf16[768,207]{0,1:T(8,128)(2,1)} %param.37) | copy-start | bytes 953860
  1.3 66.6 %copy-start.3 = (bf16[768,69]{0,1:T(8,128)(2,1)S(1)}, bf16[768,69]{0,1:T(8,128)(2,1)}, u32[]{:S(2)}) copy-start(bf16[768,69]{0,1:T(8,128)(2,1)} %param.39) | copy-start | bytes 317956
  1.3 67.6 %copy-start.4 = (f32[207]{0:T(256)S(1)}, f32[207]{0:T(256)}, u32[]{:S(2)}) copy-start(f32[207]{0:T(256)} %param.38) | copy-start | bytes 2488
  1.3 67.6 %copy-start.5 = (f32[69]{0:T(128)S(1)}, f32[69]{0:T(128)}, u32[]{:S(2)}) copy-start(f32[69]{0:T(128)} %param.40) | copy-start | bytes 832
  234.2 8.9 %copy-start = (f32[3,80,512]{2,1,0:T(8,128)S(1)}, f32[3,80,512]{2,1,0:T(8,128)}, u32[]{:S(2)}) copy-start(f32[3,80,512]{2,1,0:T(8,128)} %get-tuple-element.66) | copy-start | bytes 1474564
  234.2 9.0 %copy-start.2 = (f32[80,512]{1,0:T(8,128)S(1)}, f32[80,512]{1,0:T(8,128)}, u32[]{:S(2)}) copy-start(f32[80,512]{1,0:T(8,128)} %get-tuple-element.65) | copy-start | bytes 491524

commit v7 on v6

--- a/solution.py
+++ b/solution.py
@@ -924,7 +924,7 @@
 
 
 def mid_kernel(
-    tiles_ref, o_ref, dots_ref, off_ref, pb_ref, g2_ref, s2_ref, nb_ref, hw_ref, hb_ref, scale_ref,
+    tiles_ref, o_ref, dots_ref, off_ref, pb_ref, g2_ref, s2_ref, nb_ref, hw_ref, hb_ref, lead_ref, tally_ref,
     pj_own, pj_far, wi_own, wi_far, na_own, na_far,
     dn_ref, dw_ref, ph_ref, do_ref, dx1_ref, small_ref, gates_ref, corr_ref,
     pj, wi, na, x1, hat, rstd, c_low, act, slope, h_low, hg, dx2, dz, du, dc, dy, hd, dn, dw, ph, dos,
@@ -1008,7 +1008,7 @@
         h_low[r] = (x1[r] + dot(act[r], na[...]) + out_bias).astype(BF16)
 
     logits = dot(hw_ref[...], h_low[...], ((1,), (1,))) + hb_ref[...]
-    row_scale = scale_ref[0:1, 0:1]
+    row_scale = lax.rsqrt(jnp.full((1, 1), tally_ref[lead_ref[0]].astype(F32)))
     lg = [logits[e * HEAD_ROWS : (e + 1) * HEAD_ROWS] for e in range(EXPERTS)]
     top = jnp.maximum(jnp.maximum(lg[0], lg[1]), lg[2])
     ex = [jnp.exp(v - top) for v in lg]
@@ -1105,7 +1105,7 @@
         cp.wait()
 
 
-def mid(tiles, o_own, dots, off, vecs, hw, hb, row_scale, weights, mesh, heads):
+def mid(tiles, o_own, dots, off, vecs, hw, hb, lead, tally, weights, mesh, heads):
     rows_dev, width = tiles.shape
     tp_size = mesh.shape["tp"]
     nh = heads * HD
@@ -1117,7 +1117,7 @@
     pair = (tp_size // 2,)
     return pl.pallas_call(
         functools.partial(mid_kernel, tp_size=tp_size, heads=heads),
-        in_specs=[vmem] * 11 + [any_spec] * 6,
+        in_specs=[vmem] * 10 + [pl.BlockSpec(memory_space=pltpu.SMEM)] * 2 + [any_spec] * 6,
         out_specs=[any_spec] * 4 + [vmem] * 4,
         out_shape=[
             jax.ShapeDtypeStruct(pair + (width, width), BF16),
@@ -1170,7 +1170,7 @@
             flops=18_000_000_000, bytes_accessed=30 << 20, transcendentals=2_000_000
         ),
         name="mid",
-    )(tiles, o_own, dots, off, *vecs, hw, hb, row_scale, *weights)
+    )(tiles, o_own, dots, off, *vecs, hw, hb, lead, tally, *weights)
 
 
 def finish_kernel(
@@ -1312,9 +1312,6 @@
         scale_val = HD ** (-0.5)
         tp_index = lax.axis_index("tp")
         lead = snapshot_horizon_slot[0]
-        row_scale = lax.rsqrt(
-            lax.dynamic_slice_in_dim(horizon_sample_tally, lead, 1, 0).astype(F32)
-        )[0]
         nh = heads * HD
         w_t = jnp.transpose(triple_head_matrix, (0, 2, 1))
         (attn_rows, qkv, o_heads, lse, o_own, dots, off_all, proj_all, wide_all, narrow_all) = attn_fwd(
@@ -1350,7 +1347,8 @@
             vec,
             hw,
             hb,
-            row_scale[None, None],
+            snapshot_horizon_slot,
+            horizon_sample_tally,
             [
                 attending_matrix, proj_all, widening_matrix, wide_all,
                 narrowing_matrix, narrow_all,

time: 257 us -> 256 us (level)
  no operation moved by 1% of the time
where the time goes in v7:
time: 256 us; the launch traced here: 251 us
  Pallas kernels  236 us (92%)
  other arithmetic  9.74 us (4%)
  local copies, waits for them, and re-layouts  3.89 us (2%)
    pallas_call x1, Pallas kernels, attn_bwd(): pl.pallas_call(functools.partial(bwd_kernel, scale=scale, chunks=chunks,...  125 us
    pallas_call x1, Pallas kernels, attn_fwd(): pl.pallas_call(functools.partial(fwd_kernel, scale=scale, dp_size=dp_size...  65.2 us
    pallas_call x1, Pallas kernels, mid(): pl.pallas_call(functools.partial(mid_kernel, tp_size=tp_size, heads=heads...  38.9 us
    add x1, other arithmetic, body(): blended + gates[e][:, None, :] * specialist_outlooks[e].astype(F32)  9.04 us
    pallas_call x1, Pallas kernels, finish(): pl.pallas_call(functools.partial(finish_kernel, fields=fields), grid=(ste...  6.93 us

profile of v7, /device:TPU:0, one launch (start us, length us, event | category | flops | bytes accessed | tf_op | source)
XLA Modules:
  0.0 251.4 jit_solution(18111005047185701218)
XLA Ops:
  1.3 0.0 copy-start.1
  1.3 0.0 copy-start.3
  1.3 0.0 copy-start.4
  1.3 0.0 copy-start.5
  1.3 65.2 %attn_fwd.1 = (bf16[4,512,768]{2,1,0:T(8,128)(2,1)}, bf16[3,3,64,2048]{3,2,1,0:T(8,128)(2,1)}, bf16[4,3,64,512]{3,2,1,0:T(8,128)(2,1)}, f32[4,3,1,512]{3,2,1,0:T...) custom-call(s32[1]{0:T(128)} %copy.40.lead_ref, ...), custom_call_target="tpu_custom_call" | custom-call | flops 30000001024 | bytes 41943040 | tf_op jit(solution)/shard_map/attn_fwd/pallas_call | solution.py:299
  66.6 0.0 copy-done.1
  66.6 0.0 copy-done.3
  66.6 0.1 reshape.78
  66.8 0.8 pad.8
  67.6 0.0 copy-done.4
  67.6 0.0 copy-done.5
  67.6 0.1 pad_maximum_fusion
  67.7 0.1 reshape_broadcast_in_dim.3
  67.8 0.8 reshape.87.hb_ref
  68.6 38.9 %mid.1 = (bf16[2,768,768]{2,1,0:T(8,128)(2,1)}, bf16[2,768,768]{2,1,0:T(8,128)(2,1)}, bf16[2,384,768]{2,1,0:T(8,128)(2,1)}, bf16[4,3,64,512]{3,2,1,0:T(8,128)(2,...) custom-call(bf16[512,768]{1,0:T(8,128)(2,1)} %tiles_ref.5, ...), custom_call_target="tpu_custom_call" | custom-call | flops 17999998976 | bytes 31457280 | tf_op jit(solution)/shard_map/mid/pallas_call | solution.py:1118
  107.5 0.6 compare_convert_fusion.onehot_ref
  108.1 124.8 %attn_bwd.1 = (f32[512,768]{1,0:T(8,128)}, f32[16,768]{1,0:T(8,128)}, f32[48,768]{1,0:T(8,128)}, bf16[320,768]{1,0:T(8,128)(2,1)}, bf16[768,768]{1,0:T(8,128)(2,...) custom-call(bf16[3,3,64,2048]{3,2,1,0:T(8,128)(2,1)} %get-tuple-element.67.qkv_ref, ...), custom_call_target="tpu_custom_call" | custom-call | flops 60000002048 | bytes 31457280 | tf_op jit(solution)/shard_map/attn_bwd/pallas_call | solution.py:897
  232.9 0.0 copy-start
  232.9 0.0 copy-start.2
  232.9 6.9 %finish.1 = (f32[768,768]{1,0:T(8,128)}, f32[768,768]{1,0:T(8,128)}, f32[192,768]{1,0:T(8,128)}, f32[3,192,768]{2,1,0:T(8,128)}, f32[207,768]{1,0:T(8,128)}, /*i...) custom-call(bf16[768,768]{1,0:T(8,128)(2,1)} %get-tuple-element.76.n, ...), custom_call_target="tpu_custom_call" | custom-call | tf_op jit(solution)/shard_map/finish/pallas_call | solution.py:1213
  239.9 0.7 slice_reduce_fusion
  240.6 0.1 reshape_squeeze.3
  240.7 0.6 reshape.83
  241.3 0.5 slice_bitcast_fusion.3
  241.8 0.0 copy-done
  241.9 0.0 copy-done.2
  241.9 9.0 %fusion = f32[69,64,512]{2,1,0:T(8,128)} fusion(bf16[3,69,64,512]{3,2,1,0:T(8,128)(2,1)} %exp_ref.1, f32[69,512]{1,0:T(8,128)S(1)} %get-tuple-element.101, f32[69,512]{1,0:T(8,128)S(1)} %get-tuple-element.102, f32[69,512]{1,0:T(8,128)S(1)} %get-tuple-element.100, f32[69,512]{1,0:T(8,128)S(1)} %slice.37), kind=kLoop, calls=%fused_computation.1 | loop fusion | flops 20348928 | bytes 23175168 | tf_op jit(solution)/shard_map/add | solution.py:1364
  (4 shorter events, 0.1 us)
Async XLA Ops:
  1.3 65.3 %copy-start.1 = (bf16[768,207]{0,1:T(8,128)(2,1)S(1)}, bf16[768,207]{0,1:T(8,128)(2,1)}, u32[]{:S(2)}) copy-start(bf16[768,207]{0,1:T(8,128)(2,1)} %param.37) | copy-start | bytes 953860
  1.3 65.3 %copy-start.3 = (bf16[768,69]{0,1:T(8,128)(2,1)S(1)}, bf16[768,69]{0,1:T(8,128)(2,1)}, u32[]{:S(2)}) copy-start(bf16[768,69]{0,1:T(8,128)(2,1)} %param.39) | copy-start | bytes 317956
  1.3 66.3 %copy-start.4 = (f32[207]{0:T(256)S(1)}, f32[207]{0:T(256)}, u32[]{:S(2)}) copy-start(f32[207]{0:T(256)} %param.38) | copy-start | bytes 2488
  1.3 66.3 %copy-start.5 = (f32[69]{0:T(128)S(1)}, f32[69]{0:T(128)}, u32[]{:S(2)}) copy-start(f32[69]{0:T(128)} %param.40) | copy-start | bytes 832
  232.9 8.9 %copy-start = (f32[3,80,512]{2,1,0:T(8,128)S(1)}, f32[3,80,512]{2,1,0:T(8,128)}, u32[]{:S(2)}) copy-start(f32[3,80,512]{2,1,0:T(8,128)} %get-tuple-element.66) | copy-start | bytes 1474564
  232.9 9.0 %copy-start.2 = (f32[80,512]{1,0:T(8,128)S(1)}, f32[80,512]{1,0:T(8,128)}, u32[]{:S(2)}) copy-start(f32[80,512]{1,0:T(8,128)} %get-tuple-element.65) | copy-start | bytes 491524
